TPU v7x, 32 devices: a whole 2x2x4 slice. The times are simulated.
32 devices in a mesh: req: 8 (over z, y), tp: 4 (over x, core).
Axes of the slice: x: 2, y: 2, z: 4, core: 2. Of those that a mesh axis runs over, the one named last changes fastest.
Arguments:
- tokens: bfloat16 [4096, 2048], P('req', 'tp')
- lengths: int32 [8, 4], P('req'), may hold values from 1 to 144, 512 in all within a row
- request_adapter_index: int32 [8, 4], P('req'), may hold values from 0 to 15, as said below
- attention_norm_gain: float32 [2048], replicated, may hold values from 0.5 to 1.5
- query_norm_gain: float32 [128], replicated, may hold values from 0.5 to 1.5
- key_norm_gain: float32 [128], replicated, may hold values from 0.5 to 1.5
- feedforward_norm_gain: float32 [2048], replicated, may hold values from 0.5 to 1.5
- query_weight: bfloat16 [2048, 2048], P(None, 'tp'), may hold values from -0.125 to 0.125
- key_weight: bfloat16 [2048, 1024], P(None, 'tp'), may hold values from -0.125 to 0.125
- value_weight: bfloat16 [2048, 1024], P(None, 'tp'), may hold values from -0.125 to 0.125
- output_weight: bfloat16 [2048, 2048], P('tp'), may hold values from -0.125 to 0.125
- gate_weight: bfloat16 [2048, 3072], P(None, 'tp'), may hold values from -0.125 to 0.125
- up_weight: bfloat16 [2048, 3072], P(None, 'tp'), may hold values from -0.125 to 0.125
- down_weight: bfloat16 [3072, 2048], P('tp'), may hold values from -0.109375 to 0.109375
- query_key_value_adapter_input: bfloat16 [16, 48, 2048], P('req', None, 'tp'), may hold values from -0.125 to 0.125
- output_adapter_input: bfloat16 [16, 16, 2048], P('req', None, 'tp'), may hold values from -0.125 to 0.125
- gate_up_adapter_input: bfloat16 [16, 32, 2048], P('req', None, 'tp'), may hold values from -0.125 to 0.125
- down_adapter_input: bfloat16 [16, 16, 3072], P('req', None, 'tp'), may hold values from -0.109375 to 0.109375
- query_adapter_output: bfloat16 [16, 16, 2048], P('req', None, 'tp'), may hold values from -1.5 to 1.5
- key_adapter_output: bfloat16 [16, 16, 1024], P('req', None, 'tp'), may hold values from -1.5 to 1.5
- value_adapter_output: bfloat16 [16, 16, 1024], P('req', None, 'tp'), may hold values from -1.5 to 1.5
- projection_adapter_output: bfloat16 [16, 16, 2048], P('req', None, 'tp'), may hold values from -1.5 to 1.5
- gate_adapter_output: bfloat16 [16, 16, 3072], P('req', None, 'tp'), may hold values from -1.5 to 1.5
- up_adapter_output: bfloat16 [16, 16, 3072], P('req', None, 'tp'), may hold values from -1.5 to 1.5
- down_adapter_output: bfloat16 [16, 16, 2048], P('req', None, 'tp'), may hold values from -1.5 to 1.5
Outputs:
- layer_out: bfloat16 [4096, 2048], P('req', 'tp')
Inputs may be any that keep to these rules, and one draw needn't show every extreme that they name: `request_adapter_index`: the 4 requests of one group use adapters of 4 different owners; adapter a belongs to owner a // 2, the index of req that holds it. The lengths of one group's requests sum to 512; the longest is 144.
All inputs are finite; a program needn't handle non-finite values.
Results may differ from a plain program's by a relative error of at most 0.014.
Values may be sent and summed in bfloat16 or wider, within the bound.
No kernel may reach another device: no remote copies, remote signals or barrier semaphores. Data moves between devices by JAX's collectives and lax.ppermute only.
A program may use at most 128 MiB of HBM per device.

v0:
```python
import math

import jax
import jax.numpy as jnp
from jax import lax
from jax.sharding import PartitionSpec as P

HEAD_WIDTH = 128


epsilon = 1e-06
rope_base = 1000000.0


def rms_scale(values, gain):
    mean_square = jnp.mean(values * values, axis=-1, keepdims=True)
    return values * lax.rsqrt(mean_square + epsilon) * gain


def rotate(values, position):
    head_size = values.shape[-1]
    half_size = head_size // 2
    inverse = rope_base ** (-(jnp.arange(half_size, dtype=jnp.float32) * 2.0) / head_size)
    angle = position[:, None] * inverse[None, :]
    cosine = jnp.cos(angle)[:, None, :]
    sine = jnp.sin(angle)[:, None, :]
    first_half = values[..., :half_size]
    second_half = values[..., half_size:]
    return jnp.concatenate(
        [first_half * cosine - second_half * sine, second_half * cosine + first_half * sine],
        axis=-1,
    )


def request_layout(request_lens, row_count):
    ends = jnp.cumsum(request_lens)
    starts = ends - request_lens
    row_index = jnp.arange(row_count, dtype=jnp.int32)
    membership_mask = (row_index[:, None] >= starts[None, :]) & (row_index[:, None] < ends[None, :])
    member_int = membership_mask.astype(jnp.int32)
    request = jnp.sum(
        member_int * jnp.arange(request_lens.shape[0], dtype=jnp.int32)[None, :], axis=1
    )
    position = row_index - jnp.sum(member_int * starts[None, :], axis=1)
    return (member_int, request, position, starts)


def attend(query, keys, values, request):
    row_count, query_heads, head_size = query.shape
    kv_heads = keys.shape[1]
    grouped = query.reshape(row_count, kv_heads, query_heads // kv_heads, head_size)
    scores = jnp.einsum(
        "tkgd,skd->kgts", grouped, keys, preferred_element_type=jnp.float32
    ) / math.sqrt(head_size)
    row_index = jnp.arange(row_count, dtype=jnp.int32)
    allowed = (request[:, None] == request[None, :]) & (row_index[None, :] <= row_index[:, None])
    raw = jnp.where(allowed[None, None], jnp.exp(scores), 0.0)
    probs = (raw / jnp.sum(raw, axis=-1, keepdims=True)).astype(jnp.bfloat16)
    mixed = jnp.einsum("kgts,skd->tkgd", probs, values, preferred_element_type=jnp.float32)
    return mixed.reshape(row_count, query_heads * head_size).astype(jnp.bfloat16)


def gather_features(shard):
    return lax.all_gather(shard, "tp", axis=1, tiled=True)


def reduce_columns(term):
    return lax.psum_scatter(term, "tp", scatter_dimension=1, tiled=True)


def expand_low(low_rank, b_tables, form):
    deltas = []
    offset = 0
    for b_table in b_tables:
        rank_width = b_table.shape[1]
        piece = low_rank[..., offset : offset + rank_width]
        deltas.append(
            jnp.einsum(form, piece, b_table, preferred_element_type=jnp.float32).astype(
                jnp.bfloat16
            )
        )
        offset += rank_width
    return deltas


def route_rows(request_lens, starts, owner_of, local_of, member_int, position, owner_adapter_count):
    group_count = lax.axis_size("req")
    row_count = member_int.shape[0]
    request_count = request_lens.shape[0]
    capacity = row_count * 9 // (8 * request_count)
    owner_hit = (owner_of[None, :] == jnp.arange(group_count, dtype=jnp.int32)[:, None]).astype(
        jnp.int32
    )
    first_row = jnp.sum(owner_hit * starts[None, :], axis=1)
    live_count = jnp.sum(owner_hit * request_lens[None, :], axis=1)
    slot_place = jnp.arange(capacity, dtype=jnp.int32)
    slot_valid = slot_place[None, :] < live_count[:, None]
    source_row = jnp.where(slot_valid, first_row[:, None] + slot_place[None, :], 0)
    local_hot = (
        local_of[:, None] == jnp.arange(owner_adapter_count, dtype=jnp.int32)[None, :]
    ).astype(jnp.int32)
    owner_pick = jnp.sum(owner_hit[:, :, None] * local_hot[None, :, :], axis=1)
    pick_flags = (owner_pick[:, None, :] * slot_valid[:, :, None].astype(jnp.int32)).astype(
        jnp.bfloat16
    )
    token_owner = jnp.sum(member_int * owner_of[None, :], axis=1)
    back_index = token_owner * capacity + position
    return (source_row, slot_valid, pick_flags, back_index)


def remote_delta(inputs, a_local, b_locals, plan):
    source_row, slot_valid, pick_flags, back_index = plan
    group_count, capacity = source_row.shape
    picked = jnp.take(inputs, source_row.reshape(-1), axis=0).reshape(
        group_count, capacity, inputs.shape[1]
    )
    picked = jnp.where(slot_valid[:, :, None], picked, jnp.zeros((), inputs.dtype))
    arrived_rows = lax.all_to_all(picked, "req", split_axis=0, concat_axis=0, tiled=True)
    arrived_flags = lax.all_to_all(pick_flags, "req", split_axis=0, concat_axis=0, tiled=True)
    partial_low = jnp.einsum(
        "nkw,arw->nkar", arrived_rows, a_local, preferred_element_type=jnp.float32
    )
    partial_low = jnp.sum(partial_low * arrived_flags.astype(jnp.float32)[:, :, :, None], axis=2)
    low_rank = lax.psum(partial_low, "tp").astype(jnp.bfloat16)
    spread = arrived_flags[:, :, :, None] * low_rank[:, :, None, :]
    joined = jnp.concatenate(expand_low(spread, b_locals, "nkar,aro->nko"), axis=2)
    returned = lax.all_to_all(joined, "req", split_axis=0, concat_axis=0, tiled=True)
    flat_rows = returned.reshape(group_count * capacity, returned.shape[2])
    gathered = jnp.take(flat_rows, back_index, axis=0)
    deltas = []
    offset = 0
    for b_local in b_locals:
        out_width = b_local.shape[2]
        deltas.append(gathered[:, offset : offset + out_width])
        offset += out_width
    return deltas


def per_device(
    tokens,
    lengths,
    request_adapter_index,
    attention_norm_gain,
    query_norm_gain,
    key_norm_gain,
    feedforward_norm_gain,
    query_weight,
    key_weight,
    value_weight,
    output_weight,
    gate_weight,
    up_weight,
    down_weight,
    query_key_value_adapter_input,
    output_adapter_input,
    gate_up_adapter_input,
    down_adapter_input,
    query_adapter_output,
    key_adapter_output,
    value_adapter_output,
    projection_adapter_output,
    gate_adapter_output,
    up_adapter_output,
    down_adapter_output,
):
    row_count = tokens.shape[0]
    feature_width = tokens.shape[1]
    tp_index = lax.axis_index("tp")
    request_lens = lengths[0]
    request_index_list = request_adapter_index[0]
    member_int, request, position, starts = request_layout(request_lens, row_count)
    pos_float = position.astype(jnp.float32)
    owner_adapter_count = query_key_value_adapter_input.shape[0]
    owner_of = request_index_list // owner_adapter_count
    local_of = request_index_list % owner_adapter_count
    adapter_sets = (
        query_key_value_adapter_input,
        output_adapter_input,
        gate_up_adapter_input,
        down_adapter_input,
        query_adapter_output,
        key_adapter_output,
        value_adapter_output,
        projection_adapter_output,
        gate_adapter_output,
        up_adapter_output,
        down_adapter_output,
    )
    plan = route_rows(
        request_lens, starts, owner_of, local_of, member_int, position, owner_adapter_count
    )

    def adapt(inputs, which_a, which_b):
        return remote_delta(
            inputs, adapter_sets[which_a], [adapter_sets[number] for number in which_b], plan
        )

    whole = gather_features(tokens)
    attention_normalized = rms_scale(whole.astype(jnp.float32), attention_norm_gain).astype(
        jnp.bfloat16
    )
    normed_local = lax.dynamic_slice_in_dim(
        attention_normalized, tp_index * feature_width, feature_width, 1
    )
    query_update, key_update, value_update = adapt(normed_local, 0, (4, 5, 6))
    query = jnp.dot(
        attention_normalized, query_weight, preferred_element_type=jnp.float32
    ) + query_update.astype(jnp.float32)
    heads_here = query.shape[1] // HEAD_WIDTH
    query = rotate(
        rms_scale(query.reshape(row_count, heads_here, HEAD_WIDTH), query_norm_gain), pos_float
    ).astype(jnp.bfloat16)
    keys = jnp.dot(
        attention_normalized, key_weight, preferred_element_type=jnp.float32
    ) + key_update.astype(jnp.float32)
    kv_here = keys.shape[1] // HEAD_WIDTH
    keys = rotate(
        rms_scale(keys.reshape(row_count, kv_here, HEAD_WIDTH), key_norm_gain), pos_float
    ).astype(jnp.bfloat16)
    values = (
        jnp.dot(attention_normalized, value_weight, preferred_element_type=jnp.float32)
        + value_update.astype(jnp.float32)
    ).astype(jnp.bfloat16)
    attention_result = attend(query, keys, values.reshape(row_count, kv_here, HEAD_WIDTH), request)
    output_update = adapt(attention_result, 1, (7,))[0]
    summed = reduce_columns(
        jnp.dot(attention_result, output_weight, preferred_element_type=jnp.float32)
    )
    resid = (summed + output_update.astype(jnp.float32) + tokens.astype(jnp.float32)).astype(
        jnp.bfloat16
    )
    whole_two = gather_features(resid)
    feedforward_normalized = rms_scale(whole_two.astype(jnp.float32), feedforward_norm_gain).astype(
        jnp.bfloat16
    )
    normed_two_local = lax.dynamic_slice_in_dim(
        feedforward_normalized, tp_index * feature_width, feature_width, 1
    )
    gate_update, up_update = adapt(normed_two_local, 2, (8, 9))
    gate = jnp.dot(
        feedforward_normalized, gate_weight, preferred_element_type=jnp.float32
    ) + gate_update.astype(jnp.float32)
    upward = jnp.dot(
        feedforward_normalized, up_weight, preferred_element_type=jnp.float32
    ) + up_update.astype(jnp.float32)
    hidden_state = (jax.nn.silu(gate) * upward).astype(jnp.bfloat16)
    down_update = adapt(hidden_state, 3, (10,))[0]
    summed_two = reduce_columns(
        jnp.dot(hidden_state, down_weight, preferred_element_type=jnp.float32)
    )
    return (summed_two + down_update.astype(jnp.float32) + resid.astype(jnp.float32)).astype(
        jnp.bfloat16
    )


def solution(mesh):
    placed = (
        P("req", "tp"),
        P("req", None),
        P("req", None),
        P(),
        P(),
        P(),
        P(),
        P(None, "tp"),
        P(None, "tp"),
        P(None, "tp"),
        P("tp", None),
        P(None, "tp"),
        P(None, "tp"),
        P("tp", None),
        P("req", None, "tp"),
        P("req", None, "tp"),
        P("req", None, "tp"),
        P("req", None, "tp"),
        P("req", None, "tp"),
        P("req", None, "tp"),
        P("req", None, "tp"),
        P("req", None, "tp"),
        P("req", None, "tp"),
        P("req", None, "tp"),
        P("req", None, "tp"),
    )
    return jax.shard_map(
        per_device, mesh=mesh, in_specs=placed, out_specs=P("req", "tp"), check_vma=False
    )
```

profile of v0, /device:TPU:0, one launch (start us, length us, event | category | flops | bytes accessed | tf_op | source)
XLA Modules:
  0.0 594.9 jit_solution(12964403807250332911)
XLA Ops:
  11.8 7.3 %all-to-all-start = ((bf16[8,144,2]{1,2,0:T(2,128)(2,1)}), bf16[8,144,2]{1,2,0:T(2,128)(2,1)S(1)}, u32[]{:S(2)}, u32[]{:S(2)}) async-start(bf16[8,144,2]{1,2,0:T(2,128)(2,1)} %multiply_convert_fusion.1), calls=%async_computation | async-start | bytes 16384 | tf_op jit(solution)/shard_map/all_to_all | solution.py:119
  19.3 14.9 %all-gather.3.cloned.1.call-done = bf16[512,2048]{1,0:T(8,128)(2,1)} async-done(((bf16[512,512]{1,0:T(8,128)(2,1)}), bf16[512,2048]{1,0:T(8,128)(2,1)}) %all-gather.3.cloned.1.call-update) | async-done | bytes 2097168 | tf_op jit(solution)/shard_map/all_gather | solution.py:64
  39.3 5.8 gather_fusion.3
  47.9 5.5 all-to-all-start.1
  53.4 29.1 %all-to-all-done.1 = bf16[8,144,512]{2,1,0:T(8,128)(2,1)} async-done(((bf16[8,144,512]{2,1,0:T(8,128)(2,1)}), bf16[8,144,512]{2,1,0:T(8,128)(2,1)}, u32[]{:S(2)}, u32[]{:S(2)}) %all-to-all-start.1) | async-done | bytes 1179680 | tf_op jit(solution)/shard_map/all_to_all | solution.py:118
  85.0 15.2 %all-reduce.2 = bf16[8,144,48]{1,2,0:T(8,128)(2,1)S(1)} all-reduce(f32[8,144,48]{1,2,0:T(8,128)} %fusion.13), channel_id=1, replica_groups=mesh['req'=8,'tp'=4] {'tp'}, use_global_device_ids=true, to_apply=%region_8.10 | all-reduce | flops 55296 | bytes 331776 | tf_op jit(solution)/shard_map/psum | solution.py:124
  103.2 4.4 all-to-all-start.2
  111.7 50.1 %all-to-all-done.2 = bf16[8,144,1024]{2,1,0:T(8,128)(2,1)} async-done(((bf16[8,144,1024]{2,1,0:T(8,128)(2,1)}), bf16[8,144,1024]{2,1,0:T(8,128)(2,1)}, u32[]{:S(2)}, u32[]{:S(2)}) %all-to-all-start.2) | async-done | bytes 2359328 | tf_op jit(solution)/shard_map/all_to_all | solution.py:127
  161.8 5.4 gather_fusion
  176.6 3.6 multiply_reduce_fusion
  193.1 3.2 fusion.72
  198.5 5.8 gather_fusion.4
  206.1 32.8 %all_to_all.48 = bf16[8,144,512]{2,1,0:T(8,128)(2,1)S(1)} all-to-all(bf16[8,144,512]{2,1,0:T(8,128)(2,1)S(1)} %broadcast_select_fusion.5), channel_id=1, replica_groups=mesh['req'=8,'tp'=4] {'req'}, dimensions={0} | all-to-all | bytes 2359296 | tf_op jit(solution)/shard_map/all_to_all | solution.py:118
  239.5 12.1 %psum.29 = bf16[8,144,16]{1,2,0:T(8,128)(2,1)S(1)} all-reduce(f32[8,144,16]{1,2,0:T(8,128)S(1)} %fusion.26), channel_id=1, replica_groups=mesh['req'=8,'tp'=4] {'tp'}, use_global_device_ids=true, to_apply=%region_15.17 | all-reduce | flops 18432 | bytes 110592 | tf_op jit(solution)/shard_map/psum | solution.py:124
  253.2 4.3 all-to-all-start.4
  257.5 28.1 %all-to-all-done.4 = bf16[8,144,512]{2,1,0:T(8,128)(2,1)} async-done(((bf16[8,144,512]{2,1,0:T(8,128)(2,1)}), bf16[8,144,512]{2,1,0:T(8,128)(2,1)}, u32[]{:S(2)}, u32[]{:S(2)}) %all-to-all-start.4) | async-done | bytes 1179680 | tf_op jit(solution)/shard_map/all_to_all | solution.py:127
  285.6 4.1 gather_fusion.5
  292.3 21.6 %all-gather.5.cloned.1.call-done = bf16[512,2048]{1,0:T(8,128)(2,1)} async-done(((bf16[512,512]{1,0:T(8,128)(2,1)}), bf16[512,2048]{1,0:T(8,128)(2,1)}) %all-gather.5.cloned.1.call-update) | async-done | bytes 2097168 | tf_op jit(solution)/shard_map/all_gather | solution.py:64
  318.8 5.8 gather_fusion.6
  326.4 34.6 %all_to_all.49 = bf16[8,144,512]{2,1,0:T(8,128)(2,1)S(1)} all-to-all(bf16[8,144,512]{2,1,0:T(8,128)(2,1)S(1)} %broadcast_select_fusion.4), channel_id=1, replica_groups=mesh['req'=8,'tp'=4] {'req'}, dimensions={0} | all-to-all | bytes 2359296 | tf_op jit(solution)/shard_map/all_to_all | solution.py:118
  361.6 13.8 %all-reduce.3 = bf16[8,144,32]{1,2,0:T(8,128)(2,1)S(1)} all-reduce(f32[8,144,32]{1,2,0:T(8,128)S(1)} %fusion.15), channel_id=1, replica_groups=mesh['req'=8,'tp'=4] {'tp'}, use_global_device_ids=true, to_apply=%region_18.21 | all-reduce | flops 36864 | bytes 221184 | tf_op jit(solution)/shard_map/psum | solution.py:124
  380.4 4.5 all-to-all-start.6
  385.2 5.5 fusion.73
  390.7 72.3 %all-to-all-done.6 = bf16[8,144,1536]{2,1,0:T(8,128)(2,1)} async-done(((bf16[8,144,1536]{2,1,0:T(8,128)(2,1)}), bf16[8,144,1536]{2,1,0:T(8,128)(2,1)}, u32[]{:S(2)}, u32[]{:S(2)}) %all-to-all-start.6) | async-done | bytes 3538976 | tf_op jit(solution)/shard_map/all_to_all | solution.py:127
  463.0 6.9 %gather_fusion.1 = bf16[512,1536]{1,0:T(8,128)(2,1)} fusion(bf16[1152,1536]{1,0:T(8,128)(2,1)} %bitcast.55, s32[1024]{0:T(1024)S(1)} %copy-done.31), kind=kCustom, calls=%fused_computation.6 | custom fusion | bytes 3147776 | tf_op jit(solution)/shard_map/jit(_take)/gather | solution.py:129
  471.9 4.4 multiply_convert_fusion
  477.2 3.8 fusion.74
  481.8 7.0 %gather_fusion.2 = bf16[1152,768]{1,0:T(8,128)(2,1)} fusion(bf16[512,768]{1,0:T(8,128)(2,1)} %copy-done.1, s32[2048]{0:T(1024)S(1)} %pad_clamp_fusion), kind=kCustom, calls=%fused_computation.7 | custom fusion | bytes 3543552 | tf_op jit(solution)/shard_map/jit(_take)/gather | solution.py:114
  491.0 44.9 %all_to_all.50 = bf16[8,144,768]{2,1,0:T(8,128)(2,1)S(1)} all-to-all(bf16[8,144,768]{2,1,0:T(8,128)(2,1)S(1)} %select_select_fusion), channel_id=1, replica_groups=mesh['req'=8,'tp'=4] {'req'}, dimensions={0} | all-to-all | bytes 3538944 | tf_op jit(solution)/shard_map/all_to_all | solution.py:118
  536.5 12.0 %psum.31 = bf16[8,144,16]{1,2,0:T(8,128)(2,1)S(1)} all-reduce(f32[8,144,16]{1,2,0:T(8,128)S(1)} %fusion.29), channel_id=1, replica_groups=mesh['req'=8,'tp'=4] {'tp'}, use_global_device_ids=true, to_apply=%region_21.24 | all-reduce | flops 18432 | bytes 110592 | tf_op jit(solution)/shard_map/psum | solution.py:124
  549.1 32.7 %all_to_all.51 = bf16[8,144,512]{2,1,0:T(8,128)(2,1)} all-to-all(bf16[8,144,512]{2,1,0:T(8,128)(2,1)S(1)} %bitcast_convert_fusion.2), channel_id=1, replica_groups=mesh['req'=8,'tp'=4] {'req'}, dimensions={0} | all-to-all | bytes 2359296 | tf_op jit(solution)/shard_map/all_to_all | solution.py:127
  581.7 4.1 gather_fusion.7
  (183 shorter events, 75.6 us)
Async XLA Ops:
  6.5 470.7 %copy-start = (bf16[768,2048]{1,0:T(8,128)(2,1)S(1)}, bf16[768,2048]{1,0:T(8,128)(2,1)}, u32[]{:S(2)}) copy-start(bf16[768,2048]{1,0:T(8,128)(2,1)} %param.42) | copy-start | bytes 9437188
  6.5 29.9 %copy-start.35 = (f32[2048]{0:T(1024)S(1)}, f32[2048]{0:T(1024)}, u32[]{:S(2)}) copy-start(f32[2048]{0:T(1024)} %param.32) | copy-start | bytes 24580
  6.5 27.7 %all-gather.3.cloned.1.call-start = ((), (), s32[]{:S(2)}) async-start(), calls=%async_computation.11 | async-start | bytes 2621440 | tf_op jit(solution)/shard_map/all_gather | solution.py:64
  11.2 315.0 %copy-start.22 = (pred[8,144]{1,0:T(8,128)(4,1)}, pred[8,144]{1,0:T(8,128)(4,1)S(1)}, u32[]{:S(2)}) copy-start(pred[8,144]{1,0:T(8,128)(4,1)S(1)} %get-tuple-element.22) | copy-start | bytes 3460
  11.8 36.0 %all-to-all-start = ((bf16[8,144,2]{1,2,0:T(2,128)(2,1)}), bf16[8,144,2]{1,2,0:T(2,128)(2,1)S(1)}, u32[]{:S(2)}, u32[]{:S(2)}) async-start(bf16[8,144,2]{1,2,0:T(2,128)(2,1)} %multiply_convert_fusion.1), calls=%async_computation | async-start | bytes 16384 | tf_op jit(solution)/shard_map/all_to_all | solution.py:119
  19.2 17.8 %copy-start.19 = (s32[8,144]{1,0:T(8,128)}, s32[8,144]{1,0:T(8,128)S(1)}, u32[]{:S(2)}) copy-start(s32[8,144]{1,0:T(8,128)S(1)} %add_select_fusion) | copy-start | bytes 13828
  46.6 35.9 %copy-start.41 = (bf16[2,48,512]{2,1,0:T(8,128)(2,1)S(1)}, bf16[2,48,512]{2,1,0:T(8,128)(2,1)}, u32[]{:S(2)}) copy-start(bf16[2,48,512]{2,1,0:T(8,128)(2,1)} %param.43) | copy-start | bytes 294916
  47.9 203.7 %copy-start.17 = (bf16[8,144,2]{1,2,0:T(2,128)(2,1)}, bf16[8,144,2]{1,2,0:T(2,128)(2,1)S(1)}, u32[]{:S(2)}) copy-start(bf16[8,144,2]{1,2,0:T(2,128)(2,1)S(1)} %all-to-all-done) | copy-start | bytes 13828
  47.9 34.6 %all-to-all-start.1 = ((bf16[8,144,512]{2,1,0:T(8,128)(2,1)}), bf16[8,144,512]{2,1,0:T(8,128)(2,1)}, u32[]{:S(2)}, u32[]{:S(2)}) async-start(bf16[8,144,512]{2,1,0:T(8,128)(2,1)} %broadcast_select_fusion.6), calls=%async_computation.1 | async-start | bytes 2359296 | tf_op jit(solution)/shard_map/all_to_all | solution.py:118
  53.4 46.9 %copy-start.27 = (bf16[2,16,512]{2,1,0:T(8,128)(2,1)S(1)}, bf16[2,16,512]{2,1,0:T(8,128)(2,1)}, u32[]{:S(2)}) copy-start(bf16[2,16,512]{2,1,0:T(8,128)(2,1)} %param.47) | copy-start | bytes 98308
  53.4 47.4 %copy-start.44 = (bf16[2,16,256]{2,1,0:T(8,128)(2,1)S(1)}, bf16[2,16,256]{2,1,0:T(8,128)(2,1)}, u32[]{:S(2)}) copy-start(bf16[2,16,256]{2,1,0:T(8,128)(2,1)} %param.48) | copy-start | bytes 49156
  85.0 16.1 %copy-start.45 = (bf16[2,16,256]{2,1,0:T(8,128)(2,1)S(1)}, bf16[2,16,256]{2,1,0:T(8,128)(2,1)}, u32[]{:S(2)}) copy-start(bf16[2,16,256]{2,1,0:T(8,128)(2,1)} %param.49) | copy-start | bytes 49156
  103.2 58.5 %all-to-all-start.2 = ((bf16[8,144,1024]{2,1,0:T(8,128)(2,1)}), bf16[8,144,1024]{2,1,0:T(8,128)(2,1)}, u32[]{:S(2)}, u32[]{:S(2)}) async-start(bf16[8,144,1024]{2,1,0:T(8,128)(2,1)} %pad_maximum_fusion.1), calls=%async_computation.2 | async-start | bytes 4718592 | tf_op jit(solution)/shard_map/all_to_all | solution.py:127
  107.6 182.0 %reduce-scatter.3.cloned.1.call-start = ((), (), s32[]{:S(2)}) async-start(), calls=%async_computation.12 | async-start | bytes 5242880 | tf_op jit(solution)/shard_map/reduce_scatter | solution.py:68
  110.2 57.0 %copy-start.30 = (s32[1024]{0:T(1024)}, s32[1024]{0:T(1024)S(1)}, u32[]{:S(2)}) copy-start(s32[1024]{0:T(1024)S(1)} %pad_clamp_fusion.3) | copy-start | bytes 12292
  110.8 58.7 %copy-start.32 = (pred[512]{0:T(512)(128)(4,1)}, pred[512]{0:T(512)(128)(4,1)S(1)}, u32[]{:S(2)}) copy-start(pred[512]{0:T(512)(128)(4,1)S(1)} %get-tuple-element.12) | copy-start | bytes 1540
  205.9 33.1 %copy-start.26 = (bf16[2,16,512]{2,1,0:T(8,128)(2,1)S(1)}, bf16[2,16,512]{2,1,0:T(8,128)(2,1)}, u32[]{:S(2)}) copy-start(bf16[2,16,512]{2,1,0:T(8,128)(2,1)} %param.44) | copy-start | bytes 98308
  206.1 45.5 %copy-start.42 = (bf16[2,16,512]{2,1,0:T(8,128)(2,1)S(1)}, bf16[2,16,512]{2,1,0:T(8,128)(2,1)}, u32[]{:S(2)}) copy-start(bf16[2,16,512]{2,1,0:T(8,128)(2,1)} %param.50) | copy-start | bytes 98308
  239.4 18.0 %copy-start.38 = (s32[512]{0:T(512)S(1)}, s32[512]{0:T(512)}, u32[]{:S(2)}) copy-start(s32[512]{0:T(512)} %get-tuple-element.13) | copy-start | bytes 6148
  253.2 32.4 %all-to-all-start.4 = ((bf16[8,144,512]{2,1,0:T(8,128)(2,1)}), bf16[8,144,512]{2,1,0:T(8,128)(2,1)}, u32[]{:S(2)}, u32[]{:S(2)}) async-start(bf16[8,144,512]{2,1,0:T(8,128)(2,1)} %bitcast_convert_fusion.3), calls=%async_computation.5 | async-start | bytes 2359296 | tf_op jit(solution)/shard_map/all_to_all | solution.py:127
  257.4 56.4 %all-gather.5.cloned.1.call-start = ((), (), s32[]{:S(2)}) async-start(), calls=%async_computation.13 | async-start | bytes 2621440 | tf_op jit(solution)/shard_map/all_gather | solution.py:64
  257.5 32.2 %copy-start.28 = (s32[1024]{0:T(1024)}, s32[1024]{0:T(1024)S(1)}, u32[]{:S(2)}) copy-start(s32[1024]{0:T(1024)S(1)} %pad_clamp_fusion.2) | copy-start | bytes 12292
  289.6 26.4 %copy-start.36 = (f32[2048]{0:T(1024)S(1)}, f32[2048]{0:T(1024)}, u32[]{:S(2)}) copy-start(f32[2048]{0:T(1024)} %param.35) | copy-start | bytes 24580
  326.2 34.9 %copy-start.21 = (bf16[2,32,512]{2,1,0:T(8,128)(2,1)S(1)}, bf16[2,32,512]{2,1,0:T(8,128)(2,1)}, u32[]{:S(2)}) copy-start(bf16[2,32,512]{2,1,0:T(8,128)(2,1)} %param.45) | copy-start | bytes 196612
  380.4 82.6 %all-to-all-start.6 = ((bf16[8,144,1536]{2,1,0:T(8,128)(2,1)}), bf16[8,144,1536]{2,1,0:T(8,128)(2,1)}, u32[]{:S(2)}, u32[]{:S(2)}) async-start(bf16[8,144,1536]{2,1,0:T(8,128)(2,1)} %pad_maximum_fusion), calls=%async_computation.7 | async-start | bytes 7077888 | tf_op jit(solution)/shard_map/all_to_all | solution.py:127
  384.9 78.1 %copy-start.31 = (s32[1024]{0:T(1024)S(1)}, s32[1024]{0:T(1024)}, u32[]{:S(2)}) copy-start(s32[1024]{0:T(1024)} %copy-done.30) | copy-start | bytes 12292
  384.9 200.9 %reduce-scatter.5.cloned.1.call-start = ((), (), s32[]{:S(2)}) async-start(), calls=%async_computation.14 | async-start | bytes 5242880 | tf_op jit(solution)/shard_map/reduce_scatter | solution.py:68
  481.8 7.0 %copy-start.23 = (pred[8,144]{1,0:T(8,128)(4,1)S(1)}, pred[8,144]{1,0:T(8,128)(4,1)}, u32[]{:S(2)}) copy-start(pred[8,144]{1,0:T(8,128)(4,1)} %copy-done.22) | copy-start | bytes 3460
  490.9 44.9 %copy-start.25 = (bf16[2,16,768]{2,1,0:T(8,128)(2,1)S(1)}, bf16[2,16,768]{2,1,0:T(8,128)(2,1)}, u32[]{:S(2)}) copy-start(bf16[2,16,768]{2,1,0:T(8,128)(2,1)} %param.46) | copy-start | bytes 147460
  490.9 57.6 %copy-start.18 = (bf16[8,144,2]{1,2,0:T(2,128)(2,1)S(1)}, bf16[8,144,2]{1,2,0:T(2,128)(2,1)}, u32[]{:S(2)}) copy-start(bf16[8,144,2]{1,2,0:T(2,128)(2,1)} %copy-done.17) | copy-start | bytes 13828
  491.0 57.6 %copy-start.43 = (bf16[2,16,512]{2,1,0:T(8,128)(2,1)S(1)}, bf16[2,16,512]{2,1,0:T(8,128)(2,1)}, u32[]{:S(2)}) copy-start(bf16[2,16,512]{2,1,0:T(8,128)(2,1)} %param.53) | copy-start | bytes 98308
  536.5 45.2 %copy-start.29 = (s32[1024]{0:T(1024)S(1)}, s32[1024]{0:T(1024)}, u32[]{:S(2)}) copy-start(s32[1024]{0:T(1024)} %copy-done.28) | copy-start | bytes 12292
  (23 other events, 57.8 us)
Sparse Core Ops, SparseCore 0:
  8.9 25.2 all-gather.2
  196.5 42.7 reduce-scatter.2
  292.4 21.3 all-gather.4
  481.1 43.8 reduce-scatter.4
where the time goes:
time: 597 us; the launch traced here: 595 us
  waiting for transfers between devices  217 us (36%)
  blocking collectives  198 us (33%)
  local copies, waits for them, and re-layouts  65.6 us (11%)
  matrix products  38.9 us (7%)
  other arithmetic  35.2 us (6%)
  starting transfers between devices  26.5 us (4%)
  between operations  13.9 us (2%)
    all_to_all x3, waiting for transfers between devices, remote_delta(): lax.all_to_all(joined, 'req', split_axis=0, concat_axis=0, tiled=True)  150 us
    all_to_all x3, blocking collectives, remote_delta(): lax.all_to_all(picked, 'req', split_axis=0, concat_axis=0, tiled=True)  112 us
    psum x4, blocking collectives, remote_delta(): low_rank = lax.psum(partial_low, 'tp').astype(jnp.bfloat16)  53.1 us
    all_gather x2, waiting for transfers between devices, gather_features(): return lax.all_gather(shard, 'tp', axis=1, tiled=True)  36.5 us
    all_to_all x1, blocking collectives, remote_delta(): lax.all_to_all(joined, 'req', split_axis=0, concat_axis=0, tiled=True)  32.7 us
    all_to_all x1, waiting for transfers between devices, remote_delta(): lax.all_to_all(picked, 'req', split_axis=0, concat_axis=0, tiled=True)  29.1 us
    gather x4, local copies, waits for them, and re-layouts, remote_delta(): jnp.take(inputs, source_row.reshape(-1), axis=0)  24.5 us
    gather x5, local copies, waits for them, and re-layouts, remote_delta(): gathered = jnp.take(flat_rows, back_index, axis=0)  22.7 us
  transfers between devices with their start and end apart: 9, of which 6 were waited for; matrix products, arithmetic and copies ran while one was open for 9% of the time, Pallas kernels for 0%

commit v1 on v0

v1 whole, which is shorter than its diff:
```python
import functools
import math

import jax
import jax.numpy as jnp
from jax import lax
from jax.experimental import pallas as pl
from jax.experimental.pallas import tpu as pltpu
from jax.sharding import PartitionSpec as P

HEAD_WIDTH = 128
CHUNKS = 2

epsilon = 1e-06
rope_base = 1000000.0

bf16 = jnp.bfloat16
f32 = jnp.float32
VMEM = pl.BlockSpec(memory_space=pltpu.VMEM)
SMEM = pl.BlockSpec(memory_space=pltpu.SMEM)


def call(body, in_specs, outs, flops=0, moved=0, scratch=(), limit=40):
    single = not isinstance(outs, (list, tuple))
    listed = [outs] if single else list(outs)
    return pl.pallas_call(
        body,
        out_shape=outs if single else listed,
        in_specs=in_specs,
        out_specs=VMEM if single else [VMEM] * len(listed),
        scratch_shapes=list(scratch),
        compiler_params=pltpu.CompilerParams(vmem_limit_bytes=limit * 1024 * 1024),
        cost_estimate=pl.CostEstimate(flops=flops, bytes_accessed=moved, transcendentals=0),
    )


def shaped(shape, dtype):
    return jax.ShapeDtypeStruct(shape, dtype)


def dot(a, b):
    return lax.dot_general(a, b, (((1,), (0,)), ((), ())), preferred_element_type=f32)


def dot_nt(a, b):
    return lax.dot_general(a, b, (((1,), (1,)), ((), ())), preferred_element_type=f32)


def dot_tn(a, b):
    return lax.dot_general(a, b, (((0,), (0,)), ((), ())), preferred_element_type=f32)


def part_of(index_ref, rel, width):
    return pl.ds(pl.multiple_of((index_ref[0] ^ rel) * width, width), width)


def bounds(lens_ref, count):
    starts, total = [], jnp.int32(0)
    for j in range(count):
        starts.append(total)
        total = total + lens_ref[0, j]
    return starts, starts[1:] + [total]


def lane_masks(lens_ref, count, first, width):
    starts, ends = bounds(lens_ref, count)
    rows = lax.broadcasted_iota(jnp.int32, (1, width), 1) + first
    return [((rows >= s) & (rows < e)).astype(f32) for s, e in zip(starts, ends)]


def pack_first(me_ref, idx_ref, qkv_a, out_a, proj_b, q_b, k_b, v_b, send):
    groups, wanted = idx_ref.shape
    held, low, _ = qkv_a.shape
    rank = out_a.shape[1]
    k_width = k_b.shape[2]

    @pl.loop(0, groups)
    def _(g):
        pick = jnp.int32(0)
        for j in range(wanted):
            a = idx_ref[g, j]
            pick = pick + jnp.where(a // held == me_ref[0], a % held, 0)
        send[g, 0:low, :] = qkv_a[pick]
        send[g, low : low + rank, :] = out_a[pick]
        send[g, low + rank : low + 2 * rank, :] = proj_b[pick]
        send[g, low + 2 * rank : low + 3 * rank, :] = q_b[pick]
        send[g, low + 3 * rank : low + 4 * rank, 0:k_width] = k_b[pick]
        send[g, low + 3 * rank : low + 4 * rank, k_width:] = v_b[pick]


def pack_second(me_ref, idx_ref, gu_a, down_b, down_a, gate_b, up_b, send):
    groups, wanted = idx_ref.shape
    held = gu_a.shape[0]
    unit = send.shape[2]

    @pl.loop(0, groups)
    def _(g):
        pick = jnp.int32(0)
        for j in range(wanted):
            a = idx_ref[g, j]
            pick = pick + jnp.where(a // held == me_ref[0], a % held, 0)
        row = 0
        for table in (gu_a, down_b, down_a, gate_b, up_b):
            height, width = table.shape[1:]
            for k in range(width // unit):
                send[g, row : row + height, :] = table[pick, :, k * unit : (k + 1) * unit]
                row += height


def rel_owner(want_ref, held, j):
    return want_ref[0, j] // held


def project_qkv(index_ref, own, core, across, diagonal, gain, q_w, k_w, v_w, normed_own, *qkv_outs):
    rows, width = own.shape
    q_width, k_width = q_w.shape[1], k_w.shape[1]
    step = rows // len(qkv_outs)
    for c, out in enumerate(qkv_outs):
        here = slice(c * step, (c + 1) * step)
        blocks = [ref[here, :].astype(f32) for ref in (own, core, across, diagonal)]
        square = sum(jnp.sum(b * b, axis=1, keepdims=True) for b in blocks)
        scale = lax.rsqrt(square / (4 * width) + epsilon)
        for rel, block in enumerate(blocks):
            part = part_of(index_ref, rel, width)
            normed = (block * scale * gain[:, part]).astype(bf16)
            if rel == 0:
                normed_own[here, :] = normed
            for w, low, high in (
                (q_w, 0, q_width),
                (k_w, q_width, q_width + k_width),
                (v_w, q_width + k_width, q_width + 2 * k_width),
            ):
                term = dot(normed, w[part, :])
                if rel == 0:
                    out[:, low:high] = term
                else:
                    out[:, low:high] += term


def low_first(held, low, rank, want_ref, lens_ref, received, normed_own, out, stack):
    wanted = want_ref.shape[1]
    for j in range(wanted):
        owner = rel_owner(want_ref, held, j)
        stack[j * low : (j + 1) * low, :] = received[owner, 0:low, :]
        out[low + j * rank : low + (j + 1) * rank, :] = received[owner, low + rank : low + 2 * rank, :]
    products = dot_nt(stack[...], normed_own[...])
    masks = lane_masks(lens_ref, wanted, 0, normed_own.shape[0])
    out[0:low, :] = sum(
        products[j * low : (j + 1) * low, :] * masks[j] for j in range(wanted)
    ).astype(bf16)


def attend(
    chunk, held, low, rank, heads, kv_heads,
    index_ref, want_ref, lens_ref, qkv, shared0, shared1, shared2, shared3, received, cosine, sine,
    q_gain, k_gain, out_w, old_k, old_v, keep, send, new_k, new_v, stack_q, stack_k, stack_v, stack_o,
):
    rows = qkv.shape[0]
    width = out_w.shape[0]
    first = chunk * rows
    here = slice(first, first + rows)
    wanted = want_ref.shape[1]
    shared = (shared0, shared1, shared2, shared3)
    q_width, k_width = heads * HEAD_WIDTH, kv_heads * HEAD_WIDTH
    for j in range(wanted):
        owner = rel_owner(want_ref, held, j)
        at = slice(j * rank, (j + 1) * rank)
        stack_o[at, :] = received[owner, low : low + rank, :]
        stack_q[at, :] = received[owner, low + 2 * rank : low + 3 * rank, :]
        stack_k[at, :] = received[owner, low + 3 * rank : low + 4 * rank, 0:k_width]
        stack_v[at, :] = received[owner, low + 3 * rank : low + 4 * rank, k_width:]
    masks = lane_masks(lens_ref, wanted, first, rows)
    total = sum(ref[0:low, here].astype(f32) for ref in shared).astype(bf16).astype(f32)

    def delta(number, stack):
        piece = total[number * rank : (number + 1) * rank, :]
        spread = jnp.concatenate([piece * m for m in masks], axis=0).astype(bf16)
        return dot_tn(spread, stack[...]).astype(bf16).astype(f32)

    query = qkv[:, 0:q_width] + delta(0, stack_q)
    key = qkv[:, q_width : q_width + k_width] + delta(1, stack_k)
    new_v[...] = (qkv[:, q_width + k_width :] + delta(2, stack_v)).astype(bf16)
    cos, sin = cosine[here, :], sine[here, :]

    def turn(values, gain):
        square = jnp.mean(values * values, axis=1, keepdims=True)
        values = values * lax.rsqrt(square + epsilon) * gain[...]
        return (values * cos + pltpu.roll(values, HEAD_WIDTH // 2, 1) * sin).astype(bf16)

    def head(h):
        return slice(h * HEAD_WIDTH, (h + 1) * HEAD_WIDTH)

    for h in range(kv_heads):
        new_k[:, head(h)] = turn(key[:, head(h)], k_gain)
    seen = first + rows
    starts, _ = bounds(lens_ref, wanted)
    down = lax.broadcasted_iota(jnp.int32, (rows, 1), 0) + first
    start_of = jnp.zeros((rows, 1), jnp.int32)
    for s in starts:
        start_of = jnp.where(down >= s, s, start_of)
    along = lax.broadcasted_iota(jnp.int32, (rows, seen), 1)
    allowed = (along <= down) & (along >= start_of)
    group = heads // kv_heads
    mixed = []
    for kv in range(kv_heads):
        keys, values = new_k[:, head(kv)], new_v[:, head(kv)]
        if chunk > 0:
            keys = jnp.concatenate([old_k[:, head(kv)], keys], axis=0)
            values = jnp.concatenate([old_v[:, head(kv)], values], axis=0)
        for h in range(kv * group, (kv + 1) * group):
            scores = dot_nt(turn(query[:, head(h)], q_gain), keys) * (1.0 / math.sqrt(HEAD_WIDTH))
            raw = jnp.where(allowed, jnp.exp(scores), 0.0)
            probs = (raw / jnp.sum(raw, axis=1, keepdims=True)).astype(bf16)
            mixed.append(dot(probs, values).astype(bf16))
    attended = jnp.concatenate(mixed, axis=1)
    lows = dot_nt(stack_o[...], attended)
    lows = jnp.concatenate(
        [lows[j * rank : (j + 1) * rank, :] * masks[j] for j in range(wanted)], axis=0
    ).astype(bf16)
    for rel in range(4):
        part = part_of(index_ref, rel, width)
        table = shared[rel][low : low + wanted * rank, :]
        term = dot(attended, out_w[:, part]) + dot_tn(lows, table)
        target, at = ((keep, 0), (send, 0), (keep, 1), (send, 1))[rel]
        target[:, at * width : (at + 1) * width] = term.astype(target.dtype)


def add_pair(kept, arrived, out):
    out[...] = (kept[...] + arrived[...].astype(f32)).astype(bf16)


def residual(chunk, chip, arrived, own, across, out):
    rows = chip.shape[0]
    width = own.shape[1]
    here = slice(chunk * rows, (chunk + 1) * rows)
    left, right = slice(0, width), slice(width, 2 * width)
    for mine, theirs, tokens in ((left, right, own), (right, left, across)):
        total = chip[:, mine].astype(f32) + arrived[:, theirs].astype(f32)
        out[:, mine] = (total + tokens[here, :].astype(f32)).astype(bf16)


def choose_second(held, low, rank, want_ref, received, out):
    wanted = want_ref.shape[1]
    unit = received.shape[2]
    for j in range(wanted):
        owner = rel_owner(want_ref, held, j)
        row = 0
        for base, height in ((0, low), (wanted * low, rank)):
            at = slice(base + j * height, base + (j + 1) * height)
            for k in range(out.shape[1] // unit):
                out[at, k * unit : (k + 1) * unit] = received[owner, row : row + height, :]
                row += height


def feed_forward(
    chunk, held, low, rank,
    index_ref, want_ref, lens_ref, mine, theirs, table0, table1, table2, table3, received, gain,
    gate_w, up_w, down_w, keep, send, stack_a, stack_g, stack_u,
):
    rows = mine.shape[0]
    width = mine.shape[1] // 2
    hidden_width = gate_w.shape[1]
    first = chunk * rows
    wanted = want_ref.shape[1]
    unit = received.shape[2]
    tables = (table0, table1, table2, table3)
    for j in range(wanted):
        owner = rel_owner(want_ref, held, j)
        at = slice(j * rank, (j + 1) * rank)
        row = (low + rank) * (width // unit)
        for stack in (stack_a, stack_g, stack_u):
            for k in range(hidden_width // unit):
                stack[at, k * unit : (k + 1) * unit] = received[owner, row : row + rank, :]
                row += rank
    masks = lane_masks(lens_ref, wanted, first, rows)
    blocks = [
        ref[:, at * width : (at + 1) * width].astype(f32)
        for ref, at in ((mine, 0), (theirs, 0), (mine, 1), (theirs, 1))
    ]
    square = sum(jnp.sum(b * b, axis=1, keepdims=True) for b in blocks)
    scale = lax.rsqrt(square / (4 * width) + epsilon)
    gate = upward = products = None
    for rel, block in enumerate(blocks):
        part = part_of(index_ref, rel, width)
        normed = (block * scale * gain[:, part]).astype(bf16)
        terms = (
            dot(normed, gate_w[part, :]),
            dot(normed, up_w[part, :]),
            dot_nt(tables[rel][0 : wanted * low, :], normed),
        )
        if rel == 0:
            gate, upward, products = terms
        else:
            gate, upward, products = gate + terms[0], upward + terms[1], products + terms[2]
    total = sum(products[j * low : (j + 1) * low, :] * masks[j] for j in range(wanted))
    total = total.astype(bf16).astype(f32)

    def delta(number, stack):
        piece = total[number * rank : (number + 1) * rank, :]
        spread = jnp.concatenate([piece * m for m in masks], axis=0).astype(bf16)
        return dot_tn(spread, stack[...]).astype(bf16).astype(f32)

    gate = gate + delta(0, stack_g)
    upward = upward + delta(1, stack_u)
    hidden = (gate / (1.0 + jnp.exp(-gate)) * upward).astype(bf16)
    lows = dot_nt(stack_a[...], hidden)
    lows = jnp.concatenate(
        [lows[j * rank : (j + 1) * rank, :] * masks[j] for j in range(wanted)], axis=0
    ).astype(bf16)
    for rel in range(4):
        part = part_of(index_ref, rel, width)
        table = tables[rel][wanted * low : wanted * (low + rank), :]
        term = dot(hidden, down_w[:, part]) + dot_tn(lows, table)
        target, at = ((keep, 0), (send, 0), (keep, 1), (send, 1))[rel]
        target[:, at * width : (at + 1) * width] = term.astype(target.dtype)


def split_pair(kept, arrived, stay, away):
    width = stay.shape[1]
    stay[...] = kept[:, 0:width] + arrived[:, 0:width].astype(f32)
    away[...] = (kept[:, width:] + arrived[:, width:].astype(f32)).astype(bf16)


def finish(count, *refs):
    out = refs[-1]
    for c in range(count):
        stay, arrived, resid = refs[3 * c : 3 * c + 3]
        rows, width = stay.shape
        total = stay[...] + arrived[...].astype(f32) + resid[:, 0:width].astype(f32)
        out[c * rows : (c + 1) * rows, :] = total.astype(bf16)


def rotation_tables(lens, row_count):
    half = HEAD_WIDTH // 2
    inverse = rope_base ** (-(jnp.arange(half, dtype=f32) * 2.0) / HEAD_WIDTH)
    row = jnp.arange(row_count, dtype=jnp.int32)
    start_of = jnp.zeros_like(row)
    start = jnp.int32(0)
    for j in range(lens.shape[0]):
        start_of = jnp.where(row >= start, start, start_of)
        start = start + lens[j]
    angle = (row - start_of).astype(f32)[:, None] * jnp.concatenate([inverse, inverse])[None, :]
    sign = jnp.concatenate([-jnp.ones(half, f32), jnp.ones(half, f32)])
    return jnp.cos(angle), jnp.sin(angle) * sign[None, :]


def swap_core(values):
    return lax.ppermute(values, "tp", [(k, k ^ 1) for k in range(4)])


def swap_across(values):
    return lax.ppermute(values, "tp", [(k, k ^ 2) for k in range(4)])


def swap_diagonal(values):
    return lax.ppermute(values, "tp", [(k, k ^ 3) for k in range(4)])


def to_groups(values):
    return lax.all_to_all(values, "req", split_axis=0, concat_axis=0, tiled=True)


def per_device(
    tokens,
    lengths,
    request_adapter_index,
    attention_norm_gain,
    query_norm_gain,
    key_norm_gain,
    feedforward_norm_gain,
    query_weight,
    key_weight,
    value_weight,
    output_weight,
    gate_weight,
    up_weight,
    down_weight,
    query_key_value_adapter_input,
    output_adapter_input,
    gate_up_adapter_input,
    down_adapter_input,
    query_adapter_output,
    key_adapter_output,
    value_adapter_output,
    projection_adapter_output,
    gate_adapter_output,
    up_adapter_output,
    down_adapter_output,
):
    assert lax.axis_size("tp") == 4
    row_count, width = tokens.shape
    groups = lax.axis_size("req")
    wanted = lengths.shape[1]
    held, low_qkv, _ = query_key_value_adapter_input.shape
    rank = output_adapter_input.shape[1]
    low_gu = gate_up_adapter_input.shape[1]
    q_width, k_width = query_weight.shape[1], key_weight.shape[1]
    hidden_width = gate_weight.shape[1]
    heads, kv_heads = q_width // HEAD_WIDTH, k_width // HEAD_WIDTH
    assert row_count == width == q_width == 2 * k_width
    unit = math.gcd(width, hidden_width)
    rows = row_count // CHUNKS
    index = lax.axis_index("tp").astype(jnp.int32).reshape(1)
    me = lax.axis_index("req").astype(jnp.int32).reshape(1)

    asked = to_groups(jnp.broadcast_to(request_adapter_index, (groups, wanted)))
    first_rows = low_qkv + 4 * rank
    send_first = call(
        pack_first, [SMEM, SMEM] + [VMEM] * 6, shaped((groups, first_rows, width), bf16),
        moved=2 * groups * first_rows * width,
    )(
        me, asked, query_key_value_adapter_input, output_adapter_input, projection_adapter_output,
        query_adapter_output, key_adapter_output, value_adapter_output,
    )
    received = to_groups(send_first)

    across = swap_across(tokens)
    core = swap_core(tokens)
    diagonal = swap_core(across)
    gain_one = attention_norm_gain.reshape(1, -1)
    gain_two = feedforward_norm_gain.reshape(1, -1)
    q_gain = query_norm_gain.reshape(1, -1)
    k_gain = key_norm_gain.reshape(1, -1)
    qkv_width = q_width + 2 * k_width
    normed_own, *qkv = call(
        project_qkv, [SMEM] + [VMEM] * 8,
        [shaped((row_count, width), bf16)] + [shaped((rows, qkv_width), f32)] * CHUNKS,
        flops=2 * row_count * 4 * width * qkv_width, moved=8 * width * qkv_width,
    )(index, tokens, core, across, diagonal, gain_one, query_weight, key_weight, value_weight)

    asked, normed_own = lax.optimization_barrier((asked, normed_own))
    second_rows = ((low_gu + rank) * width + 3 * rank * hidden_width) // unit
    send_second = call(
        pack_second, [SMEM, SMEM] + [VMEM] * 5, shaped((groups, second_rows, unit), bf16),
        moved=2 * groups * second_rows * unit,
    )(
        me, asked, gate_up_adapter_input, down_adapter_output, down_adapter_input,
        gate_adapter_output, up_adapter_output,
    )
    received_second = to_groups(send_second)

    cosine, sine = rotation_tables(lengths[0], row_count)
    shared_own = call(
        functools.partial(low_first, held, low_qkv, rank), [SMEM, SMEM, VMEM, VMEM],
        shaped((low_qkv + wanted * rank, width), bf16),
        flops=2 * wanted * low_qkv * width * row_count, moved=2 * row_count * width,
        scratch=[pltpu.VMEM((wanted * low_qkv, width), bf16)],
    )(request_adapter_index, lengths, received, normed_own)
    shared = (shared_own, swap_core(shared_own), swap_across(shared_own), swap_diagonal(shared_own))

    table = call(
        functools.partial(choose_second, held, low_gu, rank), [SMEM, VMEM],
        shaped((wanted * (low_gu + rank), width), bf16),
        moved=4 * wanted * (low_gu + rank) * width,
    )(request_adapter_index, received_second)
    table_across = swap_across(table)
    tables = (table, swap_core(table), table_across, swap_core(table_across))

    wide = shaped((rows, 2 * width), bf16)
    kept = shaped((rows, 2 * width), f32)
    old_k = old_v = None
    chips = []
    for c in range(CHUNKS):
        if c == 0:
            past = [jnp.zeros((16, k_width), bf16)] * 2
        else:
            past = [old_k, old_v]
        keep, send, new_k, new_v = call(
            functools.partial(attend, c, held, low_qkv, rank, heads, kv_heads),
            [SMEM] * 3 + [VMEM] * 13,
            [kept, wide, shaped((rows, k_width), bf16), shaped((rows, k_width), bf16)],
            flops=2 * rows * width * 4 * width + 4 * heads * rows * row_count * HEAD_WIDTH,
            moved=8 * width * width,
            scratch=[
                pltpu.VMEM((wanted * rank, q_width), bf16),
                pltpu.VMEM((wanted * rank, k_width), bf16),
                pltpu.VMEM((wanted * rank, k_width), bf16),
                pltpu.VMEM((wanted * rank, width), bf16),
            ],
        )(
            index, request_adapter_index, lengths, qkv[c], *shared, received, cosine, sine,
            q_gain, k_gain, output_weight, *past,
        )
        if c == 0:
            old_k, old_v = new_k, new_v
        else:
            old_k = jnp.concatenate([old_k, new_k], axis=0)
            old_v = jnp.concatenate([old_v, new_v], axis=0)
        chips.append((keep, swap_core(send)))

    residuals = []
    for c in range(CHUNKS):
        chip = call(add_pair, [VMEM] * 2, wide, moved=8 * rows * width)(*chips[c])
        resid = call(functools.partial(residual, c), [VMEM] * 4, wide, moved=8 * rows * width)(
            chip, swap_across(chip), tokens, across
        )
        residuals.append((resid, swap_core(resid)))

    ends = []
    for c in range(CHUNKS):
        keep, send = call(
            functools.partial(feed_forward, c, held, low_gu, rank),
            [SMEM] * 3 + [VMEM] * 11,
            [kept, wide],
            flops=2 * rows * 4 * width * hidden_width * 3,
            moved=2 * 4 * width * hidden_width * 3,
            scratch=[pltpu.VMEM((wanted * rank, hidden_width), bf16)] * 3,
        )(
            index, request_adapter_index, lengths, *residuals[c], *tables, received_second,
            gain_two, gate_weight, up_weight, down_weight,
        )
        stay, away = call(
            split_pair, [VMEM] * 2,
            [shaped((rows, width), f32), shaped((rows, width), bf16)], moved=8 * rows * width,
        )(keep, swap_core(send))
        ends += [stay, swap_across(away), residuals[c][0]]
    return call(
        functools.partial(finish, CHUNKS), [VMEM] * (3 * CHUNKS), shaped((row_count, width), bf16),
        moved=8 * row_count * width,
    )(*ends)


def solution(mesh):
    placed = (
        P("req", "tp"),
        P("req", None),
        P("req", None),
        P(),
        P(),
        P(),
        P(),
        P(None, "tp"),
        P(None, "tp"),
        P(None, "tp"),
        P("tp", None),
        P(None, "tp"),
        P(None, "tp"),
        P("tp", None),
        P("req", None, "tp"),
        P("req", None, "tp"),
        P("req", None, "tp"),
        P("req", None, "tp"),
        P("req", None, "tp"),
        P("req", None, "tp"),
        P("req", None, "tp"),
        P("req", None, "tp"),
        P("req", None, "tp"),
        P("req", None, "tp"),
        P("req", None, "tp"),
    )
    return jax.shard_map(
        per_device, mesh=mesh, in_specs=placed, out_specs=P("req", "tp"), check_vma=False
    )
```

time: 597 us -> 146 us (0.24)
  blocking collectives: 198 us -> 0 us
  waiting for transfers between devices: 217 us -> 59.5 us
  local copies, waits for them, and re-layouts: 65.6 us -> 22.2 us
  matrix products: 38.9 us -> 0 us
  other arithmetic: 35.2 us -> 1.86 us
  Pallas kernels: 0 us -> 30.3 us
  between operations: 13.9 us -> 2.24 us
    all_to_all x5 -> x3, waiting for transfers between devices: 180 us -> 6.39 us  [to_groups(): lax.all_to_all(values, 'req', split_axis=0, concat_axis=0, tiled=True)]
    all_to_all x4 -> x0, blocking collectives: 145 us -> none  [the longest x3 112 us: remote_delta(): lax.all_to_all(picked, 'req', split_axis=0, concat_axis=0, tiled=True)]
    psum x4 -> x0, blocking collectives: 53.1 us -> none  [remote_delta(): low_rank = lax.psum(partial_low, 'tp').astype(jnp.bfloat16)]
    ppermute x0 -> x19, waiting for transfers between devices: none -> 53.1 us  [the longest x7 48.2 us: swap_across(): return lax.ppermute(values, 'tp', [(k, k ^ 2) for k in range(4)])]
    gather x9 -> x0, local copies, waits for them, and re-layouts: 47.2 us -> none  [the longest x4 24.5 us: remote_delta(): jnp.take(inputs, source_row.reshape(-1), axis=0)]
    dot_general x20 -> x0, matrix products: 38.9 us -> none  [the longest x1 5.48 us: per_device(): jnp.dot(feedforward_normalized, gate_weight, preferred_element_type=jnp.f...]
    all_gather x2 -> x0, waiting for transfers between devices: 36.5 us -> none  [gather_features(): return lax.all_gather(shard, 'tp', axis=1, tiled=True)]
    pallas_call x0 -> x16, Pallas kernels: none -> 30.3 us  [the longest x2 11.1 us: per_device(): call(functools.partial(feed_forward, c, held, low_gu, rank), [SMEM] * 3 +...]
  transfers between devices with their start and end apart: 9 -> 22, of which waited for: 6 -> 12; matrix products, arithmetic and copies ran while one was open for 9% -> 2% of each run, Pallas kernels for 0% -> 19%
where the time goes in v1:
time: 146 us; the launch traced here: 145 us
  waiting for transfers between devices  59.5 us (41%)
  Pallas kernels  30.3 us (21%)
  starting transfers between devices  28.6 us (20%)
  local copies, waits for them, and re-layouts  22.2 us (15%)
  between operations  2.24 us (2%)
  other arithmetic  1.86 us (1%)
    ppermute x7, waiting for transfers between devices, swap_across(): return lax.ppermute(values, 'tp', [(k, k ^ 2) for k in range(4)])  48.2 us
    unnamed x68, local copies, waits for them, and re-layouts  19.3 us
    all_to_all x3, starting transfers between devices, to_groups(): lax.all_to_all(values, 'req', split_axis=0, concat_axis=0, tiled=True)  16.4 us
    pallas_call x2, Pallas kernels, per_device(): call(functools.partial(feed_forward, c, held, low_gu, rank), [SMEM] * 3 +...  11.1 us
    ppermute x7, starting transfers between devices, swap_across(): return lax.ppermute(values, 'tp', [(k, k ^ 2) for k in range(4)])  9.82 us
    pallas_call x2, Pallas kernels, per_device(): call(functools.partial(attend, c, held, low_qkv, rank, heads, kv_heads),...  8.57 us
    all_to_all x3, waiting for transfers between devices, to_groups(): lax.all_to_all(values, 'req', split_axis=0, concat_axis=0, tiled=True)  6.39 us
    ppermute x11, waiting for transfers between devices, swap_core(): return lax.ppermute(values, 'tp', [(k, k ^ 1) for k in range(4)])  3.38 us
  transfers between devices with their start and end apart: 22, of which 12 were waited for; matrix products, arithmetic and copies ran while one was open for 2% of the time, Pallas kernels for 19%

profile of v1, /device:TPU:0, one launch (start us, length us, event | category | flops | bytes accessed | tf_op | source)
XLA Modules:
  0.0 144.7 jit_solution(13341594489998292628)
XLA Ops:
  0.0 1.2 broadcast_in_dim.15
  1.2 7.3 %all-to-all-start = ((s32[8,1,4]{2,1,0:T(1,128)}), s32[8,1,4]{2,1,0:T(1,128)S(1)}, u32[]{:S(2)}, u32[]{:S(2)}) async-start(s32[8,1,4]{2,1,0:T(1,128)} %broadcast_in_dim.15), calls=%async_computation | async-start | bytes 8192 | tf_op jit(solution)/shard_map/all_to_all | solution.py:360
  8.5 6.4 %all-to-all-done = s32[8,1,4]{2,1,0:T(1,128)S(1)} async-done(((s32[8,1,4]{2,1,0:T(1,128)}), s32[8,1,4]{2,1,0:T(1,128)S(1)}, u32[]{:S(2)}, u32[]{:S(2)}) %all-to-all-start) | async-done | bytes 160 | tf_op jit(solution)/shard_map/all_to_all | solution.py:360
  19.7 1.8 %shard_map.239 = bf16[8,112,512]{2,1,0:T(8,128)(2,1)} custom-call(s32[1]{0:T(128)} %bitcast.2.me_ref, s32[8,4]{1,0:T(8,128)S(1)} %copy.29.idx_ref, bf16[2,48,512]{2,1,0:T(8,128)(2,1)S(1)} %copy-done.11, bf16[2,16,512]{2,1,0:T(8,128)(2,1)S(1)} %copy-done.17, bf16[2,16,512]{2,1,0:T(8,128)(2,1)S(1)} %copy-done.18, bf16[2,16,512]{2,1,0:T(8,128)(2,1)S(1)} %copy-done.19, ...), custom_call_target="tpu_custom_call" | custom-call | bytes 917504 | tf_op jit(solution)/shard_map/pallas_call | solution.py:408
  21.5 3.6 %all-to-all-start.1 = ((bf16[8,112,512]{2,1,0:T(8,128)(2,1)}), bf16[8,112,512]{2,1,0:T(8,128)(2,1)S(1)}, u32[]{:S(2)}, u32[]{:S(2)}) async-start(bf16[8,112,512]{2,1,0:T(8,128)(2,1)} %shard_map.239), calls=%async_computation.1 | async-start | bytes 1835008 | tf_op jit(solution)/shard_map/all_to_all | solution.py:360
  25.1 1.6 %collective-permute-start.1 = (bf16[512,512]{1,0:T(8,128)(2,1)}, bf16[512,512]{1,0:T(8,128)(2,1)S(1)}, u32[]{:S(2)}, u32[]{:S(2)}) collective-permute-start(bf16[512,512]{1,0:T(8,128)(2,1)} %own.5), channel_id=1, source_target_pairs={{0,2},{1,3},{2,0},{3,1},{4,6},{5,7},{6,4},{7,5},{8,10},{9,11},{10,... | collective-permute-start | bytes 1572872 | tf_op jit(solution)/shard_map/ppermute | solution.py:352
  26.7 10.9 %collective-permute-done.1.across = bf16[512,512]{1,0:T(8,128)(2,1)S(1)} collective-permute-done((bf16[512,512]{1,0:T(8,128)(2,1)}, bf16[512,512]{1,0:T(8,128)(2,1)S(1)}, u32[]{:S(2)}, u32[]{:S(2)}) %collective-permute-start.1) | collective-permute-done | bytes 524320 | tf_op jit(solution)/shard_map/ppermute | solution.py:352
  37.6 1.4 fusion.1
  41.4 1.6 %copy-done.27 = bf16[2048,512]{1,0:T(8,128)(2,1)S(1)} copy-done((bf16[2048,512]{1,0:T(8,128)(2,1)S(1)}, bf16[2048,512]{1,0:T(8,128)(2,1)}, u32[]{:S(2)}) %copy-start.27) | copy-done | bytes 2097176
  47.2 2.6 %shard_map.238 = (bf16[512,512]{1,0:T(8,128)(2,1)S(1)}, f32[256,1024]{1,0:T(8,128)S(1)}, f32[256,1024]{1,0:T(8,128)S(1)}) custom-call(s32[1]{0:T(128)} %bitcast.index_ref, bf16[512,512]{1,0:T(8,128)(2,1)S(1)} %copy-done.5, bf16[512,512]{1,0:T(8,128)(2,1)S(1)} %collective-permute-done.core, bf16[512,512]{1,0:T(8,128)(2,1)S(1)} %collective-permute-done.1.across, ...), custom_call_target="tpu_custom_call" | custom-call | flops 2147483648 | bytes 4194304 | tf_op jit(solution)/shard_map/pallas_call | solution.py:425
  52.0 1.9 %shard_map.244 = bf16[8,240,256]{2,1,0:T(8,128)(2,1)} custom-call(s32[1]{0:T(128)} %bitcast.2.me_ref, s32[8,4]{1,0:T(8,128)S(1)} %copy.30.idx_ref, bf16[2,32,512]{2,1,0:T(8,128)(2,1)S(1)} %copy-done.12, bf16[2,16,512]{2,1,0:T(8,128)(2,1)S(1)} %copy-done.20, bf16[2,16,768]{2,1,0:T(8,128)(2,1)S(1)} %copy-done.13, bf16[2,16,768]{2,1,0:T(8,128)(2,1)S(1)} %copy-done.14, ...), custom_call_target="tpu_custom_call" | custom-call | bytes 983040 | tf_op jit(solution)/shard_map/pallas_call | solution.py:433
  53.8 5.6 %all-to-all-start.2 = ((bf16[8,240,256]{2,1,0:T(8,128)(2,1)}), bf16[8,240,256]{2,1,0:T(8,128)(2,1)S(1)}, u32[]{:S(2)}, u32[]{:S(2)}) async-start(bf16[8,240,256]{2,1,0:T(8,128)(2,1)} %shard_map.244), calls=%async_computation.2 | async-start | bytes 1966080 | tf_op jit(solution)/shard_map/all_to_all | solution.py:360
  63.2 1.6 %collective-permute-start.4 = (bf16[112,512]{1,0:T(8,128)(2,1)S(1)}, bf16[112,512]{1,0:T(8,128)(2,1)S(1)}, u32[]{:S(2)}, u32[]{:S(2)}) collective-permute-start(bf16[112,512]{1,0:T(8,128)(2,1)S(1)} %shard_map.240.shared0), channel_id=1, source_target_pairs={{0,2},{1,3},{2,0},{3,1},{4,6},{5,7},{6,4},{7,5},{8,10},{9,11},{10,... | collective-permute-start | bytes 344072 | tf_op jit(solution)/shard_map/ppermute | solution.py:352
  66.1 3.1 %collective-permute-done.4.shared2 = bf16[112,512]{1,0:T(8,128)(2,1)S(1)} collective-permute-done((bf16[112,512]{1,0:T(8,128)(2,1)S(1)}, bf16[112,512]{1,0:T(8,128)(2,1)S(1)}, u32[]{:S(2)}, u32[]{:S(2)}) %collective-permute-start.4) | collective-permute-done | bytes 114720 | tf_op jit(solution)/shard_map/ppermute | solution.py:352
  69.2 1.6 %collective-permute-done.5.shared3 = bf16[112,512]{1,0:T(8,128)(2,1)S(1)} collective-permute-done((bf16[112,512]{1,0:T(8,128)(2,1)S(1)}, bf16[112,512]{1,0:T(8,128)(2,1)S(1)}, u32[]{:S(2)}, u32[]{:S(2)}) %collective-permute-start.5) | collective-permute-done | bytes 114720 | tf_op jit(solution)/shard_map/ppermute | solution.py:356
  72.0 4.4 %shard_map.241 = (f32[256,1024]{1,0:T(8,128)S(1)}, bf16[256,1024]{1,0:T(8,128)(2,1)S(1)}, bf16[256,256]{1,0:T(8,128)(2,1)S(1)}, bf16[256,256]{1,0:T(8,128)(2,1)S(1)}) custom-call(s32[1]{0:T(128)} %bitcast.index_ref, s32[1,4]{1,0:T(1,128)S(1)} %copy-done.22, s32[1,4]{1,0:T(1,128)S(1)} %copy-done.16, f32[256,1024]{1,0:T(8,128)S(1)} %copy-done.10, ...), custom_call_target="tpu_custom_call" | custom-call | flops 805306368 | bytes 2097152 | tf_op jit(solution)/shard_map/pallas_call | solution.py:468
  76.4 4.2 %shard_map.248 = (f32[256,1024]{1,0:T(8,128)S(1)}, bf16[256,1024]{1,0:T(8,128)(2,1)S(1)}, bf16[256,256]{1,0:T(8,128)(2,1)}, bf16[256,256]{1,0:T(8,128)(2,1)}) custom-call(s32[1]{0:T(128)} %bitcast.index_ref, s32[1,4]{1,0:T(1,128)S(1)} %copy-done.22, s32[1,4]{1,0:T(1,128)S(1)} %copy-done.16, f32[256,1024]{1,0:T(8,128)S(1)} %copy-done.8, ...), custom_call_target="tpu_custom_call" | custom-call | flops 805306368 | bytes 2097152 | tf_op jit(solution)/shard_map/pallas_call | solution.py:468
  81.4 1.5 %collective-permute-done.14.arrived = bf16[256,1024]{1,0:T(8,128)(2,1)S(1)} collective-permute-done((bf16[256,1024]{1,0:T(8,128)(2,1)S(1)}, bf16[256,1024]{1,0:T(8,128)(2,1)S(1)}, u32[]{:S(2)}, u32[]{:S(2)}) %collective-permute-start.14) | collective-permute-done | bytes 524320 | tf_op jit(solution)/shard_map/ppermute | solution.py:348
  82.9 1.5 %collective-permute-start.15 = (bf16[256,1024]{1,0:T(8,128)(2,1)S(1)}, bf16[256,1024]{1,0:T(8,128)(2,1)S(1)}, u32[]{:S(2)}, u32[]{:S(2)}) collective-permute-start(bf16[256,1024]{1,0:T(8,128)(2,1)S(1)} %shard_map.249.chip), channel_id=1, source_target_pairs={{0,2},{1,3},{2,0},{3,1},{4,6},{5,7},{6,4},{7,5},{8,10},{9,11},{10,... | collective-permute-start | bytes 1572872 | tf_op jit(solution)/shard_map/ppermute | solution.py:352
  85.2 12.5 %collective-permute-done.15.arrived = bf16[256,1024]{1,0:T(8,128)(2,1)S(1)} collective-permute-done((bf16[256,1024]{1,0:T(8,128)(2,1)S(1)}, bf16[256,1024]{1,0:T(8,128)(2,1)S(1)}, u32[]{:S(2)}, u32[]{:S(2)}) %collective-permute-start.15) | collective-permute-done | bytes 524320 | tf_op jit(solution)/shard_map/ppermute | solution.py:352
  98.6 1.5 %collective-permute-start.10 = (bf16[192,512]{1,0:T(8,128)(2,1)S(1)}, bf16[192,512]{1,0:T(8,128)(2,1)S(1)}, u32[]{:S(2)}, u32[]{:S(2)}) collective-permute-start(bf16[192,512]{1,0:T(8,128)(2,1)S(1)} %shard_map.245.table0), channel_id=1, source_target_pairs={{0,2},{1,3},{2,0},{3,1},{4,6},{5,7},{6,4},{7,5},{8,10},{9,11},{10,... | collective-permute-start | bytes 589832 | tf_op jit(solution)/shard_map/ppermute | solution.py:352
  100.2 8.9 %collective-permute-done.7.arrived = bf16[256,1024]{1,0:T(8,128)(2,1)} collective-permute-done((bf16[256,1024]{1,0:T(8,128)(2,1)S(1)}, bf16[256,1024]{1,0:T(8,128)(2,1)}, u32[]{:S(2)}, u32[]{:S(2)}) %collective-permute-start.7) | collective-permute-done | bytes 524320 | tf_op jit(solution)/shard_map/ppermute | solution.py:352
  110.9 1.7 %collective-permute-done.10.table2 = bf16[192,512]{1,0:T(8,128)(2,1)S(1)} collective-permute-done((bf16[192,512]{1,0:T(8,128)(2,1)S(1)}, bf16[192,512]{1,0:T(8,128)(2,1)S(1)}, u32[]{:S(2)}, u32[]{:S(2)}) %collective-permute-start.10) | collective-permute-done | bytes 196640 | tf_op jit(solution)/shard_map/ppermute | solution.py:352
  112.7 1.4 collective-permute-done.11.table3
  114.1 1.9 %copy-done.1 = bf16[2048,768]{1,0:T(8,128)(2,1)S(1)} copy-done((bf16[2048,768]{1,0:T(8,128)(2,1)S(1)}, bf16[2048,768]{1,0:T(8,128)(2,1)}, u32[]{:S(2)}) %copy-start.1) | copy-done | bytes 3145752
  116.0 1.9 %copy-done.2 = bf16[768,2048]{1,0:T(8,128)(2,1)S(1)} copy-done((bf16[768,2048]{1,0:T(8,128)(2,1)S(1)}, bf16[768,2048]{1,0:T(8,128)(2,1)}, u32[]{:S(2)}) %copy-start.2) | copy-done | bytes 3145752
  117.9 5.8 %shard_map.251 = (f32[256,1024]{1,0:T(8,128)S(1)}, bf16[256,1024]{1,0:T(8,128)(2,1)S(1)}) custom-call(s32[1]{0:T(128)} %bitcast.index_ref, s32[1,4]{1,0:T(1,128)S(1)} %copy-done.22, s32[1,4]{1,0:T(1,128)S(1)} %copy-done.16, bf16[256,1024]{1,0:T(8,128)(2,1)S(1)} %shard_map.250.mine.refs_5_, bf16[256,1024]{1,0:T(8,128)(2,1)} %collective-permute-done.16.theirs, ...), custom_call_target="tpu_custom_call" | custom-call | flops 2415919104 | bytes 9437184 | tf_op jit(solution)/shard_map/pallas_call | solution.py:501
  123.9 5.3 %shard_map.246 = (f32[256,1024]{1,0:T(8,128)S(1)}, bf16[256,1024]{1,0:T(8,128)(2,1)S(1)}) custom-call(s32[1]{0:T(128)} %bitcast.index_ref, s32[1,4]{1,0:T(1,128)S(1)} %copy-done.22, s32[1,4]{1,0:T(1,128)S(1)} %copy-done.16, bf16[256,1024]{1,0:T(8,128)(2,1)S(1)} %shard_map.243.mine.refs_2_, bf16[256,1024]{1,0:T(8,128)(2,1)S(1)} %collective-permute-done.8.theirs, ...), custom_call_target="tpu_custom_call" | custom-call | flops 2415919104 | bytes 9437184 | tf_op jit(solution)/shard_map/pallas_call | solution.py:501
  129.7 1.5 %collective-permute-start.18 = (bf16[256,512]{1,0:T(8,128)(2,1)S(1)}, bf16[256,512]{1,0:T(8,128)(2,1)S(1)}, u32[]{:S(2)}, u32[]{:S(2)}) collective-permute-start(bf16[256,512]{1,0:T(8,128)(2,1)S(1)} %get-tuple-element.42), channel_id=1, source_target_pairs={{0,2},{1,3},{2,0},{3,1},{4,6},{5,7},{6,4},{7,5},{8,10},{9,11},{10,... | collective-permute-start | bytes 786440 | tf_op jit(solution)/shard_map/ppermute | solution.py:352
  131.4 1.5 %collective-permute-start.13 = (bf16[256,512]{1,0:T(8,128)(2,1)S(1)}, bf16[256,512]{1,0:T(8,128)(2,1)S(1)}, u32[]{:S(2)}, u32[]{:S(2)}) collective-permute-start(bf16[256,512]{1,0:T(8,128)(2,1)S(1)} %get-tuple-element.33), channel_id=1, source_target_pairs={{0,2},{1,3},{2,0},{3,1},{4,6},{5,7},{6,4},{7,5},{8,10},{9,11},{10,... | collective-permute-start | bytes 786440 | tf_op jit(solution)/shard_map/ppermute | solution.py:352
  132.8 6.1 %collective-permute-done.18.refs_4_ = bf16[256,512]{1,0:T(8,128)(2,1)S(1)} collective-permute-done((bf16[256,512]{1,0:T(8,128)(2,1)S(1)}, bf16[256,512]{1,0:T(8,128)(2,1)S(1)}, u32[]{:S(2)}, u32[]{:S(2)}) %collective-permute-start.18) | collective-permute-done | bytes 262176 | tf_op jit(solution)/shard_map/ppermute | solution.py:352
  138.9 4.8 %collective-permute-done.13.refs_1_ = bf16[256,512]{1,0:T(8,128)(2,1)S(1)} collective-permute-done((bf16[256,512]{1,0:T(8,128)(2,1)S(1)}, bf16[256,512]{1,0:T(8,128)(2,1)S(1)}, u32[]{:S(2)}, u32[]{:S(2)}) %collective-permute-start.13) | collective-permute-done | bytes 262176 | tf_op jit(solution)/shard_map/ppermute | solution.py:352
  (106 shorter events, 23.8 us)
Async XLA Ops:
  1.2 13.7 %all-to-all-start = ((s32[8,1,4]{2,1,0:T(1,128)}), s32[8,1,4]{2,1,0:T(1,128)S(1)}, u32[]{:S(2)}, u32[]{:S(2)}) async-start(s32[8,1,4]{2,1,0:T(1,128)} %broadcast_in_dim.15), calls=%async_computation | async-start | bytes 8192 | tf_op jit(solution)/shard_map/all_to_all | solution.py:360
  21.5 32.3 %all-to-all-start.1 = ((bf16[8,112,512]{2,1,0:T(8,128)(2,1)}), bf16[8,112,512]{2,1,0:T(8,128)(2,1)S(1)}, u32[]{:S(2)}, u32[]{:S(2)}) async-start(bf16[8,112,512]{2,1,0:T(8,128)(2,1)} %shard_map.239), calls=%async_computation.1 | async-start | bytes 1835008 | tf_op jit(solution)/shard_map/all_to_all | solution.py:360
  25.1 12.5 %collective-permute-start.1 = (bf16[512,512]{1,0:T(8,128)(2,1)}, bf16[512,512]{1,0:T(8,128)(2,1)S(1)}, u32[]{:S(2)}, u32[]{:S(2)}) collective-permute-start(bf16[512,512]{1,0:T(8,128)(2,1)} %own.5), channel_id=1, source_target_pairs={{0,2},{1,3},{2,0},{3,1},{4,6},{5,7},{6,4},{7,5},{8,10},{9,11},{10,... | collective-permute-start | bytes 1572872 | tf_op jit(solution)/shard_map/ppermute | solution.py:352
  26.7 12.4 %collective-permute-start = (bf16[512,512]{1,0:T(8,128)(2,1)}, bf16[512,512]{1,0:T(8,128)(2,1)S(1)}, u32[]{:S(2)}, u32[]{:S(2)}) collective-permute-start(bf16[512,512]{1,0:T(8,128)(2,1)} %own.5), channel_id=1, source_target_pairs={{0,1},{1,0},{2,3},{3,2},{4,5},{5,4},{6,7},{7,6},{8,9},{9,8},{10,11... | collective-permute-start | bytes 1572872 | tf_op jit(solution)/shard_map/ppermute | solution.py:348
  37.6 1.9 %collective-permute-start.2 = (bf16[512,512]{1,0:T(8,128)(2,1)S(1)}, bf16[512,512]{1,0:T(8,128)(2,1)S(1)}, u32[]{:S(2)}, u32[]{:S(2)}) collective-permute-start(bf16[512,512]{1,0:T(8,128)(2,1)S(1)} %collective-permute-done.1.across), channel_id=1, source_target_pairs={{0,1},{1,0},{2,3},{3,2},{4,5},{5,4},{6,7},{7,6},{8,9},{9,8},{10,11... | collective-permute-start | bytes 1572872 | tf_op jit(solution)/shard_map/ppermute | solution.py:348
  51.8 10.4 %copy-start.16 = (s32[1,4]{1,0:T(1,128)S(1)}, s32[1,4]{1,0:T(1,128)}, u32[]{:S(2)}) copy-start(s32[1,4]{1,0:T(1,128)} %lens_ref.9) | copy-start | bytes 52
  51.8 10.4 %copy-start.22 = (s32[1,4]{1,0:T(1,128)S(1)}, s32[1,4]{1,0:T(1,128)}, u32[]{:S(2)}) copy-start(s32[1,4]{1,0:T(1,128)} %want_ref.11) | copy-start | bytes 52
  51.8 13.3 %copy-start.33 = (f32[128]{0:T(128)S(1)}, f32[128]{0:T(128)}, u32[]{:S(2)}) copy-start(f32[128]{0:T(128)} %constant.23.clone.1) | copy-start | bytes 1540
  51.8 19.0 %copy-start.25 = (f32[128]{0:T(128)S(1)}, f32[128]{0:T(128)}, u32[]{:S(2)}) copy-start(f32[128]{0:T(128)} %param.29) | copy-start | bytes 1540
  51.8 19.0 %copy-start.26 = (f32[128]{0:T(128)S(1)}, f32[128]{0:T(128)}, u32[]{:S(2)}) copy-start(f32[128]{0:T(128)} %param.30) | copy-start | bytes 1540
  53.8 44.2 %all-to-all-start.2 = ((bf16[8,240,256]{2,1,0:T(8,128)(2,1)}), bf16[8,240,256]{2,1,0:T(8,128)(2,1)S(1)}, u32[]{:S(2)}, u32[]{:S(2)}) async-start(bf16[8,240,256]{2,1,0:T(8,128)(2,1)} %shard_map.244), calls=%async_computation.2 | async-start | bytes 1966080 | tf_op jit(solution)/shard_map/all_to_all | solution.py:360
  61.4 9.4 %copy-start.4 = (bf16[512,2048]{1,0:T(8,128)(2,1)S(1)}, bf16[512,2048]{1,0:T(8,128)(2,1)}, u32[]{:S(2)}) copy-start(bf16[512,2048]{1,0:T(8,128)(2,1)} %out_w.3) | copy-start | bytes 6291460
  63.1 13.3 %copy-start.8 = (f32[256,1024]{1,0:T(8,128)S(1)}, f32[256,1024]{1,0:T(8,128)}, u32[]{:S(2)}) copy-start(f32[256,1024]{1,0:T(8,128)} %copy-done.7) | copy-start | bytes 3145732
  63.1 2.9 %collective-permute-start.3 = (bf16[112,512]{1,0:T(8,128)(2,1)S(1)}, bf16[112,512]{1,0:T(8,128)(2,1)S(1)}, u32[]{:S(2)}, u32[]{:S(2)}) collective-permute-start(bf16[112,512]{1,0:T(8,128)(2,1)S(1)} %shard_map.240.shared0), channel_id=1, source_target_pairs={{0,1},{1,0},{2,3},{3,2},{4,5},{5,4},{6,7},{7,6},{8,9},{9,8},{10,11... | collective-permute-start | bytes 344072 | tf_op jit(solution)/shard_map/ppermute | solution.py:348
  63.2 6.0 %collective-permute-start.4 = (bf16[112,512]{1,0:T(8,128)(2,1)S(1)}, bf16[112,512]{1,0:T(8,128)(2,1)S(1)}, u32[]{:S(2)}, u32[]{:S(2)}) collective-permute-start(bf16[112,512]{1,0:T(8,128)(2,1)S(1)} %shard_map.240.shared0), channel_id=1, source_target_pairs={{0,2},{1,3},{2,0},{3,1},{4,6},{5,7},{6,4},{7,5},{8,10},{9,11},{10,... | collective-permute-start | bytes 344072 | tf_op jit(solution)/shard_map/ppermute | solution.py:352
  64.8 6.0 %collective-permute-start.5 = (bf16[112,512]{1,0:T(8,128)(2,1)S(1)}, bf16[112,512]{1,0:T(8,128)(2,1)S(1)}, u32[]{:S(2)}, u32[]{:S(2)}) collective-permute-start(bf16[112,512]{1,0:T(8,128)(2,1)S(1)} %shard_map.240.shared0), channel_id=1, source_target_pairs={{0,3},{1,2},{2,1},{3,0},{4,7},{5,6},{6,5},{7,4},{8,11},{9,10},{10,... | collective-permute-start | bytes 344072 | tf_op jit(solution)/shard_map/ppermute | solution.py:356
  80.6 17.1 %copy-start.6 = (bf16[512,512]{1,0:T(8,128)(2,1)S(1)}, bf16[512,512]{1,0:T(8,128)(2,1)}, u32[]{:S(2)}) copy-start(bf16[512,512]{1,0:T(8,128)(2,1)} %own.5) | copy-start | bytes 1572868
  80.6 2.2 %collective-permute-start.14 = (bf16[256,1024]{1,0:T(8,128)(2,1)S(1)}, bf16[256,1024]{1,0:T(8,128)(2,1)S(1)}, u32[]{:S(2)}, u32[]{:S(2)}) collective-permute-start(bf16[256,1024]{1,0:T(8,128)(2,1)S(1)} %get-tuple-element.38), channel_id=1, source_target_pairs={{0,1},{1,0},{2,3},{3,2},{4,5},{5,4},{6,7},{7,6},{8,9},{9,8},{10,11... | collective-permute-start | bytes 1572872 | tf_op jit(solution)/shard_map/ppermute | solution.py:348
  81.3 3.2 %collective-permute-start.6 = (bf16[256,1024]{1,0:T(8,128)(2,1)S(1)}, bf16[256,1024]{1,0:T(8,128)(2,1)S(1)}, u32[]{:S(2)}, u32[]{:S(2)}) collective-permute-start(bf16[256,1024]{1,0:T(8,128)(2,1)S(1)} %get-tuple-element.28), channel_id=1, source_target_pairs={{0,1},{1,0},{2,3},{3,2},{4,5},{5,4},{6,7},{7,6},{8,9},{9,8},{10,11... | collective-permute-start | bytes 1572872 | tf_op jit(solution)/shard_map/ppermute | solution.py:348
  82.9 14.8 %collective-permute-start.15 = (bf16[256,1024]{1,0:T(8,128)(2,1)S(1)}, bf16[256,1024]{1,0:T(8,128)(2,1)S(1)}, u32[]{:S(2)}, u32[]{:S(2)}) collective-permute-start(bf16[256,1024]{1,0:T(8,128)(2,1)S(1)} %shard_map.249.chip), channel_id=1, source_target_pairs={{0,2},{1,3},{2,0},{3,1},{4,6},{5,7},{6,4},{7,5},{8,10},{9,11},{10,... | collective-permute-start | bytes 1572872 | tf_op jit(solution)/shard_map/ppermute | solution.py:352
  84.6 29.5 %copy-start.21 = (f32[2048]{0:T(1024)S(1)}, f32[2048]{0:T(1024)}, u32[]{:S(2)}) copy-start(f32[2048]{0:T(1024)} %param.31) | copy-start | bytes 24580
  84.6 24.5 %collective-permute-start.7 = (bf16[256,1024]{1,0:T(8,128)(2,1)S(1)}, bf16[256,1024]{1,0:T(8,128)(2,1)}, u32[]{:S(2)}, u32[]{:S(2)}) collective-permute-start(bf16[256,1024]{1,0:T(8,128)(2,1)S(1)} %shard_map.242.chip), channel_id=1, source_target_pairs={{0,2},{1,3},{2,0},{3,1},{4,6},{5,7},{6,4},{7,5},{8,10},{9,11},{10,... | collective-permute-start | bytes 1572872 | tf_op jit(solution)/shard_map/ppermute | solution.py:352
  97.9 16.1 %collective-permute-start.16 = (bf16[256,1024]{1,0:T(8,128)(2,1)S(1)}, bf16[256,1024]{1,0:T(8,128)(2,1)}, u32[]{:S(2)}, u32[]{:S(2)}) collective-permute-start(bf16[256,1024]{1,0:T(8,128)(2,1)S(1)} %shard_map.250.mine.refs_5_), channel_id=1, source_target_pairs={{0,1},{1,0},{2,3},{3,2},{4,5},{5,4},{6,7},{7,6},{8,9},{9,8},{10,11... | collective-permute-start | bytes 1572872 | tf_op jit(solution)/shard_map/ppermute | solution.py:348
  98.0 16.1 %copy-start = (bf16[2048,768]{1,0:T(8,128)(2,1)S(1)}, bf16[2048,768]{1,0:T(8,128)(2,1)}, u32[]{:S(2)}) copy-start(bf16[2048,768]{1,0:T(8,128)(2,1)} %gate_w.3) | copy-start | bytes 9437188
  98.6 14.0 %collective-permute-start.10 = (bf16[192,512]{1,0:T(8,128)(2,1)S(1)}, bf16[192,512]{1,0:T(8,128)(2,1)S(1)}, u32[]{:S(2)}, u32[]{:S(2)}) collective-permute-start(bf16[192,512]{1,0:T(8,128)(2,1)S(1)} %shard_map.245.table0), channel_id=1, source_target_pairs={{0,2},{1,3},{2,0},{3,1},{4,6},{5,7},{6,4},{7,5},{8,10},{9,11},{10,... | collective-permute-start | bytes 589832 | tf_op jit(solution)/shard_map/ppermute | solution.py:352
  110.3 13.5 %collective-permute-start.8 = (bf16[256,1024]{1,0:T(8,128)(2,1)S(1)}, bf16[256,1024]{1,0:T(8,128)(2,1)S(1)}, u32[]{:S(2)}, u32[]{:S(2)}) collective-permute-start(bf16[256,1024]{1,0:T(8,128)(2,1)S(1)} %shard_map.243.mine.refs_2_), channel_id=1, source_target_pairs={{0,1},{1,0},{2,3},{3,2},{4,5},{5,4},{6,7},{7,6},{8,9},{9,8},{10,11... | collective-permute-start | bytes 1572872 | tf_op jit(solution)/shard_map/ppermute | solution.py:348
  110.4 2.2 %collective-permute-start.9 = (bf16[192,512]{1,0:T(8,128)(2,1)S(1)}, bf16[192,512]{1,0:T(8,128)(2,1)S(1)}, u32[]{:S(2)}, u32[]{:S(2)}) collective-permute-start(bf16[192,512]{1,0:T(8,128)(2,1)S(1)} %shard_map.245.table0), channel_id=1, source_target_pairs={{0,1},{1,0},{2,3},{3,2},{4,5},{5,4},{6,7},{7,6},{8,9},{9,8},{10,11... | collective-permute-start | bytes 589832 | tf_op jit(solution)/shard_map/ppermute | solution.py:348
  112.6 1.4 collective-permute-start.11
  123.7 6.0 %collective-permute-start.17 = (bf16[256,1024]{1,0:T(8,128)(2,1)S(1)}, bf16[256,1024]{1,0:T(8,128)(2,1)S(1)}, u32[]{:S(2)}, u32[]{:S(2)}) collective-permute-start(bf16[256,1024]{1,0:T(8,128)(2,1)S(1)} %get-tuple-element.40), channel_id=1, source_target_pairs={{0,1},{1,0},{2,3},{3,2},{4,5},{5,4},{6,7},{7,6},{8,9},{9,8},{10,11... | collective-permute-start | bytes 1572872 | tf_op jit(solution)/shard_map/ppermute | solution.py:348
  129.2 2.1 %collective-permute-start.12 = (bf16[256,1024]{1,0:T(8,128)(2,1)S(1)}, bf16[256,1024]{1,0:T(8,128)(2,1)S(1)}, u32[]{:S(2)}, u32[]{:S(2)}) collective-permute-start(bf16[256,1024]{1,0:T(8,128)(2,1)S(1)} %get-tuple-element.31), channel_id=1, source_target_pairs={{0,1},{1,0},{2,3},{3,2},{4,5},{5,4},{6,7},{7,6},{8,9},{9,8},{10,11... | collective-permute-start | bytes 1572872 | tf_op jit(solution)/shard_map/ppermute | solution.py:348
  129.7 9.2 %collective-permute-start.18 = (bf16[256,512]{1,0:T(8,128)(2,1)S(1)}, bf16[256,512]{1,0:T(8,128)(2,1)S(1)}, u32[]{:S(2)}, u32[]{:S(2)}) collective-permute-start(bf16[256,512]{1,0:T(8,128)(2,1)S(1)} %get-tuple-element.42), channel_id=1, source_target_pairs={{0,2},{1,3},{2,0},{3,1},{4,6},{5,7},{6,4},{7,5},{8,10},{9,11},{10,... | collective-permute-start | bytes 786440 | tf_op jit(solution)/shard_map/ppermute | solution.py:352
  131.4 12.4 %collective-permute-start.13 = (bf16[256,512]{1,0:T(8,128)(2,1)S(1)}, bf16[256,512]{1,0:T(8,128)(2,1)S(1)}, u32[]{:S(2)}, u32[]{:S(2)}) collective-permute-start(bf16[256,512]{1,0:T(8,128)(2,1)S(1)} %get-tuple-element.33), channel_id=1, source_target_pairs={{0,2},{1,3},{2,0},{3,1},{4,6},{5,7},{6,4},{7,5},{8,10},{9,11},{10,... | collective-permute-start | bytes 786440 | tf_op jit(solution)/shard_map/ppermute | solution.py:352
  (24 other events, 49.2 us)

commit v2 on v1

v2 whole, which is shorter than its diff:
```python
import functools
import math

import jax
import jax.numpy as jnp
from jax import lax
from jax.experimental import pallas as pl
from jax.experimental.pallas import tpu as pltpu
from jax.sharding import PartitionSpec as P

HEAD_WIDTH = 128
CHUNKS = 2

epsilon = 1e-06
rope_base = 1000000.0

bf16 = jnp.bfloat16
f32 = jnp.float32
VMEM = pl.BlockSpec(memory_space=pltpu.VMEM)
ANY = pl.BlockSpec(memory_space=pl.ANY)
HBM = pl.BlockSpec(memory_space=pltpu.HBM)
SMEM = pl.BlockSpec(memory_space=pltpu.SMEM)


def call(body, in_specs, outs, scratch=(), limit=16, out_specs=None):
    single = not isinstance(outs, (list, tuple))
    if out_specs is None:
        out_specs = VMEM if single else [VMEM] * len(outs)
    return pl.pallas_call(
        body,
        out_shape=outs if single else list(outs),
        in_specs=in_specs,
        out_specs=out_specs,
        scratch_shapes=list(scratch),
        compiler_params=pltpu.CompilerParams(vmem_limit_bytes=limit * 1024 * 1024),
        cost_estimate=pl.CostEstimate(flops=1, bytes_accessed=1, transcendentals=0),
    )


def shaped(shape, dtype):
    return jax.ShapeDtypeStruct(shape, dtype)


def dot(a, b):
    return lax.dot_general(a, b, (((1,), (0,)), ((), ())), preferred_element_type=f32)


def dot_nt(a, b):
    return lax.dot_general(a, b, (((1,), (1,)), ((), ())), preferred_element_type=f32)


def dot_tn(a, b):
    return lax.dot_general(a, b, (((0,), (0,)), ((), ())), preferred_element_type=f32)


def part_of(index_ref, rel, width):
    return pl.ds(pl.multiple_of((index_ref[0] ^ rel) * width, width), width)


def bounds(lens_ref, count):
    starts, total = [], jnp.int32(0)
    for j in range(count):
        starts.append(total)
        total = total + lens_ref[0, j]
    return starts, starts[1:] + [total]


def lane_masks(lens_ref, count, first, width):
    starts, ends = bounds(lens_ref, count)
    rows = lax.broadcasted_iota(jnp.int32, (1, width), 1) + first
    return [((rows >= s) & (rows < e)).astype(f32) for s, e in zip(starts, ends)]


def spread(piece, masks):
    return jnp.concatenate([piece * m for m in masks], axis=0).astype(bf16)


def merged(products, masks, low):
    return sum(products[j * low : (j + 1) * low, :] * m for j, m in enumerate(masks))


def delta(piece, masks, stack):
    return dot_tn(spread(piece, masks), stack).astype(bf16).astype(f32)


def start_all(pairs, sems):
    copies = [pltpu.make_async_copy(a, b, sems.at[k]) for k, (a, b) in enumerate(pairs)]
    for copy in copies:
        copy.start()
    return copies


def gather_tables(plans, *refs):
    *refs, sems = refs
    pairs = []
    for plan, out in zip(plans, refs[-len(plans) :]):
        for table, columns, row, column in plan:
            source = refs[table]
            there = out.at[:, pl.ds(row, source.shape[1]), pl.ds(column, columns[1])]
            pairs.append((source.at[:, :, pl.ds(*columns)], there))
    for copy in start_all(pairs, sems):
        copy.wait()


def load(count, *refs):
    for copy in start_all(list(zip(refs[:count], refs[-1 - count : -1])), refs[-1]):
        copy.wait()


def owner_at(me_ref, rel, flip):
    return me_ref[0] ^ (2 * rel + flip)


def pick_for_neighbour(me_ref, want_ref, *refs):
    *packed, after, send = refs
    held = packed[0].shape[0]
    for rel, ref in enumerate(packed):
        owner = owner_at(me_ref, rel, 0)
        pick = jnp.int32(0)
        for j in range(want_ref.shape[1]):
            a = want_ref[0, j]
            pick = pick + jnp.where(a // held == owner, a % held, 0)
        send[rel] = ref[pick]


def hold(block, after, out):
    out[...] = block[...]


def each_asked(me_ref, want_ref, packed, passed, use):
    held = packed[0].shape[0]
    for rel, ref in enumerate(packed):
        for flip in range(2):
            owner = owner_at(me_ref, rel, flip)
            slot, pick, found = jnp.int32(0), jnp.int32(0), jnp.int32(0)
            for j in range(want_ref.shape[1]):
                a = want_ref[0, j]
                hit = (a // held == owner).astype(jnp.int32)
                slot, pick, found = slot + hit * j, pick + hit * (a % held), found + hit

            @pl.when(found > 0)
            def _():
                use(slot, passed.at[rel] if flip else ref.at[pick])


def normalize(index_ref, refs, gain, normed, keep_own=None):
    blocks = [load() for load in refs]
    width = blocks[0].shape[1]
    square = sum(jnp.sum(b * b, axis=1, keepdims=True) for b in blocks)
    scale = lax.rsqrt(square / (len(blocks) * width) + epsilon)
    for rel, block in enumerate(blocks):
        part = part_of(index_ref, rel, width)
        value = (block * scale * gain[:, part]).astype(bf16)
        normed[:, part] = value
        if rel == 0 and keep_own is not None:
            keep_own(value)


def project_qkv(
    index_ref, own, core, across, diagonal, gain, q_hbm, k_hbm, v_hbm, out_hbm, cosine, sine,
    normed_own, out_w, *rest,
):
    *outs, normed, q_w, k_w, v_w, sems = rest
    copies = start_all([(q_hbm, q_w), (k_hbm, k_w), (v_hbm, v_w), (out_hbm, out_w)], sems)
    rows = own.shape[0] // len(outs)
    q_width, k_width = q_w.shape[1], k_w.shape[1]
    for c in range(len(outs)):
        here = slice(c * rows, (c + 1) * rows)

        def keep_own(value):
            normed_own[here, :] = value

        loads = [lambda ref=ref: ref[here, :].astype(f32) for ref in (own, core, across, diagonal)]
        normalize(index_ref, loads, gain, normed.at[here, :], keep_own)
    for w, copy, low, high in (
        (q_w, copies[0], 0, q_width),
        (k_w, copies[1], q_width, q_width + k_width),
        (v_w, copies[2], q_width + k_width, q_width + 2 * k_width),
    ):
        copy.wait()
        for c, out in enumerate(outs):
            out[:, low:high] = dot(normed[c * rows : (c + 1) * rows, :], w[...])
    copies[3].wait()


def rows_of(slot, height):
    return pl.ds(pl.multiple_of(slot * height, 16), height)


def low_first(rank, me_ref, want_ref, lens_ref, *refs):
    *packed, passed, normed_own, out, chosen, proj, stack = refs
    wanted = want_ref.shape[1]
    low = out.shape[0]

    def use(slot, block):
        stack[rows_of(slot, low), :] = block[0:low, :]
        chosen[slot] = block[low : low + 3 * rank, :]
        proj[rows_of(slot, rank), :] = block[low + 3 * rank :, :]

    each_asked(me_ref, want_ref, packed, passed, use)
    products = dot_nt(stack[...], normed_own[...])
    masks = lane_masks(lens_ref, wanted, 0, normed_own.shape[0])
    out[...] = merged(products, masks, low).astype(bf16)


def attend(
    chunk, heads, kv_heads,
    index_ref, lens_ref, qkv, low0, low1, low2, low3, chosen, cosine, sine,
    q_gain, k_gain, out_w, old_k, old_v, after,
    new_k, new_v, *terms,
):
    rows = qkv.shape[0]
    width = out_w.shape[0]
    first = chunk * rows
    here = slice(first, first + rows)
    wanted, rank = chosen.shape[0], chosen.shape[1] // 3
    q_width, k_width = heads * HEAD_WIDTH, kv_heads * HEAD_WIDTH

    def stack(number, columns=slice(None)):
        block = chosen[:, number * rank : (number + 1) * rank, columns]
        return block.reshape(wanted * rank, block.shape[2])

    masks = lane_masks(lens_ref, wanted, first, rows)
    total = sum(ref[:, here].astype(f32) for ref in (low0, low1, low2, low3))
    total = total.astype(bf16).astype(f32)
    query = qkv[:, 0:q_width] + delta(total[0:rank], masks, stack(0))
    key = qkv[:, q_width : q_width + k_width] + delta(total[rank : 2 * rank], masks, stack(1, slice(0, k_width)))
    value = qkv[:, q_width + k_width :] + delta(total[2 * rank :], masks, stack(1, slice(k_width, 2 * k_width)))
    new_v[...] = value.astype(bf16)
    cos, sin = cosine[here, :], sine[here, :]

    def turn(values, gain):
        square = jnp.mean(values * values, axis=1, keepdims=True)
        values = values * lax.rsqrt(square + epsilon) * gain[...]
        return (values * cos + pltpu.roll(values, HEAD_WIDTH // 2, 1) * sin).astype(bf16)

    def head(h):
        return slice(h * HEAD_WIDTH, (h + 1) * HEAD_WIDTH)

    for h in range(kv_heads):
        new_k[:, head(h)] = turn(key[:, head(h)], k_gain)
    seen = first + rows
    starts, _ = bounds(lens_ref, wanted)
    down = lax.broadcasted_iota(jnp.int32, (rows, 1), 0) + first
    start_of = jnp.zeros((rows, 1), jnp.int32)
    for s in starts:
        start_of = jnp.where(down >= s, s, start_of)
    along = lax.broadcasted_iota(jnp.int32, (rows, seen), 1)
    allowed = (along <= down) & (along >= start_of)
    group = heads // kv_heads
    mixed = []
    for kv in range(kv_heads):
        keys, values = new_k[:, head(kv)], new_v[:, head(kv)]
        if chunk > 0:
            keys = jnp.concatenate([old_k[:, head(kv)], keys], axis=0)
            values = jnp.concatenate([old_v[:, head(kv)], values], axis=0)
        for h in range(kv * group, (kv + 1) * group):
            scores = dot_nt(turn(query[:, head(h)], q_gain), keys) * (1.0 / math.sqrt(HEAD_WIDTH))
            raw = jnp.where(allowed, jnp.exp(scores), 0.0)
            probs = (raw * (1.0 / jnp.sum(raw, axis=1, keepdims=True))).astype(bf16)
            mixed.append(dot(probs, values).astype(bf16))
    attended = jnp.concatenate(mixed, axis=1)
    lows = merged(dot_nt(stack(2), attended), masks, rank)
    share(index_ref, attended, out_w, lows, *terms)


def share(index_ref, values, weight, lows, keep, *sends):
    rows, width = values.shape[0], sends[0].shape[1]
    half = len(sends) // 2
    left, right = slice(0, width), slice(width, 2 * width)
    for rel, at in ((1, 0), (3, half)):
        term = dot(values, weight[:, part_of(index_ref, rel, width)]).astype(bf16)
        row = 0
        for target in sends[at : at + half]:
            count = min(target.shape[0], rows - row)
            target[0:count, :] = term[row : row + count, :]
            row += count
    sends[half - 1][-lows.shape[0] :, 0:rows] = lows.astype(bf16)
    for rel, at in ((0, left), (2, right)):
        keep[0:rows, at] = dot(values, weight[:, part_of(index_ref, rel, width)])
    keep[rows:, 0:rows] = lows


def add_pair(kept, *refs):
    *arrived, _, out = refs
    half = len(arrived) // 2
    width = out.shape[1] // 2
    for at, pieces in ((slice(0, width), arrived[:half]), (slice(width, 2 * width), arrived[half:])):
        row = 0
        for piece in pieces:
            here = slice(row, row + piece.shape[0])
            out[here, at] = (kept[here, at] + piece[...].astype(f32)).astype(bf16)
            row += piece.shape[0]


def residual(chunk, lens_ref, chip, arrived, own, across, table, table_across, after, touched, out):
    rows = out.shape[0]
    width = own.shape[1]
    wanted = lens_ref.shape[1]
    rank = table.shape[0] // wanted
    here = slice(chunk * rows, (chunk + 1) * rows)
    left, right = slice(0, width), slice(width, 2 * width)
    masks = lane_masks(lens_ref, wanted, chunk * rows, rows)
    lows = chip[rows : rows + rank, 0:rows].astype(f32) + arrived[rows : rows + rank, 0:rows].astype(f32)
    lows = spread(lows.astype(bf16).astype(f32), masks)
    for mine, theirs, tokens, b in (
        (left, right, own, table),
        (right, left, across, table_across),
    ):
        total = chip[0:rows, mine].astype(f32) + arrived[0:rows, theirs].astype(f32)
        total = total + dot_tn(lows, b[...]).astype(bf16).astype(f32)
        out[:, mine] = (total + tokens[here, :].astype(f32)).astype(bf16)


def choose_second(me_ref, want_ref, *refs):
    outs = refs[-5:]
    *packed, passed = refs[:-5]
    unit = passed.shape[2]
    wanted = want_ref.shape[1]

    def use(slot, block):
        row = 0
        for out in outs:
            height = out.shape[0] // wanted
            for k in range(out.shape[1] // unit):
                out[rows_of(slot, height), k * unit : (k + 1) * unit] = block[row : row + height, :]
                row += height

    each_asked(me_ref, want_ref, packed, passed, use)


def feed_forward(
    chunk,
    index_ref, lens_ref, mine, theirs, table0, table1, table2, table3, stack_a, stack_g, stack_u, gain,
    gate_w, up_w, down_w,
    *rest,
):
    *terms, normed, hidden = rest
    rows = mine.shape[0]
    width = mine.shape[1] // 2
    wanted = lens_ref.shape[1]
    low, rank = table0.shape[0] // wanted, stack_a.shape[0] // wanted
    unit = math.gcd(width, hidden.shape[1])
    pieces = [pl.ds(k * unit, unit) for k in range(hidden.shape[1] // unit)]
    masks = lane_masks(lens_ref, wanted, chunk * rows, rows)
    loads = [
        lambda ref=ref, at=at: ref[:, at * width : (at + 1) * width].astype(f32)
        for ref, at in ((mine, 0), (theirs, 0), (mine, 1), (theirs, 1))
    ]
    normalize(index_ref, loads, gain, normed)
    products = sum(
        dot_nt(table[...], normed[:, part_of(index_ref, rel, width)])
        for rel, table in enumerate((table0, table1, table2, table3))
    )
    total = merged(products, masks, low).astype(bf16).astype(f32)
    low_gate, low_up = spread(total[0:rank], masks), spread(total[rank:], masks)
    for piece in pieces:
        gate = dot(normed[...], gate_w[:, piece])
        gate = gate + dot_tn(low_gate, stack_g[:, piece]).astype(bf16).astype(f32)
        upward = dot(normed[...], up_w[:, piece])
        upward = upward + dot_tn(low_up, stack_u[:, piece]).astype(bf16).astype(f32)
        hidden[:, piece] = (gate / (1.0 + jnp.exp(-gate)) * upward).astype(bf16)
    lows = merged(dot_nt(stack_a[...], hidden[...]), masks, rank)
    share(index_ref, hidden[...], down_w, lows, *terms)


def split_pair(rank, kept, *refs):
    *arrived, stay, away = refs
    half = len(arrived) // 2
    width = away.shape[1]
    row = 0
    for piece in arrived[:half]:
        here = slice(row, row + piece.shape[0])
        stay[here, :] = kept[here, 0:width] + piece[...].astype(f32)
        row += piece.shape[0]
    row = 0
    for piece in arrived[half:]:
        here = slice(row, row + piece.shape[0])
        away[here, :] = (kept[here, width:] + piece[...].astype(f32)).astype(bf16)
        row += piece.shape[0]
    away[row:, :] = stay[row:, :].astype(bf16)


def finish(count, lens_ref, table, *refs):
    out = refs[-1]
    wanted = lens_ref.shape[1]
    width = out.shape[1]
    for c in range(count):
        stay, arrived, resid = refs[3 * c : 3 * c + 3]
        rows = resid.shape[0]
        masks = lane_masks(lens_ref, wanted, c * rows, rows)
        lows = stay[rows:, 0:rows] + arrived[rows:, 0:rows].astype(f32)
        total = stay[0:rows, :] + arrived[0:rows, :].astype(f32)
        total = total + delta(lows.astype(bf16).astype(f32), masks, table[...])
        out[c * rows : (c + 1) * rows, :] = (total + resid[:, 0:width].astype(f32)).astype(bf16)


def rotation_tables(lens, row_count):
    half = HEAD_WIDTH // 2
    inverse = rope_base ** (-(jnp.arange(half, dtype=f32) * 2.0) / HEAD_WIDTH)
    row = jnp.arange(row_count, dtype=jnp.int32)
    start_of = jnp.zeros_like(row)
    start = jnp.int32(0)
    for j in range(lens.shape[0]):
        start_of = jnp.where(row >= start, start, start_of)
        start = start + lens[j]
    angle = (row - start_of).astype(f32)[:, None] * jnp.concatenate([inverse, inverse])[None, :]
    sign = jnp.concatenate([-jnp.ones(half, f32), jnp.ones(half, f32)])
    return jnp.cos(angle), jnp.sin(angle) * sign[None, :]


def swap_core(values):
    return lax.ppermute(values, "tp", [(k, k ^ 1) for k in range(4)])


def swap_across(values):
    return lax.ppermute(values, "tp", [(k, k ^ 2) for k in range(4)])


def swap_diagonal(values):
    return lax.ppermute(values, "tp", [(k, k ^ 3) for k in range(4)])


def swap_req(values, flips):
    return lax.ppermute(values, "req", [(k, k ^ flips) for k in range(lax.axis_size("req"))])


def per_device(
    tokens,
    lengths,
    request_adapter_index,
    attention_norm_gain,
    query_norm_gain,
    key_norm_gain,
    feedforward_norm_gain,
    query_weight,
    key_weight,
    value_weight,
    output_weight,
    gate_weight,
    up_weight,
    down_weight,
    query_key_value_adapter_input,
    output_adapter_input,
    gate_up_adapter_input,
    down_adapter_input,
    query_adapter_output,
    key_adapter_output,
    value_adapter_output,
    projection_adapter_output,
    gate_adapter_output,
    up_adapter_output,
    down_adapter_output,
):
    assert lax.axis_size("tp") == 4
    row_count, width = tokens.shape
    groups = lax.axis_size("req")
    wanted = lengths.shape[1]
    held, low_qkv, _ = query_key_value_adapter_input.shape
    rank = output_adapter_input.shape[1]
    low_gu = gate_up_adapter_input.shape[1]
    q_width, k_width = query_weight.shape[1], key_weight.shape[1]
    hidden_width = gate_weight.shape[1]
    heads, kv_heads = q_width // HEAD_WIDTH, k_width // HEAD_WIDTH
    unit = math.gcd(width, hidden_width)
    rows = row_count // CHUNKS
    assert width == q_width == 2 * k_width and rows <= width
    index = lax.axis_index("tp").astype(jnp.int32).reshape(1)
    me = lax.axis_index("req").astype(jnp.int32).reshape(1)
    want = request_adapter_index

    peers = groups // 2
    across = swap_across(tokens)
    core = swap_core(tokens)
    diagonal = swap_core(across)
    want_neighbour = swap_req(want, 1)

    def spread_out(block, *after):
        everyone = [block] + [swap_req(block, 2 * rel) for rel in range(1, peers)]
        passing = call(
            pick_for_neighbour, [SMEM] * 2 + [VMEM] * peers + [ANY] * len(after),
            shaped((peers,) + block.shape[1:], bf16),
        )(me, want_neighbour, *everyone, *after)
        return everyone, passing

    def loaded(weights, after, limit):
        return call(
            functools.partial(load, len(weights)), [ANY] * (len(weights) + len(after)),
            [shaped(w.shape, bf16) for w in weights],
            scratch=[pltpu.SemaphoreType.DMA((len(weights),))], limit=limit,
        )(*weights, *after)

    tables = (
        query_key_value_adapter_input, query_adapter_output, key_adapter_output, value_adapter_output,
        output_adapter_input, projection_adapter_output, gate_up_adapter_input, down_adapter_output,
        down_adapter_input, gate_adapter_output, up_adapter_output,
    )
    plan = (
        (0, (0, width), 0, 0),
        (1, (0, q_width), low_qkv, 0),
        (2, (0, k_width), low_qkv + rank, 0),
        (3, (0, k_width), low_qkv + rank, k_width),
        (4, (0, width), low_qkv + 2 * rank, 0),
        (5, (0, width), low_qkv + 3 * rank, 0),
    )
    plan_second, row = [], 0
    shapes = ((low_gu, width), (rank, width)) + ((rank, hidden_width),) * 3
    for table, (height, columns) in enumerate(shapes):
        for k in range(columns // unit):
            plan_second.append((6 + table, (k * unit, unit), row, 0))
            row += height
    block, block_second = call(
        functools.partial(gather_tables, (plan, tuple(plan_second))), [ANY] * len(tables),
        [shaped((held, low_qkv + 4 * rank, width), bf16), shaped((held, row, unit), bf16)],
        scratch=[pltpu.SemaphoreType.DMA((len(plan) + len(plan_second),))], limit=60,
    )(*tables)
    cosine, sine = rotation_tables(lengths[0], row_count)

    gain_one = attention_norm_gain.reshape(1, -1)
    gain_two = feedforward_norm_gain.reshape(1, -1)
    q_gain = query_norm_gain.reshape(1, -1)
    k_gain = key_norm_gain.reshape(1, -1)
    qkv_width = q_width + 2 * k_width
    normed_own, output_weight, *qkv = call(
        project_qkv, [SMEM] + [VMEM] * 5 + [ANY] * 6,
        [shaped((row_count, width), bf16), shaped(output_weight.shape, bf16)] + [shaped((rows, qkv_width), f32)] * CHUNKS,
        scratch=[
            pltpu.VMEM((row_count, 4 * width), bf16),
            pltpu.VMEM(query_weight.shape, bf16),
            pltpu.VMEM(key_weight.shape, bf16),
            pltpu.VMEM(value_weight.shape, bf16),
            pltpu.SemaphoreType.DMA((4,)),
        ],
        limit=50,
    )(
        index, tokens, core, across, diagonal, gain_one, query_weight, key_weight, value_weight,
        output_weight, cosine, sine,
    )
    everyone, passing = spread_out(block, normed_own)
    passed = swap_req(passing, 1)
    block_second = call(hold, [VMEM, ANY], shaped(block_second.shape, bf16))(block_second, passing)

    low, chosen, proj = call(
        functools.partial(low_first, rank), [SMEM] * 3 + [VMEM] * (peers + 2),
        [
            shaped((low_qkv, row_count), bf16),
            shaped((wanted, 3 * rank, width), bf16),
            shaped((wanted * rank, width), bf16),
        ],
        scratch=[pltpu.VMEM((wanted * low_qkv, width), bf16)],
    )(me, want, lengths, *everyone, passed, normed_own)
    lows = (low, swap_core(low), swap_across(low), swap_diagonal(low))
    proj_across = swap_across(proj)

    everyone, passing_second = spread_out(block_second, low)
    passed = swap_req(passing_second, 1)
    table, down_b, down_a, gate_b, up_b = call(
        choose_second, [SMEM] * 2 + [VMEM] * (peers + 1),
        [shaped((wanted * height, columns), bf16) for height, columns in shapes],
    )(me, want, *everyone, passed)
    table_across = swap_across(table)
    tables = (table, swap_core(table), table_across, swap_core(table_across))

    tall = rows + rank
    cuts = [rows // 2, rows // 2 + rank, rows // 2, rows // 2]
    terms = [shaped((tall, 2 * width), f32)] + [shaped((cut, width), bf16) for cut in cuts]
    past = [jnp.zeros((16, k_width), bf16)] * 2
    after = low
    chips = []
    for c in range(CHUNKS):
        new_k, new_v, keep, *sends = call(
            functools.partial(attend, c, heads, kv_heads),
            [SMEM] * 2 + [VMEM] * 13 + [ANY],
            [shaped((rows, k_width), bf16)] * 2 + terms,
        )(
            index, lengths, qkv[c], *lows, chosen, cosine, sine,
            q_gain, k_gain, output_weight, *past, after,
        )
        past = [new_k, new_v] if c == 0 else [
            jnp.concatenate([old, new], axis=0) for old, new in zip(past, (new_k, new_v))
        ]
        after = call(add_pair, [VMEM] * 5 + [ANY], shaped((tall, 2 * width), bf16))(
            keep, *[swap_core(piece) for piece in sends], passing_second
        )
        chips.append(after)

    gate_weight, up_weight, down_weight = loaded(
        (gate_weight, up_weight, down_weight), (after,), 44
    )
    ends = []
    for c in range(CHUNKS):
        resid = call(
            functools.partial(residual, c), [SMEM] + [VMEM] * 6 + [ANY] * 2,
            shaped((rows, 2 * width), bf16),
        )(lengths, chips[c], swap_across(chips[c]), tokens, across, proj, proj_across, after,
          gate_weight)
        keep, *sends = call(
            functools.partial(feed_forward, c),
            [SMEM] * 2 + [VMEM] * 13,
            terms,
            limit=32,
            scratch=[
                pltpu.VMEM((rows, 4 * width), bf16),
                pltpu.VMEM((rows, hidden_width), bf16),
            ],
        )(
            index, lengths, resid, swap_core(resid), *tables, down_a, gate_b, up_b,
            gain_two, gate_weight, up_weight, down_weight,
        )
        stay, away = call(
            functools.partial(split_pair, rank), [VMEM] * 5,
            [shaped((tall, width), f32), shaped((tall, width), bf16)],
        )(keep, *[swap_core(piece) for piece in sends])
        after = away
        ends += [stay, swap_across(away), resid]
    return call(
        functools.partial(finish, CHUNKS), [SMEM] + [VMEM] * (1 + 3 * CHUNKS),
        shaped((row_count, width), bf16),
    )(lengths, down_b, *ends)


def solution(mesh):
    placed = (
        P("req", "tp"),
        P("req", None),
        P("req", None),
        P(),
        P(),
        P(),
        P(),
        P(None, "tp"),
        P(None, "tp"),
        P(None, "tp"),
        P("tp", None),
        P(None, "tp"),
        P(None, "tp"),
        P("tp", None),
        P("req", None, "tp"),
        P("req", None, "tp"),
        P("req", None, "tp"),
        P("req", None, "tp"),
        P("req", None, "tp"),
        P("req", None, "tp"),
        P("req", None, "tp"),
        P("req", None, "tp"),
        P("req", None, "tp"),
        P("req", None, "tp"),
        P("req", None, "tp"),
    )
    return jax.shard_map(
        per_device, mesh=mesh, in_specs=placed, out_specs=P("req", "tp"), check_vma=False
    )
```

time: 146 us -> 129 us (0.88)
  local copies, waits for them, and re-layouts: 22.2 us -> 3.22 us
  Pallas kernels: 30.3 us -> 39 us
  waiting for transfers between devices: 59.5 us -> 51.2 us
  starting transfers between devices: 28.6 us -> 30.3 us
    unnamed x68 -> x26, local copies, waits for them, and re-layouts: 19.3 us -> 1.79 us
    all_to_all x3 -> x0, starting transfers between devices: 16.4 us -> none  [to_groups(): lax.all_to_all(values, 'req', split_axis=0, concat_axis=0, tiled=True)]
    ppermute x0 -> x9, starting transfers between devices: none -> 15.3 us  [swap_req(): lax.ppermute(values, 'req', [(k, k ^ flips) for k in range(lax.axis_size(...]
    ppermute x7 -> x8, waiting for transfers between devices: 48.2 us -> 36.1 us  [swap_across(): return lax.ppermute(values, 'tp', [(k, k ^ 2) for k in range(4)])]
    pallas_call x16 -> x19, Pallas kernels: 30.3 us -> 39 us  [the longest x2 11.1 us: per_device(): call(functools.partial(feed_forward, c), [SMEM] * 2 + [VMEM] * 13, terms,...]
    ppermute x0 -> x9, waiting for transfers between devices: none -> 8.42 us  [swap_req(): lax.ppermute(values, 'req', [(k, k ^ flips) for k in range(lax.axis_size(...]
    all_to_all x3 -> x0, waiting for transfers between devices: 6.39 us -> none  [to_groups(): lax.all_to_all(values, 'req', split_axis=0, concat_axis=0, tiled=True)]
    ppermute x11 -> x23, starting transfers between devices: 2.08 us -> 4.46 us  [swap_core(): return lax.ppermute(values, 'tp', [(k, k ^ 1) for k in range(4)])]
  transfers between devices with their start and end apart: 22 -> 41, of which waited for: 12 -> 19; matrix products, arithmetic and copies ran while one was open for 2% -> 3% of each run, Pallas kernels for 19% -> 23%
where the time goes in v2:
time: 129 us; the launch traced here: 128 us
  waiting for transfers between devices  51.2 us (40%)
  Pallas kernels  39 us (30%)
  starting transfers between devices  30.3 us (23%)
  local copies, waits for them, and re-layouts  3.22 us (2%)
  other arithmetic  2.43 us (2%)
  between operations  2.22 us (2%)
    ppermute x8, waiting for transfers between devices, swap_across(): return lax.ppermute(values, 'tp', [(k, k ^ 2) for k in range(4)])  36.1 us
    ppermute x9, starting transfers between devices, swap_req(): lax.ppermute(values, 'req', [(k, k ^ flips) for k in range(lax.axis_size(...  15.3 us
    pallas_call x2, Pallas kernels, per_device(): call(functools.partial(feed_forward, c), [SMEM] * 2 + [VMEM] * 13, terms,...  11.1 us
    ppermute x8, starting transfers between devices, swap_across(): return lax.ppermute(values, 'tp', [(k, k ^ 2) for k in range(4)])  10.5 us
    ppermute x9, waiting for transfers between devices, swap_req(): lax.ppermute(values, 'req', [(k, k ^ flips) for k in range(lax.axis_size(...  8.42 us
    pallas_call x2, Pallas kernels, per_device(): call(functools.partial(attend, c, heads, kv_heads), [SMEM] * 2 + [VMEM] *...  8.1 us
    pallas_call x1, Pallas kernels, per_device(): call(project_qkv, [SMEM] + [VMEM] * 5 + [ANY] * 6, [shaped((row_count, wi...  6.41 us
    ppermute x23, waiting for transfers between devices, swap_core(): return lax.ppermute(values, 'tp', [(k, k ^ 1) for k in range(4)])  5.3 us
  transfers between devices with their start and end apart: 41, of which 19 were waited for; matrix products, arithmetic and copies ran while one was open for 3% of the time, Pallas kernels for 23%

profile of v2, /device:TPU:0, one launch (start us, length us, event | category | flops | bytes accessed | tf_op | source)
XLA Modules:
  0.0 128.3 jit_solution(13610015177856746012)
XLA Ops:
  0.0 2.9 %collective-permute-start.5 = (bf16[512,512]{1,0:T(8,128)(2,1)}, bf16[512,512]{1,0:T(8,128)(2,1)S(1)}, u32[]{:S(2)}, u32[]{:S(2)}) collective-permute-start(bf16[512,512]{1,0:T(8,128)(2,1)} %own.5), channel_id=1, source_target_pairs={{0,2},{1,3},{2,0},{3,1},{4,6},{5,7},{6,4},{7,5},{8,10},{9,11},{10,... | collective-permute-start | bytes 1572872 | tf_op jit(solution)/shard_map/ppermute | solution.py:417
  2.9 1.9 %shard_map.235 = (bf16[2,112,512]{2,1,0:T(8,128)(2,1)}, bf16[2,240,256]{2,1,0:T(8,128)(2,1)}) custom-call(bf16[2,48,512]{2,1,0:T(8,128)(2,1)} %refs_0_.2, bf16[2,16,512]{2,1,0:T(8,128)(2,1)} %refs_1_.2, bf16[2,16,256]{2,1,0:T(8,128)(2,1)} %refs_2_.2, bf16[2,16,256]{2,1,0:T(8,128)(2,1)} %refs_3_.1, bf16[2,16,512]{2,1,0:T(8,128)(2,1)} %refs_4_.1, ...), custom_call_target="tpu_custom_call" | custom-call | flops 1 | bytes 1 | tf_op jit(solution)/shard_map/pallas_call | solution.py:512
  4.8 1.6 %collective-permute-start.1 = (bf16[2,112,512]{2,1,0:T(8,128)(2,1)}, bf16[2,112,512]{2,1,0:T(8,128)(2,1)S(1)}, u32[]{:S(2)}, u32[]{:S(2)}) collective-permute-start(bf16[2,112,512]{2,1,0:T(8,128)(2,1)} %get-tuple-element.49.refs_0_), channel_id=1, source_target_pairs={{0,8},{4,12},{8,0},{12,4},{16,24},{20,28},{24,16},{28,20},{1,9},{5... | collective-permute-start | bytes 688136 | tf_op jit(solution)/shard_map/ppermute | solution.py:425
  6.5 2.6 %collective-permute-start.2 = (bf16[2,112,512]{2,1,0:T(8,128)(2,1)}, bf16[2,112,512]{2,1,0:T(8,128)(2,1)S(1)}, u32[]{:S(2)}, u32[]{:S(2)}) collective-permute-start(bf16[2,112,512]{2,1,0:T(8,128)(2,1)} %get-tuple-element.49.refs_0_), channel_id=1, source_target_pairs={{0,16},{4,20},{8,24},{12,28},{16,0},{20,4},{24,8},{28,12},{1,17},{... | collective-permute-start | bytes 688136 | tf_op jit(solution)/shard_map/ppermute | solution.py:425
  9.3 1.4 %fusion.1 = (s32[1,1]{1,0:T(1,128)}, s32[1,1]{1,0:T(1,128)}, s32[1,1]{1,0:T(1,128)}) fusion(s32[1,4]{1,0:T(1,128)} %lens_ref.15), kind=kLoop, calls=%fused_computation.9 | loop fusion | bytes 24 | tf_op jit(solution)/shard_map/slice | solution.py:406
  12.6 2.5 %collective-permute-done.5.across = bf16[512,512]{1,0:T(8,128)(2,1)S(1)} collective-permute-done((bf16[512,512]{1,0:T(8,128)(2,1)}, bf16[512,512]{1,0:T(8,128)(2,1)S(1)}, u32[]{:S(2)}, u32[]{:S(2)}) %collective-permute-start.5) | collective-permute-done | bytes 524320 | tf_op jit(solution)/shard_map/ppermute | solution.py:417
  15.9 1.6 %fusion = (f32[512,128]{1,0:T(8,128)S(1)}, f32[512,128]{1,0:T(8,128)S(1)}) fusion(f32[128]{0:T(128)} %constant.23.clone.1, f32[128]{0:T(128)S(1)} %pad_maximum_fusion, f32[512]{0:T(512)S(1)} %subtract_convert_fusion), kind=kLoop, calls=%fused_computation.2 | loop fusion | flops 131072 | bytes 527360 | tf_op jit(solution)/shard_map/mul | solution.py:409
  17.5 1.8 %collective-permute-start = (s32[1,4]{1,0:T(1,128)}, s32[1,4]{1,0:T(1,128)S(1)}, u32[]{:S(2)}, u32[]{:S(2)}) collective-permute-start(s32[1,4]{1,0:T(1,128)} %want_ref.3), channel_id=1, source_target_pairs={{0,4},{4,0},{8,12},{12,8},{16,20},{20,16},{24,28},{28,24},{1,5},{5... | collective-permute-start | bytes 56 | tf_op jit(solution)/shard_map/ppermute | solution.py:425
  19.4 1.0 copy-done.1
  21.1 6.4 %shard_map.236 = (bf16[512,512]{1,0:T(8,128)(2,1)S(1)}, bf16[512,2048]{1,0:T(8,128)(2,1)}, f32[256,1024]{1,0:T(8,128)}, f32[256,1024]{1,0:T(8,128)}) custom-call(s32[1]{0:T(128)} %bitcast.1.index_ref, bf16[512,512]{1,0:T(8,128)(2,1)S(1)} %copy-done.1, bf16[512,512]{1,0:T(8,128)(2,1)S(1)} %collective-permute-done.4.core, ...), custom_call_target="tpu_custom_call" | custom-call | flops 1 | bytes 1 | tf_op jit(solution)/shard_map/pallas_call | solution.py:524
  28.6 3.4 %collective-permute-start.7 = (bf16[2,240,256]{2,1,0:T(8,128)(2,1)S(1)}, bf16[2,240,256]{2,1,0:T(8,128)(2,1)S(1)}, u32[]{:S(2)}, u32[]{:S(2)}) collective-permute-start(bf16[2,240,256]{2,1,0:T(8,128)(2,1)S(1)} %shard_map.238.refs_0_), channel_id=1, source_target_pairs={{0,8},{4,12},{8,0},{12,4},{16,24},{20,28},{24,16},{28,20},{1,9},{5... | collective-permute-start | bytes 737288 | tf_op jit(solution)/shard_map/ppermute | solution.py:425
  32.0 1.1 collective-permute-start.8
  33.1 7.9 %collective-permute-done.10.refs_4_ = bf16[4,112,512]{2,1,0:T(8,128)(2,1)S(1)} collective-permute-done((bf16[4,112,512]{2,1,0:T(8,128)(2,1)S(1)}, bf16[4,112,512]{2,1,0:T(8,128)(2,1)S(1)}, u32[]{:S(2)}, u32[]{:S(2)}) %collective-permute-start.10) | collective-permute-done | bytes 458784 | tf_op jit(solution)/shard_map/ppermute | solution.py:425
  41.0 1.3 %shard_map.239 = (bf16[48,512]{1,0:T(8,128)(2,1)S(1)}, bf16[4,48,512]{2,1,0:T(8,128)(2,1)S(1)}, bf16[64,512]{1,0:T(8,128)(2,1)S(1)}) custom-call(s32[1]{0:T(128)} %bitcast.me_ref, s32[1,4]{1,0:T(1,128)S(1)} %copy-done.12, s32[1,4]{1,0:T(1,128)S(1)} %copy-done.7, bf16[2,112,512]{2,1,0:T(8,128)(2,1)S(1)} %copy-done.5, ...), custom_call_target="tpu_custom_call" | custom-call | flops 1 | bytes 1 | tf_op jit(solution)/shard_map/pallas_call | solution.py:543
  42.4 3.7 %collective-permute-start.9 = (bf16[2,240,256]{2,1,0:T(8,128)(2,1)S(1)}, bf16[2,240,256]{2,1,0:T(8,128)(2,1)S(1)}, u32[]{:S(2)}, u32[]{:S(2)}) collective-permute-start(bf16[2,240,256]{2,1,0:T(8,128)(2,1)S(1)} %shard_map.238.refs_0_), channel_id=1, source_target_pairs={{0,24},{4,28},{8,16},{12,20},{16,8},{20,12},{24,0},{28,4},{1,25},{... | collective-permute-start | bytes 737288 | tf_op jit(solution)/shard_map/ppermute | solution.py:425
  46.1 1.5 %collective-permute-start.13 = (bf16[48,512]{1,0:T(8,128)(2,1)S(1)}, bf16[48,512]{1,0:T(8,128)(2,1)S(1)}, u32[]{:S(2)}, u32[]{:S(2)}) collective-permute-start(bf16[48,512]{1,0:T(8,128)(2,1)S(1)} %get-tuple-element.51.refs_4_.low0.after), channel_id=1, source_target_pairs={{0,2},{1,3},{2,0},{3,1},{4,6},{5,7},{6,4},{7,5},{8,10},{9,11},{10,... | collective-permute-start | bytes 147464 | tf_op jit(solution)/shard_map/ppermute | solution.py:417
  47.6 2.6 %collective-permute-done.13.low2 = bf16[48,512]{1,0:T(8,128)(2,1)S(1)} collective-permute-done((bf16[48,512]{1,0:T(8,128)(2,1)S(1)}, bf16[48,512]{1,0:T(8,128)(2,1)S(1)}, u32[]{:S(2)}, u32[]{:S(2)}) %collective-permute-start.13) | collective-permute-done | bytes 49184 | tf_op jit(solution)/shard_map/ppermute | solution.py:417
  50.2 1.4 %collective-permute-done.14.low3 = bf16[48,512]{1,0:T(8,128)(2,1)S(1)} collective-permute-done((bf16[48,512]{1,0:T(8,128)(2,1)S(1)}, bf16[48,512]{1,0:T(8,128)(2,1)S(1)}, u32[]{:S(2)}, u32[]{:S(2)}) %collective-permute-start.14) | collective-permute-done | bytes 49184 | tf_op jit(solution)/shard_map/ppermute | solution.py:421
  51.6 4.0 %shard_map.242 = (bf16[256,256]{1,0:T(8,128)(2,1)S(1)}, bf16[256,256]{1,0:T(8,128)(2,1)S(1)}, f32[272,1024]{1,0:T(8,128)S(1)}, bf16[128,512]{1,0:T(8,128)(2,1)S(...) custom-call(s32[1]{0:T(128)} %bitcast.1.index_ref, ...), custom_call_target="tpu_custom_call" | custom-call | flops 1 | bytes 1 | tf_op jit(solution)/shard_map/pallas_call | solution.py:571
  57.8 1.1 collective-permute-start.19
  58.9 4.1 %shard_map.244 = (bf16[256,256]{1,0:T(8,128)(2,1)}, bf16[256,256]{1,0:T(8,128)(2,1)}, f32[272,1024]{1,0:T(8,128)S(1)}, bf16[128,512]{1,0:T(8,128)(2,1)S(1)}, bf1...) custom-call(s32[1]{0:T(128)} %bitcast.1.index_ref, s32[1,4]{1,0:T(1,128)S(1)} %copy-done.7, ...), custom_call_target="tpu_custom_call" | custom-call | flops 1 | bytes 1 | tf_op jit(solution)/shard_map/pallas_call | solution.py:571
  66.0 3.8 %shard_map.246 = (bf16[2048,768]{1,0:T(8,128)(2,1)S(1)}, bf16[2048,768]{1,0:T(8,128)(2,1)S(1)}, bf16[768,2048]{1,0:T(8,128)(2,1)S(1)}) custom-call(bf16[2048,768]{1,0:T(8,128)(2,1)} %refs_0_.3, bf16[2048,768]{1,0:T(8,128)(2,1)} %refs_1_.3, bf16[768,2048]{1,0:T(8,128)(2,1)} %refs_2_.3, bf16[272,1024]{1,0:T(8,128)(2,1)S(1)} %shard_map.245.refs_3_.after.chip), custom_call_target="tpu_custom_call" | custom-call | flops 1 | bytes 1 | tf_op jit(solution)/shard_map/pallas_call | solution.py:487
  69.9 4.2 %collective-permute-done.20.table_across = bf16[64,512]{1,0:T(8,128)(2,1)S(1)} collective-permute-done((bf16[64,512]{1,0:T(8,128)(2,1)S(1)}, bf16[64,512]{1,0:T(8,128)(2,1)S(1)}, u32[]{:S(2)}, u32[]{:S(2)}) %collective-permute-start.20) | collective-permute-done | bytes 65568 | tf_op jit(solution)/shard_map/ppermute | solution.py:417
  76.7 1.1 shard_map.241
  78.8 14.2 %collective-permute-done.27.table2 = bf16[128,512]{1,0:T(8,128)(2,1)S(1)} collective-permute-done((bf16[128,512]{1,0:T(8,128)(2,1)S(1)}, bf16[128,512]{1,0:T(8,128)(2,1)S(1)}, u32[]{:S(2)}, u32[]{:S(2)}) %collective-permute-start.27) | collective-permute-done | bytes 131104 | tf_op jit(solution)/shard_map/ppermute | solution.py:417
  93.0 1.3 %collective-permute-done.28.table3 = bf16[128,512]{1,0:T(8,128)(2,1)S(1)} collective-permute-done((bf16[128,512]{1,0:T(8,128)(2,1)S(1)}, bf16[128,512]{1,0:T(8,128)(2,1)S(1)}, u32[]{:S(2)}, u32[]{:S(2)}) %collective-permute-start.28) | collective-permute-done | bytes 131104 | tf_op jit(solution)/shard_map/ppermute | solution.py:413
  94.4 5.5 %shard_map.248 = (f32[272,1024]{1,0:T(8,128)S(1)}, bf16[128,512]{1,0:T(8,128)(2,1)S(1)}, bf16[144,512]{1,0:T(8,128)(2,1)S(1)}, bf16[128,512]{1,0:T(8,128)(2,1)S(1)}, bf16[128,512]{1,0:T(8,128)(2,1)S(1)}) custom-call(s32[1]{0:T(128)} %bitcast.1.index_ref, s32[1,4]{1,0:T(1,128)S(1)} %copy-done.7, bf16[256,1024]{1,0:T(8,128)(2,1)S(1)} %shard_map.247.mine.refs_2_, ...), custom_call_target="tpu_custom_call" | custom-call | flops 1 | bytes 1 | tf_op jit(solution)/shard_map/pallas_call | solution.py:597
  103.5 1.6 %collective-permute-done.35.theirs = bf16[256,1024]{1,0:T(8,128)(2,1)S(1)} collective-permute-done((bf16[256,1024]{1,0:T(8,128)(2,1)S(1)}, bf16[256,1024]{1,0:T(8,128)(2,1)S(1)}, u32[]{:S(2)}, u32[]{:S(2)}) %collective-permute-start.35) | collective-permute-done | bytes 524320 | tf_op jit(solution)/shard_map/ppermute | solution.py:413
  105.1 5.5 %shard_map.251 = (f32[272,1024]{1,0:T(8,128)S(1)}, bf16[128,512]{1,0:T(8,128)(2,1)S(1)}, bf16[144,512]{1,0:T(8,128)(2,1)S(1)}, bf16[128,512]{1,0:T(8,128)(2,1)S(1)}, bf16[128,512]{1,0:T(8,128)(2,1)S(1)}) custom-call(s32[1]{0:T(128)} %bitcast.1.index_ref, s32[1,4]{1,0:T(1,128)S(1)} %copy-done.7, bf16[256,1024]{1,0:T(8,128)(2,1)S(1)} %shard_map.250.mine.refs_5_, ...), custom_call_target="tpu_custom_call" | custom-call | flops 1 | bytes 1 | tf_op jit(solution)/shard_map/pallas_call | solution.py:597
  114.0 7.2 %collective-permute-done.33.refs_1_ = bf16[272,512]{1,0:T(8,128)(2,1)S(1)} collective-permute-done((bf16[272,512]{1,0:T(8,128)(2,1)S(1)}, bf16[272,512]{1,0:T(8,128)(2,1)S(1)}, u32[]{:S(2)}, u32[]{:S(2)}) %collective-permute-start.33) | collective-permute-done | bytes 278560 | tf_op jit(solution)/shard_map/ppermute | solution.py:417
  121.2 5.4 %collective-permute-done.40.refs_4_ = bf16[272,512]{1,0:T(8,128)(2,1)S(1)} collective-permute-done((bf16[272,512]{1,0:T(8,128)(2,1)S(1)}, bf16[272,512]{1,0:T(8,128)(2,1)S(1)}, u32[]{:S(2)}, u32[]{:S(2)}) %collective-permute-start.40) | collective-permute-done | bytes 278560 | tf_op jit(solution)/shard_map/ppermute | solution.py:417
  126.6 1.7 %shard_map.253 = bf16[512,512]{1,0:T(8,128)(2,1)} custom-call(s32[1,4]{1,0:T(1,128)S(1)} %copy-done.7, bf16[64,512]{1,0:T(8,128)(2,1)S(1)} %get-tuple-element.52.table, f32[272,512]{1,0:T(8,128)S(1)} %get-tuple-element.82.refs_0_, bf16[272,512]{1,0:T(8,128)(2,1)S(1)} %collective-permute-done.33.refs_1_, bf16[256,1024]{1,0:T(8,128)(2,1)S(1)} %shard_map.247.mine.refs_2_, ...), custom_call_target="tpu_custom_call" | custom-call | flops 1 | bytes 1 | tf_op jit(solution)/shard_map/pallas_call | solution.py:616
  (101 shorter events, 18.5 us)
Async XLA Ops:
  0.0 15.1 %collective-permute-start.5 = (bf16[512,512]{1,0:T(8,128)(2,1)}, bf16[512,512]{1,0:T(8,128)(2,1)S(1)}, u32[]{:S(2)}, u32[]{:S(2)}) collective-permute-start(bf16[512,512]{1,0:T(8,128)(2,1)} %own.5), channel_id=1, source_target_pairs={{0,2},{1,3},{2,0},{3,1},{4,6},{5,7},{6,4},{7,5},{8,10},{9,11},{10,... | collective-permute-start | bytes 1572872 | tf_op jit(solution)/shard_map/ppermute | solution.py:417
  4.8 22.7 %collective-permute-start.1 = (bf16[2,112,512]{2,1,0:T(8,128)(2,1)}, bf16[2,112,512]{2,1,0:T(8,128)(2,1)S(1)}, u32[]{:S(2)}, u32[]{:S(2)}) collective-permute-start(bf16[2,112,512]{2,1,0:T(8,128)(2,1)} %get-tuple-element.49.refs_0_), channel_id=1, source_target_pairs={{0,8},{4,12},{8,0},{12,4},{16,24},{20,28},{24,16},{28,20},{1,9},{5... | collective-permute-start | bytes 688136 | tf_op jit(solution)/shard_map/ppermute | solution.py:425
  6.5 21.1 %collective-permute-start.2 = (bf16[2,112,512]{2,1,0:T(8,128)(2,1)}, bf16[2,112,512]{2,1,0:T(8,128)(2,1)S(1)}, u32[]{:S(2)}, u32[]{:S(2)}) collective-permute-start(bf16[2,112,512]{2,1,0:T(8,128)(2,1)} %get-tuple-element.49.refs_0_), channel_id=1, source_target_pairs={{0,16},{4,20},{8,24},{12,28},{16,0},{20,4},{24,8},{28,12},{1,17},{... | collective-permute-start | bytes 688136 | tf_op jit(solution)/shard_map/ppermute | solution.py:425
  9.1 18.5 %collective-permute-start.3 = (bf16[2,112,512]{2,1,0:T(8,128)(2,1)}, bf16[2,112,512]{2,1,0:T(8,128)(2,1)S(1)}, u32[]{:S(2)}, u32[]{:S(2)}) collective-permute-start(bf16[2,112,512]{2,1,0:T(8,128)(2,1)} %get-tuple-element.49.refs_0_), channel_id=1, source_target_pairs={{0,24},{4,28},{8,16},{12,20},{16,8},{20,12},{24,0},{28,4},{1,25},{... | collective-permute-start | bytes 688136 | tf_op jit(solution)/shard_map/ppermute | solution.py:425
  9.3 8.2 %collective-permute-start.4 = (bf16[512,512]{1,0:T(8,128)(2,1)}, bf16[512,512]{1,0:T(8,128)(2,1)S(1)}, u32[]{:S(2)}, u32[]{:S(2)}) collective-permute-start(bf16[512,512]{1,0:T(8,128)(2,1)} %own.5), channel_id=1, source_target_pairs={{0,1},{1,0},{2,3},{3,2},{4,5},{5,4},{6,7},{7,6},{8,9},{9,8},{10,11... | collective-permute-start | bytes 1572872 | tf_op jit(solution)/shard_map/ppermute | solution.py:413
  15.1 4.3 %collective-permute-start.6 = (bf16[512,512]{1,0:T(8,128)(2,1)S(1)}, bf16[512,512]{1,0:T(8,128)(2,1)S(1)}, u32[]{:S(2)}, u32[]{:S(2)}) collective-permute-start(bf16[512,512]{1,0:T(8,128)(2,1)S(1)} %collective-permute-done.5.across), channel_id=1, source_target_pairs={{0,1},{1,0},{2,3},{3,2},{4,5},{5,4},{6,7},{7,6},{8,9},{9,8},{10,11... | collective-permute-start | bytes 1572872 | tf_op jit(solution)/shard_map/ppermute | solution.py:413
  17.5 10.0 %collective-permute-start = (s32[1,4]{1,0:T(1,128)}, s32[1,4]{1,0:T(1,128)S(1)}, u32[]{:S(2)}, u32[]{:S(2)}) collective-permute-start(s32[1,4]{1,0:T(1,128)} %want_ref.3), channel_id=1, source_target_pairs={{0,4},{4,0},{8,12},{12,8},{16,20},{20,16},{24,28},{28,24},{1,5},{5... | collective-permute-start | bytes 56 | tf_op jit(solution)/shard_map/ppermute | solution.py:425
  28.3 12.7 %collective-permute-start.10 = (bf16[4,112,512]{2,1,0:T(8,128)(2,1)S(1)}, bf16[4,112,512]{2,1,0:T(8,128)(2,1)S(1)}, u32[]{:S(2)}, u32[]{:S(2)}) collective-permute-start(bf16[4,112,512]{2,1,0:T(8,128)(2,1)S(1)} %shard_map.237.after), channel_id=1, source_target_pairs={{0,4},{4,0},{8,12},{12,8},{16,20},{20,16},{24,28},{28,24},{1,5},{5... | collective-permute-start | bytes 1376264 | tf_op jit(solution)/shard_map/ppermute | solution.py:425
  28.6 27.5 %collective-permute-start.7 = (bf16[2,240,256]{2,1,0:T(8,128)(2,1)S(1)}, bf16[2,240,256]{2,1,0:T(8,128)(2,1)S(1)}, u32[]{:S(2)}, u32[]{:S(2)}) collective-permute-start(bf16[2,240,256]{2,1,0:T(8,128)(2,1)S(1)} %shard_map.238.refs_0_), channel_id=1, source_target_pairs={{0,8},{4,12},{8,0},{12,4},{16,24},{20,28},{24,16},{28,20},{1,9},{5... | collective-permute-start | bytes 737288 | tf_op jit(solution)/shard_map/ppermute | solution.py:425
  32.0 24.3 %collective-permute-start.8 = (bf16[2,240,256]{2,1,0:T(8,128)(2,1)S(1)}, bf16[2,240,256]{2,1,0:T(8,128)(2,1)S(1)}, u32[]{:S(2)}, u32[]{:S(2)}) collective-permute-start(bf16[2,240,256]{2,1,0:T(8,128)(2,1)S(1)} %shard_map.238.refs_0_), channel_id=1, source_target_pairs={{0,16},{4,20},{8,24},{12,28},{16,0},{20,4},{24,8},{28,12},{1,17},{... | collective-permute-start | bytes 737288 | tf_op jit(solution)/shard_map/ppermute | solution.py:425
  42.3 5.2 %collective-permute-start.12 = (bf16[48,512]{1,0:T(8,128)(2,1)S(1)}, bf16[48,512]{1,0:T(8,128)(2,1)S(1)}, u32[]{:S(2)}, u32[]{:S(2)}) collective-permute-start(bf16[48,512]{1,0:T(8,128)(2,1)S(1)} %get-tuple-element.51.refs_4_.low0.after), channel_id=1, source_target_pairs={{0,1},{1,0},{2,3},{3,2},{4,5},{5,4},{6,7},{7,6},{8,9},{9,8},{10,11... | collective-permute-start | bytes 147464 | tf_op jit(solution)/shard_map/ppermute | solution.py:413
  42.4 14.2 %collective-permute-start.9 = (bf16[2,240,256]{2,1,0:T(8,128)(2,1)S(1)}, bf16[2,240,256]{2,1,0:T(8,128)(2,1)S(1)}, u32[]{:S(2)}, u32[]{:S(2)}) collective-permute-start(bf16[2,240,256]{2,1,0:T(8,128)(2,1)S(1)} %shard_map.238.refs_0_), channel_id=1, source_target_pairs={{0,24},{4,28},{8,16},{12,20},{16,8},{20,12},{24,0},{28,4},{1,25},{... | collective-permute-start | bytes 737288 | tf_op jit(solution)/shard_map/ppermute | solution.py:425
  46.1 4.1 %collective-permute-start.13 = (bf16[48,512]{1,0:T(8,128)(2,1)S(1)}, bf16[48,512]{1,0:T(8,128)(2,1)S(1)}, u32[]{:S(2)}, u32[]{:S(2)}) collective-permute-start(bf16[48,512]{1,0:T(8,128)(2,1)S(1)} %get-tuple-element.51.refs_4_.low0.after), channel_id=1, source_target_pairs={{0,2},{1,3},{2,0},{3,1},{4,6},{5,7},{6,4},{7,5},{8,10},{9,11},{10,... | collective-permute-start | bytes 147464 | tf_op jit(solution)/shard_map/ppermute | solution.py:417
  47.6 4.0 %collective-permute-start.14 = (bf16[48,512]{1,0:T(8,128)(2,1)S(1)}, bf16[48,512]{1,0:T(8,128)(2,1)S(1)}, u32[]{:S(2)}, u32[]{:S(2)}) collective-permute-start(bf16[48,512]{1,0:T(8,128)(2,1)S(1)} %get-tuple-element.51.refs_4_.low0.after), channel_id=1, source_target_pairs={{0,3},{1,2},{2,1},{3,0},{4,7},{5,6},{6,5},{7,4},{8,11},{9,10},{10,... | collective-permute-start | bytes 147464 | tf_op jit(solution)/shard_map/ppermute | solution.py:421
  55.5 2.1 %collective-permute-start.16 = (bf16[144,512]{1,0:T(8,128)(2,1)S(1)}, bf16[144,512]{1,0:T(8,128)(2,1)S(1)}, u32[]{:S(2)}, u32[]{:S(2)}) collective-permute-start(bf16[144,512]{1,0:T(8,128)(2,1)S(1)} %get-tuple-element.58), channel_id=1, source_target_pairs={{0,1},{1,0},{2,3},{3,2},{4,5},{5,4},{6,7},{7,6},{8,9},{9,8},{10,11... | collective-permute-start | bytes 442376 | tf_op jit(solution)/shard_map/ppermute | solution.py:413
  55.8 1.5 %collective-permute-start.15 = (bf16[128,512]{1,0:T(8,128)(2,1)S(1)}, bf16[128,512]{1,0:T(8,128)(2,1)S(1)}, u32[]{:S(2)}, u32[]{:S(2)}) collective-permute-start(bf16[128,512]{1,0:T(8,128)(2,1)S(1)} %get-tuple-element.57), channel_id=1, source_target_pairs={{0,1},{1,0},{2,3},{3,2},{4,5},{5,4},{6,7},{7,6},{8,9},{9,8},{10,11... | collective-permute-start | bytes 393224 | tf_op jit(solution)/shard_map/ppermute | solution.py:413
  57.8 16.3 %collective-permute-start.19 = (bf16[272,1024]{1,0:T(8,128)(2,1)S(1)}, bf16[272,1024]{1,0:T(8,128)(2,1)S(1)}, u32[]{:S(2)}, u32[]{:S(2)}) collective-permute-start(bf16[272,1024]{1,0:T(8,128)(2,1)S(1)} %shard_map.243.after.chip), channel_id=1, source_target_pairs={{0,2},{1,3},{2,0},{3,1},{4,6},{5,7},{6,4},{7,5},{8,10},{9,11},{10,... | collective-permute-start | bytes 1671176 | tf_op jit(solution)/shard_map/ppermute | solution.py:417
  63.1 13.6 %collective-permute-start.11 = (bf16[4,240,256]{2,1,0:T(8,128)(2,1)S(1)}, bf16[4,240,256]{2,1,0:T(8,128)(2,1)S(1)}, u32[]{:S(2)}, u32[]{:S(2)}) collective-permute-start(bf16[4,240,256]{2,1,0:T(8,128)(2,1)S(1)} %shard_map.240.refs_4_), channel_id=1, source_target_pairs={{0,4},{4,0},{8,12},{12,8},{16,20},{20,16},{24,28},{28,24},{1,5},{5... | collective-permute-start | bytes 1474568 | tf_op jit(solution)/shard_map/ppermute | solution.py:425
  63.8 2.1 %collective-permute-start.22 = (bf16[144,512]{1,0:T(8,128)(2,1)S(1)}, bf16[144,512]{1,0:T(8,128)(2,1)S(1)}, u32[]{:S(2)}, u32[]{:S(2)}) collective-permute-start(bf16[144,512]{1,0:T(8,128)(2,1)S(1)} %get-tuple-element.67), channel_id=1, source_target_pairs={{0,1},{1,0},{2,3},{3,2},{4,5},{5,4},{6,7},{7,6},{8,9},{9,8},{10,11... | collective-permute-start | bytes 442376 | tf_op jit(solution)/shard_map/ppermute | solution.py:413
  64.4 1.5 %collective-permute-start.24 = (bf16[128,512]{1,0:T(8,128)(2,1)S(1)}, bf16[128,512]{1,0:T(8,128)(2,1)S(1)}, u32[]{:S(2)}, u32[]{:S(2)}) collective-permute-start(bf16[128,512]{1,0:T(8,128)(2,1)S(1)} %get-tuple-element.69), channel_id=1, source_target_pairs={{0,1},{1,0},{2,3},{3,2},{4,5},{5,4},{6,7},{7,6},{8,9},{9,8},{10,11... | collective-permute-start | bytes 393224 | tf_op jit(solution)/shard_map/ppermute | solution.py:413
  64.9 9.2 %collective-permute-start.20 = (bf16[64,512]{1,0:T(8,128)(2,1)S(1)}, bf16[64,512]{1,0:T(8,128)(2,1)S(1)}, u32[]{:S(2)}, u32[]{:S(2)}) collective-permute-start(bf16[64,512]{1,0:T(8,128)(2,1)S(1)} %get-tuple-element.61.table), channel_id=1, source_target_pairs={{0,2},{1,3},{2,0},{3,1},{4,6},{5,7},{6,4},{7,5},{8,10},{9,11},{10,... | collective-permute-start | bytes 196616 | tf_op jit(solution)/shard_map/ppermute | solution.py:417
  75.1 19.3 %collective-permute-start.25 = (bf16[256,1024]{1,0:T(8,128)(2,1)S(1)}, bf16[256,1024]{1,0:T(8,128)(2,1)S(1)}, u32[]{:S(2)}, u32[]{:S(2)}) collective-permute-start(bf16[256,1024]{1,0:T(8,128)(2,1)S(1)} %shard_map.247.mine.refs_2_), channel_id=1, source_target_pairs={{0,1},{1,0},{2,3},{3,2},{4,5},{5,4},{6,7},{7,6},{8,9},{9,8},{10,11... | collective-permute-start | bytes 1572872 | tf_op jit(solution)/shard_map/ppermute | solution.py:413
  75.2 27.0 %collective-permute-start.34 = (bf16[272,1024]{1,0:T(8,128)(2,1)S(1)}, bf16[272,1024]{1,0:T(8,128)(2,1)S(1)}, u32[]{:S(2)}, u32[]{:S(2)}) collective-permute-start(bf16[272,1024]{1,0:T(8,128)(2,1)S(1)} %shard_map.245.refs_3_.after.chip), channel_id=1, source_target_pairs={{0,2},{1,3},{2,0},{3,1},{4,6},{5,7},{6,4},{7,5},{8,10},{9,11},{10,... | collective-permute-start | bytes 1671176 | tf_op jit(solution)/shard_map/ppermute | solution.py:417
  77.8 15.3 %collective-permute-start.27 = (bf16[128,512]{1,0:T(8,128)(2,1)S(1)}, bf16[128,512]{1,0:T(8,128)(2,1)S(1)}, u32[]{:S(2)}, u32[]{:S(2)}) collective-permute-start(bf16[128,512]{1,0:T(8,128)(2,1)S(1)} %get-tuple-element.71.table0), channel_id=1, source_target_pairs={{0,2},{1,3},{2,0},{3,1},{4,6},{5,7},{6,4},{7,5},{8,10},{9,11},{10,... | collective-permute-start | bytes 393224 | tf_op jit(solution)/shard_map/ppermute | solution.py:417
  78.8 14.2 %collective-permute-start.26 = (bf16[128,512]{1,0:T(8,128)(2,1)S(1)}, bf16[128,512]{1,0:T(8,128)(2,1)S(1)}, u32[]{:S(2)}, u32[]{:S(2)}) collective-permute-start(bf16[128,512]{1,0:T(8,128)(2,1)S(1)} %get-tuple-element.71.table0), channel_id=1, source_target_pairs={{0,1},{1,0},{2,3},{3,2},{4,5},{5,4},{6,7},{7,6},{8,9},{9,8},{10,11... | collective-permute-start | bytes 393224 | tf_op jit(solution)/shard_map/ppermute | solution.py:413
  99.9 2.1 %collective-permute-start.30 = (bf16[144,512]{1,0:T(8,128)(2,1)S(1)}, bf16[144,512]{1,0:T(8,128)(2,1)S(1)}, u32[]{:S(2)}, u32[]{:S(2)}) collective-permute-start(bf16[144,512]{1,0:T(8,128)(2,1)S(1)} %get-tuple-element.79), channel_id=1, source_target_pairs={{0,1},{1,0},{2,3},{3,2},{4,5},{5,4},{6,7},{7,6},{8,9},{9,8},{10,11... | collective-permute-start | bytes 442376 | tf_op jit(solution)/shard_map/ppermute | solution.py:413
  103.1 2.0 %collective-permute-start.35 = (bf16[256,1024]{1,0:T(8,128)(2,1)S(1)}, bf16[256,1024]{1,0:T(8,128)(2,1)S(1)}, u32[]{:S(2)}, u32[]{:S(2)}) collective-permute-start(bf16[256,1024]{1,0:T(8,128)(2,1)S(1)} %shard_map.250.mine.refs_5_), channel_id=1, source_target_pairs={{0,1},{1,0},{2,3},{3,2},{4,5},{5,4},{6,7},{7,6},{8,9},{9,8},{10,11... | collective-permute-start | bytes 1572872 | tf_op jit(solution)/shard_map/ppermute | solution.py:413
  110.6 2.2 %collective-permute-start.37 = (bf16[144,512]{1,0:T(8,128)(2,1)S(1)}, bf16[144,512]{1,0:T(8,128)(2,1)S(1)}, u32[]{:S(2)}, u32[]{:S(2)}) collective-permute-start(bf16[144,512]{1,0:T(8,128)(2,1)S(1)} %get-tuple-element.86), channel_id=1, source_target_pairs={{0,1},{1,0},{2,3},{3,2},{4,5},{5,4},{6,7},{7,6},{8,9},{9,8},{10,11... | collective-permute-start | bytes 442376 | tf_op jit(solution)/shard_map/ppermute | solution.py:413
  111.0 1.6 %collective-permute-start.36 = (bf16[128,512]{1,0:T(8,128)(2,1)S(1)}, bf16[128,512]{1,0:T(8,128)(2,1)S(1)}, u32[]{:S(2)}, u32[]{:S(2)}) collective-permute-start(bf16[128,512]{1,0:T(8,128)(2,1)S(1)} %get-tuple-element.85), channel_id=1, source_target_pairs={{0,1},{1,0},{2,3},{3,2},{4,5},{5,4},{6,7},{7,6},{8,9},{9,8},{10,11... | collective-permute-start | bytes 393224 | tf_op jit(solution)/shard_map/ppermute | solution.py:413
  111.2 1.4 %collective-permute-start.38 = (bf16[128,512]{1,0:T(8,128)(2,1)S(1)}, bf16[128,512]{1,0:T(8,128)(2,1)S(1)}, u32[]{:S(2)}, u32[]{:S(2)}) collective-permute-start(bf16[128,512]{1,0:T(8,128)(2,1)S(1)} %get-tuple-element.87), channel_id=1, source_target_pairs={{0,1},{1,0},{2,3},{3,2},{4,5},{5,4},{6,7},{7,6},{8,9},{9,8},{10,11... | collective-permute-start | bytes 393224 | tf_op jit(solution)/shard_map/ppermute | solution.py:413
  111.7 9.5 %collective-permute-start.33 = (bf16[272,512]{1,0:T(8,128)(2,1)S(1)}, bf16[272,512]{1,0:T(8,128)(2,1)S(1)}, u32[]{:S(2)}, u32[]{:S(2)}) collective-permute-start(bf16[272,512]{1,0:T(8,128)(2,1)S(1)} %get-tuple-element.83.after), channel_id=1, source_target_pairs={{0,2},{1,3},{2,0},{3,1},{4,6},{5,7},{6,4},{7,5},{8,10},{9,11},{10,... | collective-permute-start | bytes 835592 | tf_op jit(solution)/shard_map/ppermute | solution.py:417
  113.0 13.6 %collective-permute-start.40 = (bf16[272,512]{1,0:T(8,128)(2,1)S(1)}, bf16[272,512]{1,0:T(8,128)(2,1)S(1)}, u32[]{:S(2)}, u32[]{:S(2)}) collective-permute-start(bf16[272,512]{1,0:T(8,128)(2,1)S(1)} %get-tuple-element.90), channel_id=1, source_target_pairs={{0,2},{1,3},{2,0},{3,1},{4,6},{5,7},{6,4},{7,5},{8,10},{9,11},{10,... | collective-permute-start | bytes 835592 | tf_op jit(solution)/shard_map/ppermute | solution.py:417
  (22 other events, 181.6 us)

commit v3 on v2

--- a/solution.py
+++ b/solution.py
@@ -112,10 +112,11 @@
 
 
 def pick_for_neighbour(me_ref, want_ref, *refs):
-    *packed, after, send = refs
-    held = packed[0].shape[0]
-    for rel, ref in enumerate(packed):
+    *packed, _, _, send = refs
+    held = packed[0].shape[-3]
+    for rel in range(send.shape[0]):
         owner = owner_at(me_ref, rel, 0)
+        ref = packed[rel]
         pick = jnp.int32(0)
         for j in range(want_ref.shape[1]):
             a = want_ref[0, j]
@@ -128,8 +129,8 @@
 
 
 def each_asked(me_ref, want_ref, packed, passed, use):
-    held = packed[0].shape[0]
-    for rel, ref in enumerate(packed):
+    held = packed[0].shape[-3]
+    for rel in range(passed.shape[0]):
         for flip in range(2):
             owner = owner_at(me_ref, rel, flip)
             slot, pick, found = jnp.int32(0), jnp.int32(0), jnp.int32(0)
@@ -140,7 +141,7 @@
 
             @pl.when(found > 0)
             def _():
-                use(slot, passed.at[rel] if flip else ref.at[pick])
+                use(slot, passed.at[rel] if flip else packed[rel].at[pick])
 
 
 def normalize(index_ref, refs, gain, normed, keep_own=None):
@@ -157,11 +158,11 @@
 
 
 def project_qkv(
-    index_ref, own, core, across, diagonal, gain, q_hbm, k_hbm, v_hbm, out_hbm, cosine, sine,
-    normed_own, out_w, *rest,
+    index_ref, own, core, across, diagonal, gain, q_hbm, k_hbm, v_hbm,
+    normed_own, *rest,
 ):
     *outs, normed, q_w, k_w, v_w, sems = rest
-    copies = start_all([(q_hbm, q_w), (k_hbm, k_w), (v_hbm, v_w), (out_hbm, out_w)], sems)
+    copies = start_all([(q_hbm, q_w), (k_hbm, k_w), (v_hbm, v_w)], sems)
     rows = own.shape[0] // len(outs)
     q_width, k_width = q_w.shape[1], k_w.shape[1]
     for c in range(len(outs)):
@@ -180,7 +181,6 @@
         copy.wait()
         for c, out in enumerate(outs):
             out[:, low:high] = dot(normed[c * rows : (c + 1) * rows, :], w[...])
-    copies[3].wait()
 
 
 def rows_of(slot, height):
@@ -188,19 +188,22 @@
 
 
 def low_first(rank, me_ref, want_ref, lens_ref, *refs):
-    *packed, passed, normed_own, out, chosen, proj, stack = refs
+    *packed, passed, normed_own, _, _, _, out, chosen, both, stack = refs
     wanted = want_ref.shape[1]
     low = out.shape[0]
 
     def use(slot, block):
         stack[rows_of(slot, low), :] = block[0:low, :]
         chosen[slot] = block[low : low + 3 * rank, :]
-        proj[rows_of(slot, rank), :] = block[low + 3 * rank :, :]
+        at = pl.ds(pl.multiple_of(low + slot * rank, 16), rank)
+        both[at, :] = block[low + 3 * rank :, :]
 
     each_asked(me_ref, want_ref, packed, passed, use)
     products = dot_nt(stack[...], normed_own[...])
     masks = lane_masks(lens_ref, wanted, 0, normed_own.shape[0])
-    out[...] = merged(products, masks, low).astype(bf16)
+    value = merged(products, masks, low).astype(bf16)
+    out[...] = value
+    both[0:low, :] = value
 
 
 def attend(
@@ -221,7 +224,8 @@
         return block.reshape(wanted * rank, block.shape[2])
 
     masks = lane_masks(lens_ref, wanted, first, rows)
-    total = sum(ref[:, here].astype(f32) for ref in (low0, low1, low2, low3))
+    low = low0.shape[0]
+    total = sum(ref[0:low, here].astype(f32) for ref in (low0, low1, low2, low3))
     total = total.astype(bf16).astype(f32)
     query = qkv[:, 0:q_width] + delta(total[0:rank], masks, stack(0))
     key = qkv[:, q_width : q_width + k_width] + delta(total[rank : 2 * rank], masks, stack(1, slice(0, k_width)))
@@ -282,7 +286,7 @@
 
 
 def add_pair(kept, *refs):
-    *arrived, _, out = refs
+    *arrived, _, _, out = refs
     half = len(arrived) // 2
     width = out.shape[1] // 2
     for at, pieces in ((slice(0, width), arrived[:half]), (slice(width, 2 * width), arrived[half:])):
@@ -293,28 +297,29 @@
             row += piece.shape[0]
 
 
-def residual(chunk, lens_ref, chip, arrived, own, across, table, table_across, after, touched, out):
-    rows = out.shape[0]
-    width = own.shape[1]
+def residual(chunk, lens_ref, chip, arrived, own, across, table, table_across, after, touched, *outs):
+    half, width = outs[0].shape
+    rows = 2 * half
     wanted = lens_ref.shape[1]
-    rank = table.shape[0] // wanted
-    here = slice(chunk * rows, (chunk + 1) * rows)
+    rank = chip.shape[0] - rows
+    low = table.shape[0] - wanted * rank
     left, right = slice(0, width), slice(width, 2 * width)
     masks = lane_masks(lens_ref, wanted, chunk * rows, rows)
     lows = chip[rows : rows + rank, 0:rows].astype(f32) + arrived[rows : rows + rank, 0:rows].astype(f32)
     lows = spread(lows.astype(bf16).astype(f32), masks)
-    for mine, theirs, tokens, b in (
-        (left, right, own, table),
-        (right, left, across, table_across),
+    for number, (mine, theirs, tokens, b) in enumerate(
+        ((left, right, own, table), (right, left, across, table_across))
     ):
         total = chip[0:rows, mine].astype(f32) + arrived[0:rows, theirs].astype(f32)
-        total = total + dot_tn(lows, b[...]).astype(bf16).astype(f32)
-        out[:, mine] = (total + tokens[here, :].astype(f32)).astype(bf16)
+        total = total + dot_tn(lows, b[low:, :]).astype(bf16).astype(f32)
+        total = (total + tokens[chunk * rows : (chunk + 1) * rows, :].astype(f32)).astype(bf16)
+        outs[2 * number][...] = total[:half]
+        outs[2 * number + 1][...] = total[half:]
 
 
 def choose_second(me_ref, want_ref, *refs):
+    *packed, passed, _ = refs[:-5]
     outs = refs[-5:]
-    *packed, passed = refs[:-5]
     unit = passed.shape[2]
     wanted = want_ref.shape[1]
 
@@ -331,23 +336,21 @@
 
 def feed_forward(
     chunk,
-    index_ref, lens_ref, mine, theirs, table0, table1, table2, table3, stack_a, stack_g, stack_u, gain,
-    gate_w, up_w, down_w,
+    index_ref, lens_ref, left0, left1, right0, right1, left2, left3, right2, right3,
+    table0, table1, table2, table3, stack_a, stack_g, stack_u, gain, gate_w, up_w, down_w,
     *rest,
 ):
     *terms, normed, hidden = rest
-    rows = mine.shape[0]
-    width = mine.shape[1] // 2
+    half, width = left0.shape
+    rows = 2 * half
     wanted = lens_ref.shape[1]
     low, rank = table0.shape[0] // wanted, stack_a.shape[0] // wanted
     unit = math.gcd(width, hidden.shape[1])
     pieces = [pl.ds(k * unit, unit) for k in range(hidden.shape[1] // unit)]
     masks = lane_masks(lens_ref, wanted, chunk * rows, rows)
-    loads = [
-        lambda ref=ref, at=at: ref[:, at * width : (at + 1) * width].astype(f32)
-        for ref, at in ((mine, 0), (theirs, 0), (mine, 1), (theirs, 1))
-    ]
-    normalize(index_ref, loads, gain, normed)
+    for k, refs in enumerate(((left0, left2, right0, right2), (left1, left3, right1, right3))):
+        loads = [lambda ref=ref: ref[...].astype(f32) for ref in refs]
+        normalize(index_ref, loads, gain, normed.at[k * half : (k + 1) * half, :])
     products = sum(
         dot_nt(table[...], normed[:, part_of(index_ref, rel, width)])
         for rel, table in enumerate((table0, table1, table2, table3))
@@ -365,7 +368,7 @@
 
 
 def split_pair(rank, kept, *refs):
-    *arrived, stay, away = refs
+    *arrived, _, stay, away = refs
     half = len(arrived) // 2
     width = away.shape[1]
     row = 0
@@ -386,13 +389,18 @@
     wanted = lens_ref.shape[1]
     width = out.shape[1]
     for c in range(count):
-        stay, arrived, resid = refs[3 * c : 3 * c + 3]
-        rows = resid.shape[0]
+        stay, arrived, *resid = refs[4 * c : 4 * c + 4]
+        half = resid[0].shape[0]
+        rows = 2 * half
         masks = lane_masks(lens_ref, wanted, c * rows, rows)
         lows = stay[rows:, 0:rows] + arrived[rows:, 0:rows].astype(f32)
         total = stay[0:rows, :] + arrived[0:rows, :].astype(f32)
         total = total + delta(lows.astype(bf16).astype(f32), masks, table[...])
-        out[c * rows : (c + 1) * rows, :] = (total + resid[:, 0:width].astype(f32)).astype(bf16)
+        for k, piece in enumerate(resid):
+            at = slice(k * half, (k + 1) * half)
+            out[c * rows + k * half : c * rows + (k + 1) * half, :] = (
+                total[at, :] + piece[...].astype(f32)
+            ).astype(bf16)
 
 
 def rotation_tables(lens, row_count):
@@ -464,7 +472,7 @@
     heads, kv_heads = q_width // HEAD_WIDTH, k_width // HEAD_WIDTH
     unit = math.gcd(width, hidden_width)
     rows = row_count // CHUNKS
-    assert width == q_width == 2 * k_width and rows <= width
+    assert width == q_width == 2 * k_width == row_count
     index = lax.axis_index("tp").astype(jnp.int32).reshape(1)
     me = lax.axis_index("req").astype(jnp.int32).reshape(1)
     want = request_adapter_index
@@ -472,16 +480,14 @@
     peers = groups // 2
     across = swap_across(tokens)
     core = swap_core(tokens)
-    diagonal = swap_core(across)
+    diagonal = swap_diagonal(tokens)
     want_neighbour = swap_req(want, 1)
 
-    def spread_out(block, *after):
-        everyone = [block] + [swap_req(block, 2 * rel) for rel in range(1, peers)]
-        passing = call(
-            pick_for_neighbour, [SMEM] * 2 + [VMEM] * peers + [ANY] * len(after),
-            shaped((peers,) + block.shape[1:], bf16),
-        )(me, want_neighbour, *everyone, *after)
-        return everyone, passing
+    def for_neighbour(blocks, *after):
+        return call(
+            pick_for_neighbour, [SMEM] * 2 + [VMEM] * len(blocks) + [ANY] * 2,
+            shaped((peers,) + blocks[0].shape[-2:], bf16),
+        )(me, want_neighbour, *blocks, *after)
 
     def loaded(weights, after, limit):
         return call(
@@ -521,52 +527,46 @@
     q_gain = query_norm_gain.reshape(1, -1)
     k_gain = key_norm_gain.reshape(1, -1)
     qkv_width = q_width + 2 * k_width
-    normed_own, output_weight, *qkv = call(
-        project_qkv, [SMEM] + [VMEM] * 5 + [ANY] * 6,
-        [shaped((row_count, width), bf16), shaped(output_weight.shape, bf16)] + [shaped((rows, qkv_width), f32)] * CHUNKS,
+    normed_own, *qkv = call(
+        project_qkv, [SMEM] + [VMEM] * 5 + [HBM] * 3,
+        [shaped((row_count, width), bf16)] + [shaped((rows, qkv_width), f32)] * CHUNKS,
         scratch=[
             pltpu.VMEM((row_count, 4 * width), bf16),
             pltpu.VMEM(query_weight.shape, bf16),
             pltpu.VMEM(key_weight.shape, bf16),
             pltpu.VMEM(value_weight.shape, bf16),
-            pltpu.SemaphoreType.DMA((4,)),
+            pltpu.SemaphoreType.DMA((3,)),
         ],
         limit=50,
     )(
         index, tokens, core, across, diagonal, gain_one, query_weight, key_weight, value_weight,
-        output_weight, cosine, sine,
-    )
-    everyone, passing = spread_out(block, normed_own)
-    passed = swap_req(passing, 1)
+    )
+    everyone = [block] + [swap_req(block, 2 * rel) for rel in range(1, peers)]
+    passing = for_neighbour(everyone, cosine, sine)
     block_second = call(hold, [VMEM, ANY], shaped(block_second.shape, bf16))(block_second, passing)
-
-    low, chosen, proj = call(
-        functools.partial(low_first, rank), [SMEM] * 3 + [VMEM] * (peers + 2),
+    second = [block_second] + [swap_req(block_second, 2 * rel) for rel in range(1, peers)]
+    (output_weight,) = loaded((output_weight,), (passing,), 48)
+    low, chosen, low_proj = call(
+        functools.partial(low_first, rank), [SMEM] * 3 + [VMEM] * (peers + 2) + [ANY] * 3,
         [
             shaped((low_qkv, row_count), bf16),
             shaped((wanted, 3 * rank, width), bf16),
-            shaped((wanted * rank, width), bf16),
+            shaped((low_qkv + wanted * rank, width), bf16),
         ],
         scratch=[pltpu.VMEM((wanted * low_qkv, width), bf16)],
-    )(me, want, lengths, *everyone, passed, normed_own)
-    lows = (low, swap_core(low), swap_across(low), swap_diagonal(low))
-    proj_across = swap_across(proj)
-
-    everyone, passing_second = spread_out(block_second, low)
-    passed = swap_req(passing_second, 1)
-    table, down_b, down_a, gate_b, up_b = call(
-        choose_second, [SMEM] * 2 + [VMEM] * (peers + 1),
-        [shaped((wanted * height, columns), bf16) for height, columns in shapes],
-    )(me, want, *everyone, passed)
-    table_across = swap_across(table)
-    tables = (table, swap_core(table), table_across, swap_core(table_across))
+    )(
+        me, want, lengths, *everyone, swap_req(passing, 1), normed_own,
+        cosine, sine, output_weight,
+    )
+    low_proj_across = swap_across(low_proj)
+    lows = (low, swap_core(low), low_proj_across, swap_diagonal(low))
 
     tall = rows + rank
     cuts = [rows // 2, rows // 2 + rank, rows // 2, rows // 2]
     terms = [shaped((tall, 2 * width), f32)] + [shaped((cut, width), bf16) for cut in cuts]
     past = [jnp.zeros((16, k_width), bf16)] * 2
     after = low
-    chips = []
+    residuals = []
     for c in range(CHUNKS):
         new_k, new_v, keep, *sends = call(
             functools.partial(attend, c, heads, kv_heads),
@@ -579,24 +579,38 @@
         past = [new_k, new_v] if c == 0 else [
             jnp.concatenate([old, new], axis=0) for old, new in zip(past, (new_k, new_v))
         ]
-        after = call(add_pair, [VMEM] * 5 + [ANY], shaped((tall, 2 * width), bf16))(
-            keep, *[swap_core(piece) for piece in sends], passing_second
+        if c == 0:
+            passing_second = for_neighbour(second, new_k, low)
+        chip = call(add_pair, [VMEM] * 5 + [ANY] * 2, shaped((tall, 2 * width), bf16))(
+            keep, *[swap_core(piece) for piece in sends], passing_second if c == 0 else residuals[-1][0],
+            keep if c == 0 else table_across,
         )
-        chips.append(after)
-
-    gate_weight, up_weight, down_weight = loaded(
-        (gate_weight, up_weight, down_weight), (after,), 44
-    )
-    ends = []
-    for c in range(CHUNKS):
+        after = chip
+        if c == 0:
+            gate_weight, up_weight, down_weight = loaded(
+                (gate_weight, up_weight, down_weight), (chip,), 44
+            )
+            table, down_b, down_a, gate_b, up_b = call(
+                choose_second, [SMEM] * 2 + [VMEM] * (peers + 1) + [ANY],
+                [shaped((wanted * height, columns), bf16) for height, columns in shapes],
+            )(me, want, *second, swap_req(passing_second, 1), gate_weight)
+            table_across = swap_across(table)
+            tables = (table, swap_core(table), table_across, swap_core(table_across))
         resid = call(
             functools.partial(residual, c), [SMEM] + [VMEM] * 6 + [ANY] * 2,
-            shaped((rows, 2 * width), bf16),
-        )(lengths, chips[c], swap_across(chips[c]), tokens, across, proj, proj_across, after,
-          gate_weight)
+            [shaped((rows // 2, width), bf16)] * 4,
+        )(
+            lengths, chip, swap_across(chip), tokens, across, low_proj, low_proj_across, new_k, table,
+        )
+        residuals.append(resid)
+
+    ends = []
+    arrived = gate_weight
+    for c in range(CHUNKS):
+        resid = residuals[c]
         keep, *sends = call(
             functools.partial(feed_forward, c),
-            [SMEM] * 2 + [VMEM] * 13,
+            [SMEM] * 2 + [VMEM] * 19,
             terms,
             limit=32,
             scratch=[
@@ -604,17 +618,18 @@
                 pltpu.VMEM((rows, hidden_width), bf16),
             ],
         )(
-            index, lengths, resid, swap_core(resid), *tables, down_a, gate_b, up_b,
+            index, lengths, *resid, *[swap_core(piece) for piece in resid], *tables, down_a, gate_b, up_b,
             gain_two, gate_weight, up_weight, down_weight,
         )
         stay, away = call(
-            functools.partial(split_pair, rank), [VMEM] * 5,
+            functools.partial(split_pair, rank), [VMEM] * 5 + [ANY],
             [shaped((tall, width), f32), shaped((tall, width), bf16)],
-        )(keep, *[swap_core(piece) for piece in sends])
+        )(keep, *[swap_core(piece) for piece in sends], arrived)
         after = away
-        ends += [stay, swap_across(away), resid]
+        arrived = swap_across(away)
+        ends += [stay, arrived, *resid[:2]]
     return call(
-        functools.partial(finish, CHUNKS), [SMEM] + [VMEM] * (1 + 3 * CHUNKS),
+        functools.partial(finish, CHUNKS), [SMEM] + [VMEM] * (1 + 4 * CHUNKS),
         shaped((row_count, width), bf16),
     )(lengths, down_b, *ends)
 

time: 129 us -> 115 us (0.89)
  waiting for transfers between devices: 51.2 us -> 32.3 us
  starting transfers between devices: 30.3 us -> 32.4 us
  local copies, waits for them, and re-layouts: 3.22 us -> 4.81 us
    ppermute x8 -> x7, waiting for transfers between devices: 36.1 us -> 12.1 us  [swap_across(): return lax.ppermute(values, 'tp', [(k, k ^ 2) for k in range(4)])]
    ppermute x9, waiting for transfers between devices: 8.42 us -> 11.5 us  [swap_req(): lax.ppermute(values, 'req', [(k, k ^ flips) for k in range(lax.axis_size(...]
    ppermute x1 -> x2, waiting for transfers between devices: 1.38 us -> 3.37 us  [swap_diagonal(): return lax.ppermute(values, 'tp', [(k, k ^ 3) for k in range(4)])]
    ppermute x23 -> x28, starting transfers between devices: 4.46 us -> 6.42 us  [swap_core(): return lax.ppermute(values, 'tp', [(k, k ^ 1) for k in range(4)])]
    unnamed x26 -> x24, local copies, waits for them, and re-layouts: 1.79 us -> 3.43 us
    ppermute x8 -> x7, starting transfers between devices: 10.5 us -> 8.91 us  [swap_across(): return lax.ppermute(values, 'tp', [(k, k ^ 2) for k in range(4)])]
    pallas_call x1 -> x2, Pallas kernels: 3.83 us -> 3.93 us  [loaded(): call(functools.partial(load, len(weights)), [ANY] * (len(weights) + len(a...]
    ppermute x23 -> x28, waiting for transfers between devices: 5.3 us -> 5.31 us  [swap_core(): return lax.ppermute(values, 'tp', [(k, k ^ 1) for k in range(4)])]
  transfers between devices with their start and end apart: 41 -> 46, of which waited for: 19 -> 26; matrix products, arithmetic and copies ran while one was open for 3% -> 3% of each run, Pallas kernels for 23% -> 31%
where the time goes in v3:
time: 115 us; the launch traced here: 114 us
  Pallas kernels  39.7 us (35%)
  starting transfers between devices  32.4 us (28%)
  waiting for transfers between devices  32.3 us (28%)
  local copies, waits for them, and re-layouts  4.81 us (4%)
  other arithmetic  2.37 us (2%)
  between operations  2.21 us (2%)
    ppermute x9, starting transfers between devices, swap_req(): lax.ppermute(values, 'req', [(k, k ^ flips) for k in range(lax.axis_size(...  16.1 us
    ppermute x7, waiting for transfers between devices, swap_across(): return lax.ppermute(values, 'tp', [(k, k ^ 2) for k in range(4)])  12.1 us
    ppermute x9, waiting for transfers between devices, swap_req(): lax.ppermute(values, 'req', [(k, k ^ flips) for k in range(lax.axis_size(...  11.5 us
    pallas_call x2, Pallas kernels, per_device(): call(functools.partial(feed_forward, c), [SMEM] * 2 + [VMEM] * 19, terms,...  10.9 us
    ppermute x7, starting transfers between devices, swap_across(): return lax.ppermute(values, 'tp', [(k, k ^ 2) for k in range(4)])  8.91 us
    pallas_call x2, Pallas kernels, per_device(): call(functools.partial(attend, c, heads, kv_heads), [SMEM] * 2 + [VMEM] *...  8.11 us
    pallas_call x1, Pallas kernels, per_device(): call(project_qkv, [SMEM] + [VMEM] * 5 + [HBM] * 3, [shaped((row_count, wi...  6.8 us
    ppermute x28, starting transfers between devices, swap_core(): return lax.ppermute(values, 'tp', [(k, k ^ 1) for k in range(4)])  6.42 us
  transfers between devices with their start and end apart: 46, of which 26 were waited for; matrix products, arithmetic and copies ran while one was open for 3% of the time, Pallas kernels for 31%

profile of v3, /device:TPU:0, one launch (start us, length us, event | category | flops | bytes accessed | tf_op | source)
XLA Modules:
  0.0 113.7 jit_solution(17724397696486338484)
XLA Ops:
  0.0 1.9 %shard_map.235 = (bf16[2,112,512]{2,1,0:T(8,128)(2,1)}, bf16[2,240,256]{2,1,0:T(8,128)(2,1)}) custom-call(bf16[2,48,512]{2,1,0:T(8,128)(2,1)} %refs_0_.3, bf16[2,16,512]{2,1,0:T(8,128)(2,1)} %refs_1_.2, bf16[2,16,256]{2,1,0:T(8,128)(2,1)} %refs_2_.2, bf16[2,16,256]{2,1,0:T(8,128)(2,1)} %refs_3_.1, bf16[2,16,512]{2,1,0:T(8,128)(2,1)} %refs_4_.1, ...), custom_call_target="tpu_custom_call" | custom-call | flops 1 | bytes 1 | tf_op jit(solution)/shard_map/pallas_call | solution.py:518
  1.9 3.1 %collective-permute-start.1 = (bf16[2,112,512]{2,1,0:T(8,128)(2,1)}, bf16[2,112,512]{2,1,0:T(8,128)(2,1)S(1)}, u32[]{:S(2)}, u32[]{:S(2)}) collective-permute-start(bf16[2,112,512]{2,1,0:T(8,128)(2,1)} %get-tuple-element.57.refs_0_), channel_id=1, source_target_pairs={{0,8},{4,12},{8,0},{12,4},{16,24},{20,28},{24,16},{28,20},{1,9},{5... | collective-permute-start | bytes 688136 | tf_op jit(solution)/shard_map/ppermute | solution.py:433
  5.0 2.6 %collective-permute-start.2 = (bf16[2,112,512]{2,1,0:T(8,128)(2,1)}, bf16[2,112,512]{2,1,0:T(8,128)(2,1)S(1)}, u32[]{:S(2)}, u32[]{:S(2)}) collective-permute-start(bf16[2,112,512]{2,1,0:T(8,128)(2,1)} %get-tuple-element.57.refs_0_), channel_id=1, source_target_pairs={{0,16},{4,20},{8,24},{12,28},{16,0},{20,4},{24,8},{28,12},{1,17},{... | collective-permute-start | bytes 688136 | tf_op jit(solution)/shard_map/ppermute | solution.py:433
  7.6 1.7 %collective-permute-start = (s32[1,4]{1,0:T(1,128)}, s32[1,4]{1,0:T(1,128)S(1)}, u32[]{:S(2)}, u32[]{:S(2)}) collective-permute-start(s32[1,4]{1,0:T(1,128)} %want_ref.3), channel_id=1, source_target_pairs={{0,4},{4,0},{8,12},{12,8},{16,20},{20,16},{24,28},{28,24},{1,5},{5... | collective-permute-start | bytes 56 | tf_op jit(solution)/shard_map/ppermute | solution.py:433
  9.3 1.5 %collective-permute-start.8 = (bf16[512,512]{1,0:T(8,128)(2,1)}, bf16[512,512]{1,0:T(8,128)(2,1)S(1)}, u32[]{:S(2)}, u32[]{:S(2)}) collective-permute-start(bf16[512,512]{1,0:T(8,128)(2,1)} %own.5), channel_id=1, source_target_pairs={{0,2},{1,3},{2,0},{3,1},{4,6},{5,7},{6,4},{7,5},{8,10},{9,11},{10,... | collective-permute-start | bytes 1572872 | tf_op jit(solution)/shard_map/ppermute | solution.py:425
  10.8 1.4 %fusion.1 = (s32[1,1]{1,0:T(1,128)}, s32[1,1]{1,0:T(1,128)}, s32[1,1]{1,0:T(1,128)}) fusion(s32[1,4]{1,0:T(1,128)} %lens_ref.15), kind=kLoop, calls=%fused_computation.9 | loop fusion | bytes 24 | tf_op jit(solution)/shard_map/slice | solution.py:414
  15.5 1.6 %fusion = (f32[512,128]{1,0:T(8,128)S(1)}, f32[512,128]{1,0:T(8,128)S(1)}) fusion(f32[128]{0:T(128)} %constant.22.clone.1, f32[128]{0:T(128)S(1)} %pad_maximum_fusion, f32[512]{0:T(512)S(1)} %subtract_convert_fusion), kind=kLoop, calls=%fused_computation.2 | loop fusion | flops 131072 | bytes 527360 | tf_op jit(solution)/shard_map/mul | solution.py:417
  17.2 7.3 %collective-permute-done.2.refs_2_ = bf16[2,112,512]{2,1,0:T(8,128)(2,1)S(1)} collective-permute-done((bf16[2,112,512]{2,1,0:T(8,128)(2,1)}, bf16[2,112,512]{2,1,0:T(8,128)(2,1)S(1)}, u32[]{:S(2)}, u32[]{:S(2)}) %collective-permute-start.2) | collective-permute-done | bytes 229408 | tf_op jit(solution)/shard_map/ppermute | solution.py:433
  26.0 1.6 %collective-permute-start.10 = (bf16[4,112,512]{2,1,0:T(8,128)(2,1)S(1)}, bf16[4,112,512]{2,1,0:T(8,128)(2,1)}, u32[]{:S(2)}, u32[]{:S(2)}) collective-permute-start(bf16[4,112,512]{2,1,0:T(8,128)(2,1)S(1)} %shard_map.236.after.refs_1_), channel_id=1, source_target_pairs={{0,4},{4,0},{8,12},{12,8},{16,20},{20,16},{24,28},{28,24},{1,5},{5... | collective-permute-start | bytes 1376264 | tf_op jit(solution)/shard_map/ppermute | solution.py:433
  27.6 4.1 %collective-permute-start.4 = (bf16[2,240,256]{2,1,0:T(8,128)(2,1)S(1)}, bf16[2,240,256]{2,1,0:T(8,128)(2,1)S(1)}, u32[]{:S(2)}, u32[]{:S(2)}) collective-permute-start(bf16[2,240,256]{2,1,0:T(8,128)(2,1)S(1)} %shard_map.237.refs_0_), channel_id=1, source_target_pairs={{0,8},{4,12},{8,0},{12,4},{16,24},{20,28},{24,16},{28,20},{1,9},{5... | collective-permute-start | bytes 737288 | tf_op jit(solution)/shard_map/ppermute | solution.py:433
  31.8 1.1 collective-permute-start.5
  32.8 1.6 %copy-done.1 = bf16[512,2048]{1,0:T(8,128)(2,1)S(1)} copy-done((bf16[512,2048]{1,0:T(8,128)(2,1)S(1)}, bf16[512,2048]{1,0:T(8,128)(2,1)}, u32[]{:S(2)}) %copy-start.1) | copy-done | bytes 2097176
  35.5 6.8 %shard_map.238 = (bf16[512,512]{1,0:T(8,128)(2,1)S(1)}, f32[256,1024]{1,0:T(8,128)S(1)}, f32[256,1024]{1,0:T(8,128)}) custom-call(s32[1]{0:T(128)} %bitcast.4.index_ref, bf16[512,512]{1,0:T(8,128)(2,1)S(1)} %copy-done, bf16[512,512]{1,0:T(8,128)(2,1)S(1)} %collective-permute-done.7.core, bf16[512,512]{1,0:T(8,128)(2,1)S(1)} %collective-permute-done.8.across, ...), custom_call_target="tpu_custom_call" | custom-call | flops 1 | bytes 1 | tf_op jit(solution)/shard_map/pallas_call | solution.py:530
  42.4 1.7 %shard_map.240 = (bf16[48,512]{1,0:T(8,128)(2,1)S(1)}, bf16[4,48,512]{2,1,0:T(8,128)(2,1)S(1)}, bf16[112,512]{1,0:T(8,128)(2,1)S(1)}) custom-call(s32[1]{0:T(128)} %bitcast.me_ref, s32[1,4]{1,0:T(1,128)S(1)} %copy-done.11, s32[1,4]{1,0:T(1,128)S(1)} %copy-done.6, bf16[2,112,512]{2,1,0:T(8,128)(2,1)S(1)} %copy-done.4, ...), custom_call_target="tpu_custom_call" | custom-call | flops 1 | bytes 1 | tf_op jit(solution)/shard_map/pallas_call | solution.py:549
  44.0 1.6 %collective-permute-start.12 = (bf16[112,512]{1,0:T(8,128)(2,1)S(1)}, bf16[112,512]{1,0:T(8,128)(2,1)S(1)}, u32[]{:S(2)}, u32[]{:S(2)}) collective-permute-start(bf16[112,512]{1,0:T(8,128)(2,1)S(1)} %get-tuple-element.61.table), channel_id=1, source_target_pairs={{0,2},{1,3},{2,0},{3,1},{4,6},{5,7},{6,4},{7,5},{8,10},{9,11},{10,... | collective-permute-start | bytes 344072 | tf_op jit(solution)/shard_map/ppermute | solution.py:425
  45.6 1.4 %collective-permute-start.6 = (bf16[2,240,256]{2,1,0:T(8,128)(2,1)S(1)}, bf16[2,240,256]{2,1,0:T(8,128)(2,1)S(1)}, u32[]{:S(2)}, u32[]{:S(2)}) collective-permute-start(bf16[2,240,256]{2,1,0:T(8,128)(2,1)S(1)} %shard_map.237.refs_0_), channel_id=1, source_target_pairs={{0,24},{4,28},{8,16},{12,20},{16,8},{20,12},{24,0},{28,4},{1,25},{... | collective-permute-start | bytes 737288 | tf_op jit(solution)/shard_map/ppermute | solution.py:433
  47.3 3.4 %collective-permute-done.13.low3 = bf16[48,512]{1,0:T(8,128)(2,1)S(1)} collective-permute-done((bf16[48,512]{1,0:T(8,128)(2,1)S(1)}, bf16[48,512]{1,0:T(8,128)(2,1)S(1)}, u32[]{:S(2)}, u32[]{:S(2)}) %collective-permute-start.13) | collective-permute-done | bytes 49184 | tf_op jit(solution)/shard_map/ppermute | solution.py:429
  50.7 4.0 %shard_map.241 = (bf16[256,256]{1,0:T(8,128)(2,1)S(1)}, bf16[256,256]{1,0:T(8,128)(2,1)S(1)}, f32[272,1024]{1,0:T(8,128)S(1)}, bf16[128,512]{1,0:T(8,128)(2,1)S(...) custom-call(s32[1]{0:T(128)} %bitcast.4.index_ref, ...), custom_call_target="tpu_custom_call" | custom-call | flops 1 | bytes 1 | tf_op jit(solution)/shard_map/pallas_call | solution.py:571
  58.3 4.2 %shard_map.249 = (bf16[256,256]{1,0:T(8,128)(2,1)S(1)}, bf16[256,256]{1,0:T(8,128)(2,1)}, f32[272,1024]{1,0:T(8,128)S(1)}, bf16[128,512]{1,0:T(8,128)(2,1)S(1)},...) custom-call(s32[1]{0:T(128)} %bitcast.4.index_ref, ...), custom_call_target="tpu_custom_call" | custom-call | flops 1 | bytes 1 | tf_op jit(solution)/shard_map/pallas_call | solution.py:571
  62.9 3.8 %shard_map.244 = (bf16[2048,768]{1,0:T(8,128)(2,1)S(1)}, bf16[2048,768]{1,0:T(8,128)(2,1)S(1)}, bf16[768,2048]{1,0:T(8,128)(2,1)S(1)}) custom-call(bf16[2048,768]{1,0:T(8,128)(2,1)} %refs_0_.5, bf16[2048,768]{1,0:T(8,128)(2,1)} %refs_1_.3, bf16[768,2048]{1,0:T(8,128)(2,1)} %refs_2_.3, bf16[272,1024]{1,0:T(8,128)(2,1)S(1)} %shard_map.243.refs_3_.chip.after), custom_call_target="tpu_custom_call" | custom-call | flops 1 | bytes 1 | tf_op jit(solution)/shard_map/pallas_call | solution.py:493
  66.7 4.1 %collective-permute-done.14.refs_4_ = bf16[4,240,256]{2,1,0:T(8,128)(2,1)S(1)} collective-permute-done((bf16[4,240,256]{2,1,0:T(8,128)(2,1)S(1)}, bf16[4,240,256]{2,1,0:T(8,128)(2,1)S(1)}, u32[]{:S(2)}, u32[]{:S(2)}) %collective-permute-start.14) | collective-permute-done | bytes 491552 | tf_op jit(solution)/shard_map/ppermute | solution.py:433
  70.8 1.0 shard_map.245
  71.9 1.5 %collective-permute-start.25 = (bf16[128,512]{1,0:T(8,128)(2,1)S(1)}, bf16[128,512]{1,0:T(8,128)(2,1)S(1)}, u32[]{:S(2)}, u32[]{:S(2)}) collective-permute-start(bf16[128,512]{1,0:T(8,128)(2,1)S(1)} %get-tuple-element.71.touched.table0), channel_id=1, source_target_pairs={{0,2},{1,3},{2,0},{3,1},{4,6},{5,7},{6,4},{7,5},{8,10},{9,11},{10,... | collective-permute-start | bytes 393224 | tf_op jit(solution)/shard_map/ppermute | solution.py:425
  74.4 3.4 %collective-permute-done.25.table2.refs_5_ = bf16[128,512]{1,0:T(8,128)(2,1)S(1)} collective-permute-done((bf16[128,512]{1,0:T(8,128)(2,1)S(1)}, bf16[128,512]{1,0:T(8,128)(2,1)S(1)}, u32[]{:S(2)}, u32[]{:S(2)}) %collective-permute-start.25) | collective-permute-done | bytes 131104 | tf_op jit(solution)/shard_map/ppermute | solution.py:425
  77.9 1.6 %collective-permute-start.36 = (bf16[272,1024]{1,0:T(8,128)(2,1)S(1)}, bf16[272,1024]{1,0:T(8,128)(2,1)S(1)}, u32[]{:S(2)}, u32[]{:S(2)}) collective-permute-start(bf16[272,1024]{1,0:T(8,128)(2,1)S(1)} %shard_map.250.chip), channel_id=1, source_target_pairs={{0,2},{1,3},{2,0},{3,1},{4,6},{5,7},{6,4},{7,5},{8,10},{9,11},{10,... | collective-permute-start | bytes 1671176 | tf_op jit(solution)/shard_map/ppermute | solution.py:425
  82.4 5.5 %shard_map.247 = (f32[272,1024]{1,0:T(8,128)S(1)}, bf16[128,512]{1,0:T(8,128)(2,1)S(1)}, bf16[144,512]{1,0:T(8,128)(2,1)S(1)}, bf16[128,512]{1,0:T(8,128)(2,1)S(1)}, bf16[128,512]{1,0:T(8,128)(2,1)S(1)}) custom-call(s32[1]{0:T(128)} %bitcast.4.index_ref, s32[1,4]{1,0:T(1,128)S(1)} %copy-done.6, bf16[128,512]{1,0:T(8,128)(2,1)S(1)} %get-tuple-element.72.left0.refs_4_.refs_2_, ...), custom_call_target="tpu_custom_call" | custom-call | flops 1 | bytes 1 | tf_op jit(solution)/shard_map/pallas_call | solution.py:611
  90.8 1.4 %collective-permute-done.36.arrived = bf16[272,1024]{1,0:T(8,128)(2,1)S(1)} collective-permute-done((bf16[272,1024]{1,0:T(8,128)(2,1)S(1)}, bf16[272,1024]{1,0:T(8,128)(2,1)S(1)}, u32[]{:S(2)}, u32[]{:S(2)}) %collective-permute-start.36) | collective-permute-done | bytes 557088 | tf_op jit(solution)/shard_map/ppermute | solution.py:425
  92.2 1.0 shard_map.251
  95.3 5.5 %shard_map.252 = (f32[272,1024]{1,0:T(8,128)S(1)}, bf16[128,512]{1,0:T(8,128)(2,1)S(1)}, bf16[144,512]{1,0:T(8,128)(2,1)S(1)}, bf16[128,512]{1,0:T(8,128)(2,1)S(1)}, bf16[128,512]{1,0:T(8,128)(2,1)S(1)}) custom-call(s32[1]{0:T(128)} %bitcast.4.index_ref, s32[1,4]{1,0:T(1,128)S(1)} %copy-done.6, bf16[128,512]{1,0:T(8,128)(2,1)S(1)} %get-tuple-element.96.left0.refs_6_, ...), custom_call_target="tpu_custom_call" | custom-call | flops 1 | bytes 1 | tf_op jit(solution)/shard_map/pallas_call | solution.py:611
  103.2 1.6 %collective-permute-start.45 = (bf16[272,512]{1,0:T(8,128)(2,1)S(1)}, bf16[272,512]{1,0:T(8,128)(2,1)S(1)}, u32[]{:S(2)}, u32[]{:S(2)}) collective-permute-start(bf16[272,512]{1,0:T(8,128)(2,1)S(1)} %get-tuple-element.106), channel_id=1, source_target_pairs={{0,2},{1,3},{2,0},{3,1},{4,6},{5,7},{6,4},{7,5},{8,10},{9,11},{10,... | collective-permute-start | bytes 835592 | tf_op jit(solution)/shard_map/ppermute | solution.py:425
  104.8 7.2 %collective-permute-done.45.refs_5_ = bf16[272,512]{1,0:T(8,128)(2,1)S(1)} collective-permute-done((bf16[272,512]{1,0:T(8,128)(2,1)S(1)}, bf16[272,512]{1,0:T(8,128)(2,1)S(1)}, u32[]{:S(2)}, u32[]{:S(2)}) %collective-permute-start.45) | collective-permute-done | bytes 278560 | tf_op jit(solution)/shard_map/ppermute | solution.py:425
  112.0 1.7 %shard_map.254 = bf16[512,512]{1,0:T(8,128)(2,1)} custom-call(s32[1,4]{1,0:T(1,128)S(1)} %copy-done.6, bf16[64,512]{1,0:T(8,128)(2,1)S(1)} %get-tuple-element.70.table, f32[272,512]{1,0:T(8,128)S(1)} %get-tuple-element.86.refs_0_, bf16[272,512]{1,0:T(8,128)(2,1)S(1)} %collective-permute-done.31.refs_4_.refs_1_, ...), custom_call_target="tpu_custom_call" | custom-call | flops 1 | bytes 1 | tf_op jit(solution)/shard_map/pallas_call | solution.py:631
  (110 shorter events, 20.0 us)
Async XLA Ops:
  1.9 13.1 %collective-permute-start.1 = (bf16[2,112,512]{2,1,0:T(8,128)(2,1)}, bf16[2,112,512]{2,1,0:T(8,128)(2,1)S(1)}, u32[]{:S(2)}, u32[]{:S(2)}) collective-permute-start(bf16[2,112,512]{2,1,0:T(8,128)(2,1)} %get-tuple-element.57.refs_0_), channel_id=1, source_target_pairs={{0,8},{4,12},{8,0},{12,4},{16,24},{20,28},{24,16},{28,20},{1,9},{5... | collective-permute-start | bytes 688136 | tf_op jit(solution)/shard_map/ppermute | solution.py:433
  5.0 19.5 %collective-permute-start.2 = (bf16[2,112,512]{2,1,0:T(8,128)(2,1)}, bf16[2,112,512]{2,1,0:T(8,128)(2,1)S(1)}, u32[]{:S(2)}, u32[]{:S(2)}) collective-permute-start(bf16[2,112,512]{2,1,0:T(8,128)(2,1)} %get-tuple-element.57.refs_0_), channel_id=1, source_target_pairs={{0,16},{4,20},{8,24},{12,28},{16,0},{20,4},{24,8},{28,12},{1,17},{... | collective-permute-start | bytes 688136 | tf_op jit(solution)/shard_map/ppermute | solution.py:433
  7.6 16.9 %collective-permute-start.3 = (bf16[2,112,512]{2,1,0:T(8,128)(2,1)}, bf16[2,112,512]{2,1,0:T(8,128)(2,1)S(1)}, u32[]{:S(2)}, u32[]{:S(2)}) collective-permute-start(bf16[2,112,512]{2,1,0:T(8,128)(2,1)} %get-tuple-element.57.refs_0_), channel_id=1, source_target_pairs={{0,24},{4,28},{8,16},{12,20},{16,8},{20,12},{24,0},{28,4},{1,25},{... | collective-permute-start | bytes 688136 | tf_op jit(solution)/shard_map/ppermute | solution.py:433
  7.6 7.2 %collective-permute-start = (s32[1,4]{1,0:T(1,128)}, s32[1,4]{1,0:T(1,128)S(1)}, u32[]{:S(2)}, u32[]{:S(2)}) collective-permute-start(s32[1,4]{1,0:T(1,128)} %want_ref.3), channel_id=1, source_target_pairs={{0,4},{4,0},{8,12},{12,8},{16,20},{20,16},{24,28},{28,24},{1,5},{5... | collective-permute-start | bytes 56 | tf_op jit(solution)/shard_map/ppermute | solution.py:433
  9.3 22.4 %collective-permute-start.8 = (bf16[512,512]{1,0:T(8,128)(2,1)}, bf16[512,512]{1,0:T(8,128)(2,1)S(1)}, u32[]{:S(2)}, u32[]{:S(2)}) collective-permute-start(bf16[512,512]{1,0:T(8,128)(2,1)} %own.5), channel_id=1, source_target_pairs={{0,2},{1,3},{2,0},{3,1},{4,6},{5,7},{6,4},{7,5},{8,10},{9,11},{10,... | collective-permute-start | bytes 1572872 | tf_op jit(solution)/shard_map/ppermute | solution.py:425
  14.8 19.8 %collective-permute-start.7 = (bf16[512,512]{1,0:T(8,128)(2,1)}, bf16[512,512]{1,0:T(8,128)(2,1)S(1)}, u32[]{:S(2)}, u32[]{:S(2)}) collective-permute-start(bf16[512,512]{1,0:T(8,128)(2,1)} %own.5), channel_id=1, source_target_pairs={{0,1},{1,0},{2,3},{3,2},{4,5},{5,4},{6,7},{7,6},{8,9},{9,8},{10,11... | collective-permute-start | bytes 1572872 | tf_op jit(solution)/shard_map/ppermute | solution.py:421
  14.9 19.7 %collective-permute-start.9 = (bf16[512,512]{1,0:T(8,128)(2,1)}, bf16[512,512]{1,0:T(8,128)(2,1)}, u32[]{:S(2)}, u32[]{:S(2)}) collective-permute-start(bf16[512,512]{1,0:T(8,128)(2,1)} %own.5), channel_id=1, source_target_pairs={{0,3},{1,2},{2,1},{3,0},{4,7},{5,6},{6,5},{7,4},{8,11},{9,10},{10,... | collective-permute-start | bytes 1572872 | tf_op jit(solution)/shard_map/ppermute | solution.py:429
  26.0 16.3 %collective-permute-start.10 = (bf16[4,112,512]{2,1,0:T(8,128)(2,1)S(1)}, bf16[4,112,512]{2,1,0:T(8,128)(2,1)}, u32[]{:S(2)}, u32[]{:S(2)}) collective-permute-start(bf16[4,112,512]{2,1,0:T(8,128)(2,1)S(1)} %shard_map.236.after.refs_1_), channel_id=1, source_target_pairs={{0,4},{4,0},{8,12},{12,8},{16,20},{20,16},{24,28},{28,24},{1,5},{5... | collective-permute-start | bytes 1376264 | tf_op jit(solution)/shard_map/ppermute | solution.py:433
  27.6 27.6 %collective-permute-start.4 = (bf16[2,240,256]{2,1,0:T(8,128)(2,1)S(1)}, bf16[2,240,256]{2,1,0:T(8,128)(2,1)S(1)}, u32[]{:S(2)}, u32[]{:S(2)}) collective-permute-start(bf16[2,240,256]{2,1,0:T(8,128)(2,1)S(1)} %shard_map.237.refs_0_), channel_id=1, source_target_pairs={{0,8},{4,12},{8,0},{12,4},{16,24},{20,28},{24,16},{28,20},{1,9},{5... | collective-permute-start | bytes 737288 | tf_op jit(solution)/shard_map/ppermute | solution.py:433
  31.8 23.9 %collective-permute-start.5 = (bf16[2,240,256]{2,1,0:T(8,128)(2,1)S(1)}, bf16[2,240,256]{2,1,0:T(8,128)(2,1)S(1)}, u32[]{:S(2)}, u32[]{:S(2)}) collective-permute-start(bf16[2,240,256]{2,1,0:T(8,128)(2,1)S(1)} %shard_map.237.refs_0_), channel_id=1, source_target_pairs={{0,16},{4,20},{8,24},{12,28},{16,0},{20,4},{24,8},{28,12},{1,17},{... | collective-permute-start | bytes 737288 | tf_op jit(solution)/shard_map/ppermute | solution.py:433
  44.0 6.7 %collective-permute-start.12 = (bf16[112,512]{1,0:T(8,128)(2,1)S(1)}, bf16[112,512]{1,0:T(8,128)(2,1)S(1)}, u32[]{:S(2)}, u32[]{:S(2)}) collective-permute-start(bf16[112,512]{1,0:T(8,128)(2,1)S(1)} %get-tuple-element.61.table), channel_id=1, source_target_pairs={{0,2},{1,3},{2,0},{3,1},{4,6},{5,7},{6,4},{7,5},{8,10},{9,11},{10,... | collective-permute-start | bytes 344072 | tf_op jit(solution)/shard_map/ppermute | solution.py:425
  45.6 10.3 %collective-permute-start.6 = (bf16[2,240,256]{2,1,0:T(8,128)(2,1)S(1)}, bf16[2,240,256]{2,1,0:T(8,128)(2,1)S(1)}, u32[]{:S(2)}, u32[]{:S(2)}) collective-permute-start(bf16[2,240,256]{2,1,0:T(8,128)(2,1)S(1)} %shard_map.237.refs_0_), channel_id=1, source_target_pairs={{0,24},{4,28},{8,16},{12,20},{16,8},{20,12},{24,0},{28,4},{1,25},{... | collective-permute-start | bytes 737288 | tf_op jit(solution)/shard_map/ppermute | solution.py:433
  47.0 3.7 %collective-permute-start.13 = (bf16[48,512]{1,0:T(8,128)(2,1)S(1)}, bf16[48,512]{1,0:T(8,128)(2,1)S(1)}, u32[]{:S(2)}, u32[]{:S(2)}) collective-permute-start(bf16[48,512]{1,0:T(8,128)(2,1)S(1)} %get-tuple-element.60.low0.after.refs_5_), channel_id=1, source_target_pairs={{0,3},{1,2},{2,1},{3,0},{4,7},{5,6},{6,5},{7,4},{8,11},{9,10},{10,... | collective-permute-start | bytes 147464 | tf_op jit(solution)/shard_map/ppermute | solution.py:429
  54.7 2.4 %collective-permute-start.16 = (bf16[144,512]{1,0:T(8,128)(2,1)S(1)}, bf16[144,512]{1,0:T(8,128)(2,1)S(1)}, u32[]{:S(2)}, u32[]{:S(2)}) collective-permute-start(bf16[144,512]{1,0:T(8,128)(2,1)S(1)} %get-tuple-element.66), channel_id=1, source_target_pairs={{0,1},{1,0},{2,3},{3,2},{4,5},{5,4},{6,7},{7,6},{8,9},{9,8},{10,11... | collective-permute-start | bytes 442376 | tf_op jit(solution)/shard_map/ppermute | solution.py:421
  55.3 1.4 %collective-permute-start.17 = (bf16[128,512]{1,0:T(8,128)(2,1)S(1)}, bf16[128,512]{1,0:T(8,128)(2,1)S(1)}, u32[]{:S(2)}, u32[]{:S(2)}) collective-permute-start(bf16[128,512]{1,0:T(8,128)(2,1)S(1)} %get-tuple-element.67), channel_id=1, source_target_pairs={{0,1},{1,0},{2,3},{3,2},{4,5},{5,4},{6,7},{7,6},{8,9},{9,8},{10,11... | collective-permute-start | bytes 393224 | tf_op jit(solution)/shard_map/ppermute | solution.py:421
  57.1 14.8 %collective-permute-start.19 = (bf16[272,1024]{1,0:T(8,128)(2,1)S(1)}, bf16[272,1024]{1,0:T(8,128)(2,1)S(1)}, u32[]{:S(2)}, u32[]{:S(2)}) collective-permute-start(bf16[272,1024]{1,0:T(8,128)(2,1)S(1)} %shard_map.243.refs_3_.chip.after), channel_id=1, source_target_pairs={{0,2},{1,3},{2,0},{3,1},{4,6},{5,7},{6,4},{7,5},{8,10},{9,11},{10,... | collective-permute-start | bytes 1671176 | tf_op jit(solution)/shard_map/ppermute | solution.py:425
  57.8 13.0 %collective-permute-start.14 = (bf16[4,240,256]{2,1,0:T(8,128)(2,1)S(1)}, bf16[4,240,256]{2,1,0:T(8,128)(2,1)S(1)}, u32[]{:S(2)}, u32[]{:S(2)}) collective-permute-start(bf16[4,240,256]{2,1,0:T(8,128)(2,1)S(1)} %shard_map.242.refs_4_), channel_id=1, source_target_pairs={{0,4},{4,0},{8,12},{12,8},{16,20},{20,16},{24,28},{28,24},{1,5},{5... | collective-permute-start | bytes 1474568 | tf_op jit(solution)/shard_map/ppermute | solution.py:433
  62.4 12.0 %collective-permute-start.33 = (bf16[144,512]{1,0:T(8,128)(2,1)S(1)}, bf16[144,512]{1,0:T(8,128)(2,1)S(1)}, u32[]{:S(2)}, u32[]{:S(2)}) collective-permute-start(bf16[144,512]{1,0:T(8,128)(2,1)S(1)} %get-tuple-element.92), channel_id=1, source_target_pairs={{0,1},{1,0},{2,3},{3,2},{4,5},{5,4},{6,7},{7,6},{8,9},{9,8},{10,11... | collective-permute-start | bytes 442376 | tf_op jit(solution)/shard_map/ppermute | solution.py:421
  62.4 11.9 %collective-permute-start.32 = (bf16[128,512]{1,0:T(8,128)(2,1)S(1)}, bf16[128,512]{1,0:T(8,128)(2,1)S(1)}, u32[]{:S(2)}, u32[]{:S(2)}) collective-permute-start(bf16[128,512]{1,0:T(8,128)(2,1)S(1)} %get-tuple-element.91), channel_id=1, source_target_pairs={{0,1},{1,0},{2,3},{3,2},{4,5},{5,4},{6,7},{7,6},{8,9},{9,8},{10,11... | collective-permute-start | bytes 393224 | tf_op jit(solution)/shard_map/ppermute | solution.py:421
  62.9 11.4 %collective-permute-start.34 = (bf16[128,512]{1,0:T(8,128)(2,1)S(1)}, bf16[128,512]{1,0:T(8,128)(2,1)S(1)}, u32[]{:S(2)}, u32[]{:S(2)}) collective-permute-start(bf16[128,512]{1,0:T(8,128)(2,1)S(1)} %get-tuple-element.93), channel_id=1, source_target_pairs={{0,1},{1,0},{2,3},{3,2},{4,5},{5,4},{6,7},{7,6},{8,9},{9,8},{10,11... | collective-permute-start | bytes 393224 | tf_op jit(solution)/shard_map/ppermute | solution.py:421
  70.8 3.6 %collective-permute-start.35 = (bf16[128,512]{1,0:T(8,128)(2,1)S(1)}, bf16[128,512]{1,0:T(8,128)(2,1)S(1)}, u32[]{:S(2)}, u32[]{:S(2)}) collective-permute-start(bf16[128,512]{1,0:T(8,128)(2,1)S(1)} %get-tuple-element.94), channel_id=1, source_target_pairs={{0,1},{1,0},{2,3},{3,2},{4,5},{5,4},{6,7},{7,6},{8,9},{9,8},{10,11... | collective-permute-start | bytes 393224 | tf_op jit(solution)/shard_map/ppermute | solution.py:421
  71.9 5.9 %collective-permute-start.25 = (bf16[128,512]{1,0:T(8,128)(2,1)S(1)}, bf16[128,512]{1,0:T(8,128)(2,1)S(1)}, u32[]{:S(2)}, u32[]{:S(2)}) collective-permute-start(bf16[128,512]{1,0:T(8,128)(2,1)S(1)} %get-tuple-element.71.touched.table0), channel_id=1, source_target_pairs={{0,2},{1,3},{2,0},{3,1},{4,6},{5,7},{6,4},{7,5},{8,10},{9,11},{10,... | collective-permute-start | bytes 393224 | tf_op jit(solution)/shard_map/ppermute | solution.py:425
  77.9 14.3 %collective-permute-start.36 = (bf16[272,1024]{1,0:T(8,128)(2,1)S(1)}, bf16[272,1024]{1,0:T(8,128)(2,1)S(1)}, u32[]{:S(2)}, u32[]{:S(2)}) collective-permute-start(bf16[272,1024]{1,0:T(8,128)(2,1)S(1)} %shard_map.250.chip), channel_id=1, source_target_pairs={{0,2},{1,3},{2,0},{3,1},{4,6},{5,7},{6,4},{7,5},{8,10},{9,11},{10,... | collective-permute-start | bytes 1671176 | tf_op jit(solution)/shard_map/ppermute | solution.py:425
  79.5 1.5 %collective-permute-start.26 = (bf16[128,512]{1,0:T(8,128)(2,1)S(1)}, bf16[128,512]{1,0:T(8,128)(2,1)S(1)}, u32[]{:S(2)}, u32[]{:S(2)}) collective-permute-start(bf16[128,512]{1,0:T(8,128)(2,1)S(1)} %collective-permute-done.25.table2.refs_5_), channel_id=1, source_target_pairs={{0,1},{1,0},{2,3},{3,2},{4,5},{5,4},{6,7},{7,6},{8,9},{9,8},{10,11... | collective-permute-start | bytes 393224 | tf_op jit(solution)/shard_map/ppermute | solution.py:421
  80.0 1.5 %collective-permute-start.21 = (bf16[128,512]{1,0:T(8,128)(2,1)S(1)}, bf16[128,512]{1,0:T(8,128)(2,1)S(1)}, u32[]{:S(2)}, u32[]{:S(2)}) collective-permute-start(bf16[128,512]{1,0:T(8,128)(2,1)S(1)} %get-tuple-element.73.left1.refs_3_), channel_id=1, source_target_pairs={{0,1},{1,0},{2,3},{3,2},{4,5},{5,4},{6,7},{7,6},{8,9},{9,8},{10,11... | collective-permute-start | bytes 393224 | tf_op jit(solution)/shard_map/ppermute | solution.py:421
  87.9 2.3 %collective-permute-start.28 = (bf16[144,512]{1,0:T(8,128)(2,1)S(1)}, bf16[144,512]{1,0:T(8,128)(2,1)S(1)}, u32[]{:S(2)}, u32[]{:S(2)}) collective-permute-start(bf16[144,512]{1,0:T(8,128)(2,1)S(1)} %get-tuple-element.83), channel_id=1, source_target_pairs={{0,1},{1,0},{2,3},{3,2},{4,5},{5,4},{6,7},{7,6},{8,9},{9,8},{10,11... | collective-permute-start | bytes 442376 | tf_op jit(solution)/shard_map/ppermute | solution.py:421
  90.2 11.6 %collective-permute-start.31 = (bf16[272,512]{1,0:T(8,128)(2,1)S(1)}, bf16[272,512]{1,0:T(8,128)(2,1)S(1)}, u32[]{:S(2)}, u32[]{:S(2)}) collective-permute-start(bf16[272,512]{1,0:T(8,128)(2,1)S(1)} %get-tuple-element.87), channel_id=1, source_target_pairs={{0,2},{1,3},{2,0},{3,1},{4,6},{5,7},{6,4},{7,5},{8,10},{9,11},{10,... | collective-permute-start | bytes 835592 | tf_op jit(solution)/shard_map/ppermute | solution.py:425
  93.2 1.4 %collective-permute-start.37 = (bf16[128,512]{1,0:T(8,128)(2,1)S(1)}, bf16[128,512]{1,0:T(8,128)(2,1)S(1)}, u32[]{:S(2)}, u32[]{:S(2)}) collective-permute-start(bf16[128,512]{1,0:T(8,128)(2,1)S(1)} %get-tuple-element.96.left0.refs_6_), channel_id=1, source_target_pairs={{0,1},{1,0},{2,3},{3,2},{4,5},{5,4},{6,7},{7,6},{8,9},{9,8},{10,11... | collective-permute-start | bytes 393224 | tf_op jit(solution)/shard_map/ppermute | solution.py:421
  93.3 1.5 %collective-permute-start.38 = (bf16[128,512]{1,0:T(8,128)(2,1)S(1)}, bf16[128,512]{1,0:T(8,128)(2,1)S(1)}, u32[]{:S(2)}, u32[]{:S(2)}) collective-permute-start(bf16[128,512]{1,0:T(8,128)(2,1)S(1)} %get-tuple-element.97.left1.refs_7_), channel_id=1, source_target_pairs={{0,1},{1,0},{2,3},{3,2},{4,5},{5,4},{6,7},{7,6},{8,9},{9,8},{10,11... | collective-permute-start | bytes 393224 | tf_op jit(solution)/shard_map/ppermute | solution.py:421
  93.9 1.5 %collective-permute-start.40 = (bf16[128,512]{1,0:T(8,128)(2,1)S(1)}, bf16[128,512]{1,0:T(8,128)(2,1)S(1)}, u32[]{:S(2)}, u32[]{:S(2)}) collective-permute-start(bf16[128,512]{1,0:T(8,128)(2,1)S(1)} %get-tuple-element.99.right1), channel_id=1, source_target_pairs={{0,1},{1,0},{2,3},{3,2},{4,5},{5,4},{6,7},{7,6},{8,9},{9,8},{10,11... | collective-permute-start | bytes 393224 | tf_op jit(solution)/shard_map/ppermute | solution.py:421
  100.8 2.2 %collective-permute-start.42 = (bf16[144,512]{1,0:T(8,128)(2,1)S(1)}, bf16[144,512]{1,0:T(8,128)(2,1)S(1)}, u32[]{:S(2)}, u32[]{:S(2)}) collective-permute-start(bf16[144,512]{1,0:T(8,128)(2,1)S(1)} %get-tuple-element.102), channel_id=1, source_target_pairs={{0,1},{1,0},{2,3},{3,2},{4,5},{5,4},{6,7},{7,6},{8,9},{9,8},{10,11... | collective-permute-start | bytes 442376 | tf_op jit(solution)/shard_map/ppermute | solution.py:421
  103.2 8.8 %collective-permute-start.45 = (bf16[272,512]{1,0:T(8,128)(2,1)S(1)}, bf16[272,512]{1,0:T(8,128)(2,1)S(1)}, u32[]{:S(2)}, u32[]{:S(2)}) collective-permute-start(bf16[272,512]{1,0:T(8,128)(2,1)S(1)} %get-tuple-element.106), channel_id=1, source_target_pairs={{0,2},{1,3},{2,0},{3,1},{4,6},{5,7},{6,4},{7,5},{8,10},{9,11},{10,... | collective-permute-start | bytes 835592 | tf_op jit(solution)/shard_map/ppermute | solution.py:425
  (26 other events, 98.8 us)

commit v4 on v3

--- a/solution.py
+++ b/solution.py
@@ -111,24 +111,27 @@
     return me_ref[0] ^ (2 * rel + flip)
 
 
-def pick_for_neighbour(me_ref, want_ref, *refs):
-    *packed, _, _, send = refs
-    held = packed[0].shape[-3]
-    for rel in range(send.shape[0]):
+def pick_for_neighbour(count, me_ref, want_ref, *refs):
+    packed, sends = refs[:count], refs[count + 1 :]
+    held = packed[0].shape[0]
+    for rel, ref in enumerate(packed):
         owner = owner_at(me_ref, rel, 0)
-        ref = packed[rel]
         pick = jnp.int32(0)
         for j in range(want_ref.shape[1]):
             a = want_ref[0, j]
             pick = pick + jnp.where(a // held == owner, a % held, 0)
-        send[rel] = ref[pick]
+        row = 0
+        for send in sends:
+            height = send.shape[1]
+            send[rel] = ref[pick, row : row + height, :]
+            row += height
 
 
 def hold(block, after, out):
     out[...] = block[...]
 
 
-def each_asked(me_ref, want_ref, packed, passed, use):
+def each_asked(me_ref, want_ref, packed, passed, use, first=0):
     held = packed[0].shape[-3]
     for rel in range(passed.shape[0]):
         for flip in range(2):
@@ -141,7 +144,8 @@
 
             @pl.when(found > 0)
             def _():
-                use(slot, passed.at[rel] if flip else packed[rel].at[pick])
+                rows = pl.ds(first, passed.shape[1])
+                use(slot, passed.at[rel] if flip else packed[rel].at[pick, rows, :])
 
 
 def normalize(index_ref, refs, gain, normed, keep_own=None):
@@ -158,29 +162,45 @@
 
 
 def project_qkv(
-    index_ref, own, core, across, diagonal, gain, q_hbm, k_hbm, v_hbm,
-    normed_own, *rest,
+    index_ref, own, core, across, diagonal, gain, q_hbm, k_hbm, v_hbm, out_hbm,
+    normed_own, out_w, *rest,
 ):
-    *outs, normed, q_w, k_w, v_w, sems = rest
-    copies = start_all([(q_hbm, q_w), (k_hbm, k_w), (v_hbm, v_w)], sems)
-    rows = own.shape[0] // len(outs)
+    *outs, q_w, k_w, v_w, sems = rest
+    rows, width = own.shape[0] // len(outs), own.shape[1]
     q_width, k_width = q_w.shape[1], k_w.shape[1]
+    parts = [part_of(index_ref, rel, width) for rel in range(4)]
+    pairs = []
+    for part in parts:
+        pairs += [(a.at[part, :], b.at[part, :]) for a, b in ((q_hbm, q_w), (k_hbm, k_w), (v_hbm, v_w))]
+    copies = start_all(pairs + [(out_hbm, out_w)], sems)
+    scales = []
     for c in range(len(outs)):
         here = slice(c * rows, (c + 1) * rows)
-
-        def keep_own(value):
-            normed_own[here, :] = value
-
-        loads = [lambda ref=ref: ref[here, :].astype(f32) for ref in (own, core, across, diagonal)]
-        normalize(index_ref, loads, gain, normed.at[here, :], keep_own)
-    for w, copy, low, high in (
-        (q_w, copies[0], 0, q_width),
-        (k_w, copies[1], q_width, q_width + k_width),
-        (v_w, copies[2], q_width + k_width, q_width + 2 * k_width),
-    ):
-        copy.wait()
+        square = jnp.zeros((rows, 1), f32)
+        for ref in (own, core, across, diagonal):
+            block = ref[here, :].astype(f32)
+            square = square + jnp.sum(block * block, axis=1, keepdims=True)
+        scales.append(lax.rsqrt(square / (4 * width) + epsilon))
+    for rel, ref in enumerate((own, core, across, diagonal)):
+        part = parts[rel]
+        for copy in copies[3 * rel : 3 * rel + 3]:
+            copy.wait()
         for c, out in enumerate(outs):
-            out[:, low:high] = dot(normed[c * rows : (c + 1) * rows, :], w[...])
+            here = slice(c * rows, (c + 1) * rows)
+            normed = (ref[here, :].astype(f32) * scales[c] * gain[:, part]).astype(bf16)
+            if rel == 0:
+                normed_own[here, :] = normed
+            for w, low, high in (
+                (q_w, 0, q_width),
+                (k_w, q_width, q_width + k_width),
+                (v_w, q_width + k_width, q_width + 2 * k_width),
+            ):
+                term = dot(normed, w[part, :])
+                if rel == 0:
+                    out[:, low:high] = term
+                else:
+                    out[:, low:high] += term
+    copies[-1].wait()
 
 
 def rows_of(slot, height):
@@ -188,22 +208,18 @@
 
 
 def low_first(rank, me_ref, want_ref, lens_ref, *refs):
-    *packed, passed, normed_own, _, _, _, out, chosen, both, stack = refs
+    *packed, passed, normed_own, _, _, out, chosen, stack = refs
     wanted = want_ref.shape[1]
     low = out.shape[0]
 
     def use(slot, block):
         stack[rows_of(slot, low), :] = block[0:low, :]
         chosen[slot] = block[low : low + 3 * rank, :]
-        at = pl.ds(pl.multiple_of(low + slot * rank, 16), rank)
-        both[at, :] = block[low + 3 * rank :, :]
 
     each_asked(me_ref, want_ref, packed, passed, use)
     products = dot_nt(stack[...], normed_own[...])
     masks = lane_masks(lens_ref, wanted, 0, normed_own.shape[0])
-    value = merged(products, masks, low).astype(bf16)
-    out[...] = value
-    both[0:low, :] = value
+    out[...] = merged(products, masks, low).astype(bf16)
 
 
 def attend(
@@ -286,7 +302,7 @@
 
 
 def add_pair(kept, *refs):
-    *arrived, _, _, out = refs
+    *arrived, _, _, _, out = refs
     half = len(arrived) // 2
     width = out.shape[1] // 2
     for at, pieces in ((slice(0, width), arrived[:half]), (slice(width, 2 * width), arrived[half:])):
@@ -297,7 +313,7 @@
             row += piece.shape[0]
 
 
-def residual(chunk, lens_ref, chip, arrived, own, across, table, table_across, after, touched, *outs):
+def residual(chunk, lens_ref, chip, arrived, own, across, table, table_across, after, *outs):
     half, width = outs[0].shape
     rows = 2 * half
     wanted = lens_ref.shape[1]
@@ -317,21 +333,20 @@
         outs[2 * number + 1][...] = total[half:]
 
 
-def choose_second(me_ref, want_ref, *refs):
-    *packed, passed, _ = refs[:-5]
-    outs = refs[-5:]
+def choose_second(first, count, sizes, me_ref, want_ref, *refs):
+    packed, passed, outs = refs[:count], refs[count], refs[count + 2 :]
     unit = passed.shape[2]
-    wanted = want_ref.shape[1]
 
     def use(slot, block):
         row = 0
-        for out in outs:
-            height = out.shape[0] // wanted
+        for number, start, height in sizes:
+            out = outs[number]
+            at = pl.ds(pl.multiple_of(start + slot * height, 16), height)
             for k in range(out.shape[1] // unit):
-                out[rows_of(slot, height), k * unit : (k + 1) * unit] = block[row : row + height, :]
+                out[at, k * unit : (k + 1) * unit] = block[row : row + height, :]
                 row += height
 
-    each_asked(me_ref, want_ref, packed, passed, use)
+    each_asked(me_ref, want_ref, packed, passed, use, first)
 
 
 def feed_forward(
@@ -344,7 +359,8 @@
     half, width = left0.shape
     rows = 2 * half
     wanted = lens_ref.shape[1]
-    low, rank = table0.shape[0] // wanted, stack_a.shape[0] // wanted
+    rank = stack_a.shape[0] // wanted
+    low = table0.shape[0] // wanted - rank
     unit = math.gcd(width, hidden.shape[1])
     pieces = [pl.ds(k * unit, unit) for k in range(hidden.shape[1] // unit)]
     masks = lane_masks(lens_ref, wanted, chunk * rows, rows)
@@ -352,7 +368,7 @@
         loads = [lambda ref=ref: ref[...].astype(f32) for ref in refs]
         normalize(index_ref, loads, gain, normed.at[k * half : (k + 1) * half, :])
     products = sum(
-        dot_nt(table[...], normed[:, part_of(index_ref, rel, width)])
+        dot_nt(table[0 : wanted * low, :], normed[:, part_of(index_ref, rel, width)])
         for rel, table in enumerate((table0, table1, table2, table3))
     )
     total = merged(products, masks, low).astype(bf16).astype(f32)
@@ -480,14 +496,15 @@
     peers = groups // 2
     across = swap_across(tokens)
     core = swap_core(tokens)
-    diagonal = swap_diagonal(tokens)
+    diagonal = swap_core(across)
     want_neighbour = swap_req(want, 1)
 
-    def for_neighbour(blocks, *after):
+    def for_neighbour(blocks, after, heights):
         return call(
-            pick_for_neighbour, [SMEM] * 2 + [VMEM] * len(blocks) + [ANY] * 2,
-            shaped((peers,) + blocks[0].shape[-2:], bf16),
-        )(me, want_neighbour, *blocks, *after)
+            functools.partial(pick_for_neighbour, len(blocks)),
+            [SMEM] * 2 + [VMEM] * len(blocks) + [ANY],
+            [shaped((peers, height, blocks[0].shape[2]), bf16) for height in heights],
+        )(me, want_neighbour, *blocks, after)
 
     def loaded(weights, after, limit):
         return call(
@@ -498,7 +515,7 @@
 
     tables = (
         query_key_value_adapter_input, query_adapter_output, key_adapter_output, value_adapter_output,
-        output_adapter_input, projection_adapter_output, gate_up_adapter_input, down_adapter_output,
+        output_adapter_input, gate_up_adapter_input, projection_adapter_output, down_adapter_output,
         down_adapter_input, gate_adapter_output, up_adapter_output,
     )
     plan = (
@@ -507,17 +524,16 @@
         (2, (0, k_width), low_qkv + rank, 0),
         (3, (0, k_width), low_qkv + rank, k_width),
         (4, (0, width), low_qkv + 2 * rank, 0),
-        (5, (0, width), low_qkv + 3 * rank, 0),
     )
     plan_second, row = [], 0
-    shapes = ((low_gu, width), (rank, width)) + ((rank, hidden_width),) * 3
+    shapes = ((low_gu, width), (rank, width), (rank, width)) + ((rank, hidden_width),) * 3
     for table, (height, columns) in enumerate(shapes):
         for k in range(columns // unit):
-            plan_second.append((6 + table, (k * unit, unit), row, 0))
+            plan_second.append((5 + table, (k * unit, unit), row, 0))
             row += height
     block, block_second = call(
         functools.partial(gather_tables, (plan, tuple(plan_second))), [ANY] * len(tables),
-        [shaped((held, low_qkv + 4 * rank, width), bf16), shaped((held, row, unit), bf16)],
+        [shaped((held, low_qkv + 3 * rank, width), bf16), shaped((held, row, unit), bf16)],
         scratch=[pltpu.SemaphoreType.DMA((len(plan) + len(plan_second),))], limit=60,
     )(*tables)
     cosine, sine = rotation_tables(lengths[0], row_count)
@@ -527,39 +543,36 @@
     q_gain = query_norm_gain.reshape(1, -1)
     k_gain = key_norm_gain.reshape(1, -1)
     qkv_width = q_width + 2 * k_width
-    normed_own, *qkv = call(
-        project_qkv, [SMEM] + [VMEM] * 5 + [HBM] * 3,
-        [shaped((row_count, width), bf16)] + [shaped((rows, qkv_width), f32)] * CHUNKS,
+    normed_own, output_weight, *qkv = call(
+        project_qkv, [SMEM] + [VMEM] * 5 + [HBM] * 4,
+        [shaped((row_count, width), bf16), shaped(output_weight.shape, bf16)] + [shaped((rows, qkv_width), f32)] * CHUNKS,
         scratch=[
-            pltpu.VMEM((row_count, 4 * width), bf16),
             pltpu.VMEM(query_weight.shape, bf16),
             pltpu.VMEM(key_weight.shape, bf16),
             pltpu.VMEM(value_weight.shape, bf16),
-            pltpu.SemaphoreType.DMA((3,)),
+            pltpu.SemaphoreType.DMA((13,)),
         ],
         limit=50,
     )(
         index, tokens, core, across, diagonal, gain_one, query_weight, key_weight, value_weight,
+        output_weight,
     )
     everyone = [block] + [swap_req(block, 2 * rel) for rel in range(1, peers)]
-    passing = for_neighbour(everyone, cosine, sine)
+    (passing,) = for_neighbour(everyone, sine, [low_qkv + 3 * rank])
     block_second = call(hold, [VMEM, ANY], shaped(block_second.shape, bf16))(block_second, passing)
     second = [block_second] + [swap_req(block_second, 2 * rel) for rel in range(1, peers)]
-    (output_weight,) = loaded((output_weight,), (passing,), 48)
-    low, chosen, low_proj = call(
-        functools.partial(low_first, rank), [SMEM] * 3 + [VMEM] * (peers + 2) + [ANY] * 3,
+    low, chosen = call(
+        functools.partial(low_first, rank), [SMEM] * 3 + [VMEM] * (peers + 2) + [ANY] * 2,
         [
             shaped((low_qkv, row_count), bf16),
             shaped((wanted, 3 * rank, width), bf16),
-            shaped((low_qkv + wanted * rank, width), bf16),
         ],
         scratch=[pltpu.VMEM((wanted * low_qkv, width), bf16)],
     )(
         me, want, lengths, *everyone, swap_req(passing, 1), normed_own,
-        cosine, sine, output_weight,
-    )
-    low_proj_across = swap_across(low_proj)
-    lows = (low, swap_core(low), low_proj_across, swap_diagonal(low))
+        cosine, sine,
+    )
+    lows = (low, swap_core(low), swap_across(low), swap_diagonal(low))
 
     tall = rows + rank
     cuts = [rows // 2, rows // 2 + rank, rows // 2, rows // 2]
@@ -580,27 +593,40 @@
             jnp.concatenate([old, new], axis=0) for old, new in zip(past, (new_k, new_v))
         ]
         if c == 0:
-            passing_second = for_neighbour(second, new_k, low)
-        chip = call(add_pair, [VMEM] * 5 + [ANY] * 2, shaped((tall, 2 * width), bf16))(
-            keep, *[swap_core(piece) for piece in sends], passing_second if c == 0 else residuals[-1][0],
-            keep if c == 0 else table_across,
+            heights = [height * (columns // unit) for height, columns in shapes]
+            cuts_second = [sum(heights[:2]), sum(heights[2:])]
+            passing_second = for_neighbour(second, new_k, cuts_second)
+        chip = call(add_pair, [VMEM] * 5 + [ANY] * 3, shaped((tall, 2 * width), bf16))(
+            keep, *[swap_core(piece) for piece in sends], passing_second[0] if c == 0 else arrived,
+            keep if c == 0 else table_across, keep if c == 0 else gate_weight,
         )
         after = chip
         if c == 0:
+            def chosen_second(part, outs, sizes, after):
+                return call(
+                    functools.partial(choose_second, part * cuts_second[0], peers, sizes),
+                    [SMEM] * 2 + [VMEM] * (peers + 1) + [ANY], outs,
+                )(me, want, *second, swap_req(passing_second[part], 1), after)
+
+            (table,) = chosen_second(
+                0, [shaped((wanted * (low_gu + rank), width), bf16)],
+                ((0, 0, low_gu), (0, wanted * low_gu, rank)), chip,
+            )
             gate_weight, up_weight, down_weight = loaded(
-                (gate_weight, up_weight, down_weight), (chip,), 44
+                (gate_weight, up_weight, down_weight), (table,), 44
             )
-            table, down_b, down_a, gate_b, up_b = call(
-                choose_second, [SMEM] * 2 + [VMEM] * (peers + 1) + [ANY],
-                [shaped((wanted * height, columns), bf16) for height, columns in shapes],
-            )(me, want, *second, swap_req(passing_second, 1), gate_weight)
+            down_b, down_a, gate_b, up_b = chosen_second(
+                1, [shaped((wanted * h, w), bf16) for h, w in shapes[2:]],
+                tuple((k, 0, h) for k, (h, _) in enumerate(shapes[2:])), table,
+            )
             table_across = swap_across(table)
             tables = (table, swap_core(table), table_across, swap_core(table_across))
+        arrived = swap_across(chip)
         resid = call(
-            functools.partial(residual, c), [SMEM] + [VMEM] * 6 + [ANY] * 2,
+            functools.partial(residual, c), [SMEM] + [VMEM] * 6 + [ANY],
             [shaped((rows // 2, width), bf16)] * 4,
         )(
-            lengths, chip, swap_across(chip), tokens, across, low_proj, low_proj_across, new_k, table,
+            lengths, chip, arrived, tokens, across, table, table_across, gate_weight,
         )
         residuals.append(resid)
 

time: 115 us -> 109 us (0.948); the launches traced: 114 us -> 109 us
  starting transfers between devices: 32.4 us -> 29.3 us
  waiting for transfers between devices: 32.3 us -> 30.6 us
    ppermute x9 -> x10, starting transfers between devices: 16.1 us -> 13 us  [swap_req(): lax.ppermute(values, 'req', [(k, k ^ flips) for k in range(lax.axis_size(...]
    ppermute x7, waiting for transfers between devices: 12.1 us -> 13.8 us  [swap_across(): return lax.ppermute(values, 'tp', [(k, k ^ 2) for k in range(4)])]
    ppermute x9 -> x10, waiting for transfers between devices: 11.5 us -> 9.82 us  [swap_req(): lax.ppermute(values, 'req', [(k, k ^ flips) for k in range(lax.axis_size(...]
    mul x1 -> x0, other arithmetic: 1.64 us -> none  [rotation_tables(): return (jnp.cos(angle), jnp.sin(angle) * sign[None, :])]
    cos x0 -> x1, other arithmetic: none -> 1.64 us  [rotation_tables(): return (jnp.cos(angle), jnp.sin(angle) * sign[None, :])]
    ppermute x28 -> x29, waiting for transfers between devices: 5.31 us -> 4.1 us  [swap_core(): return lax.ppermute(values, 'tp', [(k, k ^ 1) for k in range(4)])]
    ppermute x28 -> x29, starting transfers between devices: 6.42 us -> 7.26 us  [swap_core(): return lax.ppermute(values, 'tp', [(k, k ^ 1) for k in range(4)])]
    unnamed x24 -> x32, local copies, waits for them, and re-layouts: 3.43 us -> 2.89 us
  transfers between devices with their start and end apart: 46 -> 47, of which waited for: 26 -> 22; matrix products, arithmetic and copies ran while one was open for 3% -> 3% of each run, Pallas kernels for 31% -> 35%
where the time goes in v4:
time: 109 us
  Pallas kernels  40.2 us (37%)
  waiting for transfers between devices  30.6 us (28%)
  starting transfers between devices  29.3 us (27%)
  local copies, waits for them, and re-layouts  4.31 us (4%)
  other arithmetic  2.3 us (2%)
  between operations  2.27 us (2%)
    ppermute x7, waiting for transfers between devices, swap_across(): return lax.ppermute(values, 'tp', [(k, k ^ 2) for k in range(4)])  13.8 us
    ppermute x10, starting transfers between devices, swap_req(): lax.ppermute(values, 'req', [(k, k ^ flips) for k in range(lax.axis_size(...  13 us
    pallas_call x2, Pallas kernels, per_device(): call(functools.partial(feed_forward, c), [SMEM] * 2 + [VMEM] * 19, terms,...  11 us
    ppermute x10, waiting for transfers between devices, swap_req(): lax.ppermute(values, 'req', [(k, k ^ flips) for k in range(lax.axis_size(...  9.82 us
    ppermute x7, starting transfers between devices, swap_across(): return lax.ppermute(values, 'tp', [(k, k ^ 2) for k in range(4)])  8.97 us
    pallas_call x2, Pallas kernels, per_device(): call(functools.partial(attend, c, heads, kv_heads), [SMEM] * 2 + [VMEM] *...  8.08 us
    ppermute x29, starting transfers between devices, swap_core(): return lax.ppermute(values, 'tp', [(k, k ^ 1) for k in range(4)])  7.26 us
    pallas_call x1, Pallas kernels, per_device(): call(project_qkv, [SMEM] + [VMEM] * 5 + [HBM] * 4, [shaped((row_count, wi...  6.6 us
  transfers between devices with their start and end apart: 47, of which 22 were waited for; matrix products, arithmetic and copies ran while one was open for 3% of the time, Pallas kernels for 35%

profile of v4, /device:TPU:0, one launch (start us, length us, event | category | flops | bytes accessed | tf_op | source)
XLA Modules:
  0.0 109.0 jit_solution(6196404864667182215)
XLA Ops:
  0.0 2.9 %collective-permute-start.8 = (bf16[512,512]{1,0:T(8,128)(2,1)}, bf16[512,512]{1,0:T(8,128)(2,1)S(1)}, u32[]{:S(2)}, u32[]{:S(2)}) collective-permute-start(bf16[512,512]{1,0:T(8,128)(2,1)} %own.5), channel_id=1, source_target_pairs={{0,2},{1,3},{2,0},{3,1},{4,6},{5,7},{6,4},{7,5},{8,10},{9,11},{10,... | collective-permute-start | bytes 1572872 | tf_op jit(solution)/shard_map/ppermute | solution.py:441
  2.9 1.9 %shard_map.235 = (bf16[2,96,512]{2,1,0:T(8,128)(2,1)}, bf16[2,272,256]{2,1,0:T(8,128)(2,1)}) custom-call(bf16[2,48,512]{2,1,0:T(8,128)(2,1)} %refs_0_.2, bf16[2,16,512]{2,1,0:T(8,128)(2,1)} %refs_1_.2, bf16[2,16,256]{2,1,0:T(8,128)(2,1)} %refs_2_.2, bf16[2,16,256]{2,1,0:T(8,128)(2,1)} %refs_3_.1, bf16[2,16,512]{2,1,0:T(8,128)(2,1)} %refs_4_.1, ...), custom_call_target="tpu_custom_call" | custom-call | flops 1 | bytes 1 | tf_op jit(solution)/shard_map/pallas_call | solution.py:534
  4.9 3.7 %collective-permute-start.3 = (bf16[2,96,512]{2,1,0:T(8,128)(2,1)}, bf16[2,96,512]{2,1,0:T(8,128)(2,1)S(1)}, u32[]{:S(2)}, u32[]{:S(2)}) collective-permute-start(bf16[2,96,512]{2,1,0:T(8,128)(2,1)} %get-tuple-element.57.refs_0_), channel_id=1, source_target_pairs={{0,24},{4,28},{8,16},{12,20},{16,8},{20,12},{24,0},{28,4},{1,25},{... | collective-permute-start | bytes 589832 | tf_op jit(solution)/shard_map/ppermute | solution.py:449
  9.3 1.5 %collective-permute-start = (s32[1,4]{1,0:T(1,128)}, s32[1,4]{1,0:T(1,128)S(1)}, u32[]{:S(2)}, u32[]{:S(2)}) collective-permute-start(s32[1,4]{1,0:T(1,128)} %want_ref.5), channel_id=1, source_target_pairs={{0,4},{4,0},{8,12},{12,8},{16,20},{20,16},{24,28},{28,24},{1,5},{5... | collective-permute-start | bytes 56 | tf_op jit(solution)/shard_map/ppermute | solution.py:449
  10.8 1.4 %fusion.1 = (s32[1,1]{1,0:T(1,128)}, s32[1,1]{1,0:T(1,128)}, s32[1,1]{1,0:T(1,128)}) fusion(s32[1,4]{1,0:T(1,128)} %lens_ref.15), kind=kLoop, calls=%fused_computation.9 | loop fusion | bytes 24 | tf_op jit(solution)/shard_map/slice | solution.py:430
  15.4 1.6 %multiply_cosine_fusion = (f32[512,128]{1,0:T(8,128)S(1)}, f32[512,128]{1,0:T(8,128)S(1)}) fusion(f32[128]{0:T(128)S(1)} %pad_maximum_fusion, f32[512]{0:T(512)S(1)} %subtract_convert_fusion, f32[128]{0:T(128)} %constant.22.clone.1), kind=kLoop, calls=%fused_computation | loop fusion | flops 131072 | bytes 527360 | tf_op jit(solution)/shard_map/cos | solution.py:433
  17.0 8.1 %collective-permute-done.2.refs_2_ = bf16[2,96,512]{2,1,0:T(8,128)(2,1)S(1)} collective-permute-done((bf16[2,96,512]{2,1,0:T(8,128)(2,1)}, bf16[2,96,512]{2,1,0:T(8,128)(2,1)S(1)}, u32[]{:S(2)}, u32[]{:S(2)}) %collective-permute-start.2) | collective-permute-done | bytes 196640 | tf_op jit(solution)/shard_map/ppermute | solution.py:449
  25.2 1.0 copy-done.3
  26.8 1.6 %collective-permute-start.10 = (bf16[4,96,512]{2,1,0:T(8,128)(2,1)S(1)}, bf16[4,96,512]{2,1,0:T(8,128)(2,1)}, u32[]{:S(2)}, u32[]{:S(2)}) collective-permute-start(bf16[4,96,512]{2,1,0:T(8,128)(2,1)S(1)} %shard_map.236.after), channel_id=1, source_target_pairs={{0,4},{4,0},{8,12},{12,8},{16,20},{20,16},{24,28},{28,24},{1,5},{5... | collective-permute-start | bytes 1179656 | tf_op jit(solution)/shard_map/ppermute | solution.py:449
  28.4 2.5 %collective-permute-start.6 = (bf16[2,272,256]{2,1,0:T(8,128)(2,1)S(1)}, bf16[2,272,256]{2,1,0:T(8,128)(2,1)S(1)}, u32[]{:S(2)}, u32[]{:S(2)}) collective-permute-start(bf16[2,272,256]{2,1,0:T(8,128)(2,1)S(1)} %shard_map.237.refs_0_), channel_id=1, source_target_pairs={{0,24},{4,28},{8,16},{12,20},{16,8},{20,12},{24,0},{28,4},{1,25},{... | collective-permute-start | bytes 835592 | tf_op jit(solution)/shard_map/ppermute | solution.py:449
  31.7 1.9 %collective-permute-start.4 = (bf16[2,272,256]{2,1,0:T(8,128)(2,1)S(1)}, bf16[2,272,256]{2,1,0:T(8,128)(2,1)S(1)}, u32[]{:S(2)}, u32[]{:S(2)}) collective-permute-start(bf16[2,272,256]{2,1,0:T(8,128)(2,1)S(1)} %shard_map.237.refs_0_), channel_id=1, source_target_pairs={{0,8},{4,12},{8,0},{12,4},{16,24},{20,28},{24,16},{28,20},{1,9},{5... | collective-permute-start | bytes 835592 | tf_op jit(solution)/shard_map/ppermute | solution.py:449
  33.6 1.0 copy-done.8
  34.7 6.6 %shard_map.238 = (bf16[512,512]{1,0:T(8,128)(2,1)S(1)}, bf16[512,2048]{1,0:T(8,128)(2,1)}, f32[256,1024]{1,0:T(8,128)S(1)}, f32[256,1024]{1,0:T(8,128)}) custom-call(s32[1]{0:T(128)} %bitcast.4.index_ref, bf16[512,512]{1,0:T(8,128)(2,1)S(1)} %copy-done.1, bf16[512,512]{1,0:T(8,128)(2,1)S(1)} %copy-done.8, ...), custom_call_target="tpu_custom_call" | custom-call | flops 1 | bytes 1 | tf_op jit(solution)/shard_map/pallas_call | solution.py:546
  41.4 1.8 %shard_map.239 = (bf16[48,512]{1,0:T(8,128)(2,1)S(1)}, bf16[4,48,512]{2,1,0:T(8,128)(2,1)S(1)}) custom-call(s32[1]{0:T(128)} %bitcast.me_ref, s32[1,4]{1,0:T(1,128)S(1)} %copy-done.13, s32[1,4]{1,0:T(1,128)S(1)} %copy-done.10, bf16[2,96,512]{2,1,0:T(8,128)(2,1)S(1)} %copy-done.4, bf16[2,96,512]{2,1,0:T(8,128)(2,1)S(1)} %copy-done.6, ...), custom_call_target="tpu_custom_call" | custom-call | flops 1 | bytes 1 | tf_op jit(solution)/shard_map/pallas_call | solution.py:564
  43.8 2.9 %collective-permute-done.13.low3 = bf16[48,512]{1,0:T(8,128)(2,1)S(1)} collective-permute-done((bf16[48,512]{1,0:T(8,128)(2,1)S(1)}, bf16[48,512]{1,0:T(8,128)(2,1)S(1)}, u32[]{:S(2)}, u32[]{:S(2)}) %collective-permute-start.13) | collective-permute-done | bytes 49184 | tf_op jit(solution)/shard_map/ppermute | solution.py:445
  46.7 1.0 collective-permute-done.12.low2
  48.0 3.9 %shard_map.240 = (bf16[256,256]{1,0:T(8,128)(2,1)S(1)}, bf16[256,256]{1,0:T(8,128)(2,1)S(1)}, f32[272,1024]{1,0:T(8,128)S(1)}, bf16[128,512]{1,0:T(8,128)(2,1)S(...) custom-call(s32[1]{0:T(128)} %bitcast.4.index_ref, ...), custom_call_target="tpu_custom_call" | custom-call | flops 1 | bytes 1 | tf_op jit(solution)/shard_map/pallas_call | solution.py:584
  54.2 1.1 collective-permute-start.20
  55.8 4.1 %shard_map.249 = (bf16[256,256]{1,0:T(8,128)(2,1)}, bf16[256,256]{1,0:T(8,128)(2,1)}, f32[272,1024]{1,0:T(8,128)S(1)}, bf16[128,512]{1,0:T(8,128)(2,1)S(1)}, bf1...) custom-call(s32[1]{0:T(128)} %bitcast.4.index_ref, s32[1,4]{1,0:T(1,128)S(1)} %copy-done.10, ...), custom_call_target="tpu_custom_call" | custom-call | flops 1 | bytes 1 | tf_op jit(solution)/shard_map/pallas_call | solution.py:584
  60.4 1.7 %collective-permute-done.15.refs_4_ = bf16[4,96,256]{2,1,0:T(8,128)(2,1)S(1)} collective-permute-done((bf16[4,96,256]{2,1,0:T(8,128)(2,1)S(1)}, bf16[4,96,256]{2,1,0:T(8,128)(2,1)S(1)}, u32[]{:S(2)}, u32[]{:S(2)}) %collective-permute-start.15) | collective-permute-done | bytes 196640 | tf_op jit(solution)/shard_map/ppermute | solution.py:449
  62.1 1.0 shard_map.243.refs_5_.refs_3_.table.table0
  63.1 1.1 collective-permute-start.21
  65.2 3.8 %shard_map.245 = (bf16[2048,768]{1,0:T(8,128)(2,1)S(1)}, bf16[2048,768]{1,0:T(8,128)(2,1)S(1)}, bf16[768,2048]{1,0:T(8,128)(2,1)S(1)}) custom-call(bf16[2048,768]{1,0:T(8,128)(2,1)} %refs_0_.3, bf16[2048,768]{1,0:T(8,128)(2,1)} %refs_1_.3, bf16[768,2048]{1,0:T(8,128)(2,1)} %refs_2_.3, bf16[192,512]{1,0:T(8,128)(2,1)S(1)} %shard_map.243.refs_5_.refs_3_.table.table0), custom_call_target="tpu_custom_call" | custom-call | flops 1 | bytes 1 | tf_op jit(solution)/shard_map/pallas_call | solution.py:510
  69.0 4.3 %collective-permute-done.21.table_across.table2.refs_5_ = bf16[192,512]{1,0:T(8,128)(2,1)S(1)} collective-permute-done((bf16[192,512]{1,0:T(8,128)(2,1)S(1)}, bf16[192,512]{1,0:T(8,128)(2,1)S(1)}, u32[]{:S(2)}, u32[]{:S(2)}) %collective-permute-start.21) | collective-permute-done | bytes 196640 | tf_op jit(solution)/shard_map/ppermute | solution.py:441
  73.4 1.1 collective-permute-start.37
  78.1 5.5 %shard_map.247 = (f32[272,1024]{1,0:T(8,128)S(1)}, bf16[128,512]{1,0:T(8,128)(2,1)S(1)}, bf16[144,512]{1,0:T(8,128)(2,1)S(1)}, bf16[128,512]{1,0:T(8,128)(2,1)S(1)}, bf16[128,512]{1,0:T(8,128)(2,1)S(1)}) custom-call(s32[1]{0:T(128)} %bitcast.4.index_ref, s32[1,4]{1,0:T(1,128)S(1)} %copy-done.10, bf16[128,512]{1,0:T(8,128)(2,1)S(1)} %get-tuple-element.73.left0.refs_2_, ...), custom_call_target="tpu_custom_call" | custom-call | flops 1 | bytes 1 | tf_op jit(solution)/shard_map/pallas_call | solution.py:637
  85.9 1.1 collective-permute-start.32
  87.5 1.0 shard_map.251
  90.6 5.5 %shard_map.252 = (f32[272,1024]{1,0:T(8,128)S(1)}, bf16[128,512]{1,0:T(8,128)(2,1)S(1)}, bf16[144,512]{1,0:T(8,128)(2,1)S(1)}, bf16[128,512]{1,0:T(8,128)(2,1)S(1)}, bf16[128,512]{1,0:T(8,128)(2,1)S(1)}) custom-call(s32[1]{0:T(128)} %bitcast.4.index_ref, s32[1,4]{1,0:T(1,128)S(1)} %copy-done.10, bf16[128,512]{1,0:T(8,128)(2,1)S(1)} %get-tuple-element.96.left0.refs_6_, ...), custom_call_target="tpu_custom_call" | custom-call | flops 1 | bytes 1 | tf_op jit(solution)/shard_map/pallas_call | solution.py:637
  98.5 1.1 %collective-permute-start.46 = (bf16[272,512]{1,0:T(8,128)(2,1)S(1)}, bf16[272,512]{1,0:T(8,128)(2,1)S(1)}, u32[]{:S(2)}, u32[]{:S(2)}) collective-permute-start(bf16[272,512]{1,0:T(8,128)(2,1)S(1)} %get-tuple-element.106), channel_id=1, source_target_pairs={{0,2},{1,3},{2,0},{3,1},{4,6},{5,7},{6,4},{7,5},{8,10},{9,11},{10,... | collective-permute-start | bytes 835592 | tf_op jit(solution)/shard_map/ppermute | solution.py:441
  99.6 7.7 %collective-permute-done.46.refs_5_ = bf16[272,512]{1,0:T(8,128)(2,1)S(1)} collective-permute-done((bf16[272,512]{1,0:T(8,128)(2,1)S(1)}, bf16[272,512]{1,0:T(8,128)(2,1)S(1)}, u32[]{:S(2)}, u32[]{:S(2)}) %collective-permute-start.46) | collective-permute-done | bytes 278560 | tf_op jit(solution)/shard_map/ppermute | solution.py:441
  107.3 1.7 %shard_map.254 = bf16[512,512]{1,0:T(8,128)(2,1)} custom-call(s32[1,4]{1,0:T(1,128)S(1)} %copy-done.10, bf16[64,512]{1,0:T(8,128)(2,1)S(1)} %get-tuple-element.71.table, f32[272,512]{1,0:T(8,128)S(1)} %get-tuple-element.87.refs_0_, bf16[272,512]{1,0:T(8,128)(2,1)S(1)} %collective-permute-done.32.refs_4_.refs_1_, ...), custom_call_target="tpu_custom_call" | custom-call | flops 1 | bytes 1 | tf_op jit(solution)/shard_map/pallas_call | solution.py:657
  (120 shorter events, 19.5 us)
Async XLA Ops:
  0.0 15.1 %collective-permute-start.8 = (bf16[512,512]{1,0:T(8,128)(2,1)}, bf16[512,512]{1,0:T(8,128)(2,1)S(1)}, u32[]{:S(2)}, u32[]{:S(2)}) collective-permute-start(bf16[512,512]{1,0:T(8,128)(2,1)} %own.5), channel_id=1, source_target_pairs={{0,2},{1,3},{2,0},{3,1},{4,6},{5,7},{6,4},{7,5},{8,10},{9,11},{10,... | collective-permute-start | bytes 1572872 | tf_op jit(solution)/shard_map/ppermute | solution.py:441
  4.9 12.2 %collective-permute-start.3 = (bf16[2,96,512]{2,1,0:T(8,128)(2,1)}, bf16[2,96,512]{2,1,0:T(8,128)(2,1)S(1)}, u32[]{:S(2)}, u32[]{:S(2)}) collective-permute-start(bf16[2,96,512]{2,1,0:T(8,128)(2,1)} %get-tuple-element.57.refs_0_), channel_id=1, source_target_pairs={{0,24},{4,28},{8,16},{12,20},{16,8},{20,12},{24,0},{28,4},{1,25},{... | collective-permute-start | bytes 589832 | tf_op jit(solution)/shard_map/ppermute | solution.py:449
  8.5 16.6 %collective-permute-start.2 = (bf16[2,96,512]{2,1,0:T(8,128)(2,1)}, bf16[2,96,512]{2,1,0:T(8,128)(2,1)S(1)}, u32[]{:S(2)}, u32[]{:S(2)}) collective-permute-start(bf16[2,96,512]{2,1,0:T(8,128)(2,1)} %get-tuple-element.57.refs_0_), channel_id=1, source_target_pairs={{0,16},{4,20},{8,24},{12,28},{16,0},{20,4},{24,8},{28,12},{1,17},{... | collective-permute-start | bytes 589832 | tf_op jit(solution)/shard_map/ppermute | solution.py:449
  8.5 16.6 %collective-permute-start.1 = (bf16[2,96,512]{2,1,0:T(8,128)(2,1)}, bf16[2,96,512]{2,1,0:T(8,128)(2,1)S(1)}, u32[]{:S(2)}, u32[]{:S(2)}) collective-permute-start(bf16[2,96,512]{2,1,0:T(8,128)(2,1)} %get-tuple-element.57.refs_0_), channel_id=1, source_target_pairs={{0,8},{4,12},{8,0},{12,4},{16,24},{20,28},{24,16},{28,20},{1,9},{5... | collective-permute-start | bytes 589832 | tf_op jit(solution)/shard_map/ppermute | solution.py:449
  9.3 5.5 %collective-permute-start = (s32[1,4]{1,0:T(1,128)}, s32[1,4]{1,0:T(1,128)S(1)}, u32[]{:S(2)}, u32[]{:S(2)}) collective-permute-start(s32[1,4]{1,0:T(1,128)} %want_ref.5), channel_id=1, source_target_pairs={{0,4},{4,0},{8,12},{12,8},{16,20},{20,16},{24,28},{28,24},{1,5},{5... | collective-permute-start | bytes 56 | tf_op jit(solution)/shard_map/ppermute | solution.py:449
  14.8 16.1 %collective-permute-start.7 = (bf16[512,512]{1,0:T(8,128)(2,1)}, bf16[512,512]{1,0:T(8,128)(2,1)S(1)}, u32[]{:S(2)}, u32[]{:S(2)}) collective-permute-start(bf16[512,512]{1,0:T(8,128)(2,1)} %own.5), channel_id=1, source_target_pairs={{0,1},{1,0},{2,3},{3,2},{4,5},{5,4},{6,7},{7,6},{8,9},{9,8},{10,11... | collective-permute-start | bytes 1572872 | tf_op jit(solution)/shard_map/ppermute | solution.py:437
  15.1 18.5 %collective-permute-start.9 = (bf16[512,512]{1,0:T(8,128)(2,1)S(1)}, bf16[512,512]{1,0:T(8,128)(2,1)}, u32[]{:S(2)}, u32[]{:S(2)}) collective-permute-start(bf16[512,512]{1,0:T(8,128)(2,1)S(1)} %collective-permute-done.8.across), channel_id=1, source_target_pairs={{0,1},{1,0},{2,3},{3,2},{4,5},{5,4},{6,7},{7,6},{8,9},{9,8},{10,11... | collective-permute-start | bytes 1572872 | tf_op jit(solution)/shard_map/ppermute | solution.py:437
  26.8 14.6 %collective-permute-start.10 = (bf16[4,96,512]{2,1,0:T(8,128)(2,1)S(1)}, bf16[4,96,512]{2,1,0:T(8,128)(2,1)}, u32[]{:S(2)}, u32[]{:S(2)}) collective-permute-start(bf16[4,96,512]{2,1,0:T(8,128)(2,1)S(1)} %shard_map.236.after), channel_id=1, source_target_pairs={{0,4},{4,0},{8,12},{12,8},{16,20},{20,16},{24,28},{28,24},{1,5},{5... | collective-permute-start | bytes 1179656 | tf_op jit(solution)/shard_map/ppermute | solution.py:449
  28.4 24.1 %collective-permute-start.6 = (bf16[2,272,256]{2,1,0:T(8,128)(2,1)S(1)}, bf16[2,272,256]{2,1,0:T(8,128)(2,1)S(1)}, u32[]{:S(2)}, u32[]{:S(2)}) collective-permute-start(bf16[2,272,256]{2,1,0:T(8,128)(2,1)S(1)} %shard_map.237.refs_0_), channel_id=1, source_target_pairs={{0,24},{4,28},{8,16},{12,20},{16,8},{20,12},{24,0},{28,4},{1,25},{... | collective-permute-start | bytes 835592 | tf_op jit(solution)/shard_map/ppermute | solution.py:449
  30.9 21.8 %collective-permute-start.5 = (bf16[2,272,256]{2,1,0:T(8,128)(2,1)S(1)}, bf16[2,272,256]{2,1,0:T(8,128)(2,1)S(1)}, u32[]{:S(2)}, u32[]{:S(2)}) collective-permute-start(bf16[2,272,256]{2,1,0:T(8,128)(2,1)S(1)} %shard_map.237.refs_0_), channel_id=1, source_target_pairs={{0,16},{4,20},{8,24},{12,28},{16,0},{20,4},{24,8},{28,12},{1,17},{... | collective-permute-start | bytes 835592 | tf_op jit(solution)/shard_map/ppermute | solution.py:449
  31.7 21.3 %collective-permute-start.4 = (bf16[2,272,256]{2,1,0:T(8,128)(2,1)S(1)}, bf16[2,272,256]{2,1,0:T(8,128)(2,1)S(1)}, u32[]{:S(2)}, u32[]{:S(2)}) collective-permute-start(bf16[2,272,256]{2,1,0:T(8,128)(2,1)S(1)} %shard_map.237.refs_0_), channel_id=1, source_target_pairs={{0,8},{4,12},{8,0},{12,4},{16,24},{20,28},{24,16},{28,20},{1,9},{5... | collective-permute-start | bytes 835592 | tf_op jit(solution)/shard_map/ppermute | solution.py:449
  43.2 3.6 %collective-permute-start.13 = (bf16[48,512]{1,0:T(8,128)(2,1)S(1)}, bf16[48,512]{1,0:T(8,128)(2,1)S(1)}, u32[]{:S(2)}, u32[]{:S(2)}) collective-permute-start(bf16[48,512]{1,0:T(8,128)(2,1)S(1)} %get-tuple-element.60.low0.after), channel_id=1, source_target_pairs={{0,3},{1,2},{2,1},{3,0},{4,7},{5,6},{6,5},{7,4},{8,11},{9,10},{10,... | collective-permute-start | bytes 147464 | tf_op jit(solution)/shard_map/ppermute | solution.py:445
  43.2 4.6 %collective-permute-start.12 = (bf16[48,512]{1,0:T(8,128)(2,1)S(1)}, bf16[48,512]{1,0:T(8,128)(2,1)S(1)}, u32[]{:S(2)}, u32[]{:S(2)}) collective-permute-start(bf16[48,512]{1,0:T(8,128)(2,1)S(1)} %get-tuple-element.60.low0.after), channel_id=1, source_target_pairs={{0,2},{1,3},{2,0},{3,1},{4,6},{5,7},{6,4},{7,5},{8,10},{9,11},{10,... | collective-permute-start | bytes 147464 | tf_op jit(solution)/shard_map/ppermute | solution.py:441
  51.9 2.1 %collective-permute-start.17 = (bf16[144,512]{1,0:T(8,128)(2,1)S(1)}, bf16[144,512]{1,0:T(8,128)(2,1)S(1)}, u32[]{:S(2)}, u32[]{:S(2)}) collective-permute-start(bf16[144,512]{1,0:T(8,128)(2,1)S(1)} %get-tuple-element.68), channel_id=1, source_target_pairs={{0,1},{1,0},{2,3},{3,2},{4,5},{5,4},{6,7},{7,6},{8,9},{9,8},{10,11... | collective-permute-start | bytes 442376 | tf_op jit(solution)/shard_map/ppermute | solution.py:437
  54.2 19.1 %collective-permute-start.20 = (bf16[272,1024]{1,0:T(8,128)(2,1)S(1)}, bf16[272,1024]{1,0:T(8,128)(2,1)S(1)}, u32[]{:S(2)}, u32[]{:S(2)}) collective-permute-start(bf16[272,1024]{1,0:T(8,128)(2,1)S(1)} %shard_map.242.refs_5_.chip.after), channel_id=1, source_target_pairs={{0,2},{1,3},{2,0},{3,1},{4,6},{5,7},{6,4},{7,5},{8,10},{9,11},{10,... | collective-permute-start | bytes 1671176 | tf_op jit(solution)/shard_map/ppermute | solution.py:441
  55.3 6.9 %collective-permute-start.15 = (bf16[4,96,256]{2,1,0:T(8,128)(2,1)S(1)}, bf16[4,96,256]{2,1,0:T(8,128)(2,1)S(1)}, u32[]{:S(2)}, u32[]{:S(2)}) collective-permute-start(bf16[4,96,256]{2,1,0:T(8,128)(2,1)S(1)} %get-tuple-element.65.refs_4_), channel_id=1, source_target_pairs={{0,4},{4,0},{8,12},{12,8},{16,20},{20,16},{24,28},{28,24},{1,5},{5... | collective-permute-start | bytes 589832 | tf_op jit(solution)/shard_map/ppermute | solution.py:449
  59.9 4.3 %collective-permute-start.33 = (bf16[128,512]{1,0:T(8,128)(2,1)S(1)}, bf16[128,512]{1,0:T(8,128)(2,1)S(1)}, u32[]{:S(2)}, u32[]{:S(2)}) collective-permute-start(bf16[128,512]{1,0:T(8,128)(2,1)S(1)} %get-tuple-element.92), channel_id=1, source_target_pairs={{0,1},{1,0},{2,3},{3,2},{4,5},{5,4},{6,7},{7,6},{8,9},{9,8},{10,11... | collective-permute-start | bytes 393224 | tf_op jit(solution)/shard_map/ppermute | solution.py:437
  59.9 4.8 %collective-permute-start.35 = (bf16[128,512]{1,0:T(8,128)(2,1)S(1)}, bf16[128,512]{1,0:T(8,128)(2,1)S(1)}, u32[]{:S(2)}, u32[]{:S(2)}) collective-permute-start(bf16[128,512]{1,0:T(8,128)(2,1)S(1)} %get-tuple-element.94), channel_id=1, source_target_pairs={{0,1},{1,0},{2,3},{3,2},{4,5},{5,4},{6,7},{7,6},{8,9},{9,8},{10,11... | collective-permute-start | bytes 393224 | tf_op jit(solution)/shard_map/ppermute | solution.py:437
  63.1 10.2 %collective-permute-start.21 = (bf16[192,512]{1,0:T(8,128)(2,1)S(1)}, bf16[192,512]{1,0:T(8,128)(2,1)S(1)}, u32[]{:S(2)}, u32[]{:S(2)}) collective-permute-start(bf16[192,512]{1,0:T(8,128)(2,1)S(1)} %shard_map.243.refs_5_.refs_3_.table.table0), channel_id=1, source_target_pairs={{0,2},{1,3},{2,0},{3,1},{4,6},{5,7},{6,4},{7,5},{8,10},{9,11},{10,... | collective-permute-start | bytes 589832 | tf_op jit(solution)/shard_map/ppermute | solution.py:441
  64.2 4.8 %collective-permute-start.34 = (bf16[144,512]{1,0:T(8,128)(2,1)S(1)}, bf16[144,512]{1,0:T(8,128)(2,1)S(1)}, u32[]{:S(2)}, u32[]{:S(2)}) collective-permute-start(bf16[144,512]{1,0:T(8,128)(2,1)S(1)} %get-tuple-element.93), channel_id=1, source_target_pairs={{0,1},{1,0},{2,3},{3,2},{4,5},{5,4},{6,7},{7,6},{8,9},{9,8},{10,11... | collective-permute-start | bytes 442376 | tf_op jit(solution)/shard_map/ppermute | solution.py:437
  64.2 4.8 %collective-permute-start.36 = (bf16[128,512]{1,0:T(8,128)(2,1)S(1)}, bf16[128,512]{1,0:T(8,128)(2,1)S(1)}, u32[]{:S(2)}, u32[]{:S(2)}) collective-permute-start(bf16[128,512]{1,0:T(8,128)(2,1)S(1)} %get-tuple-element.95), channel_id=1, source_target_pairs={{0,1},{1,0},{2,3},{3,2},{4,5},{5,4},{6,7},{7,6},{8,9},{9,8},{10,11... | collective-permute-start | bytes 393224 | tf_op jit(solution)/shard_map/ppermute | solution.py:437
  64.7 11.4 %collective-permute-start.14 = (bf16[4,176,256]{2,1,0:T(8,128)(2,1)S(1)}, bf16[4,176,256]{2,1,0:T(8,128)(2,1)S(1)}, u32[]{:S(2)}, u32[]{:S(2)}) collective-permute-start(bf16[4,176,256]{2,1,0:T(8,128)(2,1)S(1)} %get-tuple-element.64), channel_id=1, source_target_pairs={{0,4},{4,0},{8,12},{12,8},{16,20},{20,16},{24,28},{28,24},{1,5},{5... | collective-permute-start | bytes 1081352 | tf_op jit(solution)/shard_map/ppermute | solution.py:449
  73.4 14.1 %collective-permute-start.37 = (bf16[272,1024]{1,0:T(8,128)(2,1)S(1)}, bf16[272,1024]{1,0:T(8,128)(2,1)S(1)}, u32[]{:S(2)}, u32[]{:S(2)}) collective-permute-start(bf16[272,1024]{1,0:T(8,128)(2,1)S(1)} %shard_map.250.chip), channel_id=1, source_target_pairs={{0,2},{1,3},{2,0},{3,1},{4,6},{5,7},{6,4},{7,5},{8,10},{9,11},{10,... | collective-permute-start | bytes 1671176 | tf_op jit(solution)/shard_map/ppermute | solution.py:441
  74.5 2.1 %collective-permute-start.26 = (bf16[192,512]{1,0:T(8,128)(2,1)S(1)}, bf16[192,512]{1,0:T(8,128)(2,1)S(1)}, u32[]{:S(2)}, u32[]{:S(2)}) collective-permute-start(bf16[192,512]{1,0:T(8,128)(2,1)S(1)} %shard_map.243.refs_5_.refs_3_.table.table0), channel_id=1, source_target_pairs={{0,1},{1,0},{2,3},{3,2},{4,5},{5,4},{6,7},{7,6},{8,9},{9,8},{10,11... | collective-permute-start | bytes 589832 | tf_op jit(solution)/shard_map/ppermute | solution.py:437
  74.5 2.1 %collective-permute-start.27 = (bf16[192,512]{1,0:T(8,128)(2,1)S(1)}, bf16[192,512]{1,0:T(8,128)(2,1)S(1)}, u32[]{:S(2)}, u32[]{:S(2)}) collective-permute-start(bf16[192,512]{1,0:T(8,128)(2,1)S(1)} %collective-permute-done.21.table_across.table2.refs_5_), channel_id=1, source_target_pairs={{0,1},{1,0},{2,3},{3,2},{4,5},{5,4},{6,7},{7,6},{8,9},{9,8},{10,11... | collective-permute-start | bytes 589832 | tf_op jit(solution)/shard_map/ppermute | solution.py:437
  76.0 1.9 %collective-permute-start.24 = (bf16[128,512]{1,0:T(8,128)(2,1)S(1)}, bf16[128,512]{1,0:T(8,128)(2,1)S(1)}, u32[]{:S(2)}, u32[]{:S(2)}) collective-permute-start(bf16[128,512]{1,0:T(8,128)(2,1)S(1)} %get-tuple-element.75.right0), channel_id=1, source_target_pairs={{0,1},{1,0},{2,3},{3,2},{4,5},{5,4},{6,7},{7,6},{8,9},{9,8},{10,11... | collective-permute-start | bytes 393224 | tf_op jit(solution)/shard_map/ppermute | solution.py:437
  76.1 1.9 %collective-permute-start.25 = (bf16[128,512]{1,0:T(8,128)(2,1)S(1)}, bf16[128,512]{1,0:T(8,128)(2,1)S(1)}, u32[]{:S(2)}, u32[]{:S(2)}) collective-permute-start(bf16[128,512]{1,0:T(8,128)(2,1)S(1)} %get-tuple-element.76.right1), channel_id=1, source_target_pairs={{0,1},{1,0},{2,3},{3,2},{4,5},{5,4},{6,7},{7,6},{8,9},{9,8},{10,11... | collective-permute-start | bytes 393224 | tf_op jit(solution)/shard_map/ppermute | solution.py:437
  83.6 2.3 %collective-permute-start.29 = (bf16[144,512]{1,0:T(8,128)(2,1)S(1)}, bf16[144,512]{1,0:T(8,128)(2,1)S(1)}, u32[]{:S(2)}, u32[]{:S(2)}) collective-permute-start(bf16[144,512]{1,0:T(8,128)(2,1)S(1)} %get-tuple-element.84), channel_id=1, source_target_pairs={{0,1},{1,0},{2,3},{3,2},{4,5},{5,4},{6,7},{7,6},{8,9},{9,8},{10,11... | collective-permute-start | bytes 442376 | tf_op jit(solution)/shard_map/ppermute | solution.py:437
  85.9 11.2 %collective-permute-start.32 = (bf16[272,512]{1,0:T(8,128)(2,1)S(1)}, bf16[272,512]{1,0:T(8,128)(2,1)S(1)}, u32[]{:S(2)}, u32[]{:S(2)}) collective-permute-start(bf16[272,512]{1,0:T(8,128)(2,1)S(1)} %get-tuple-element.88), channel_id=1, source_target_pairs={{0,2},{1,3},{2,0},{3,1},{4,6},{5,7},{6,4},{7,5},{8,10},{9,11},{10,... | collective-permute-start | bytes 835592 | tf_op jit(solution)/shard_map/ppermute | solution.py:441
  88.6 1.5 %collective-permute-start.41 = (bf16[128,512]{1,0:T(8,128)(2,1)S(1)}, bf16[128,512]{1,0:T(8,128)(2,1)S(1)}, u32[]{:S(2)}, u32[]{:S(2)}) collective-permute-start(bf16[128,512]{1,0:T(8,128)(2,1)S(1)} %get-tuple-element.99.right1), channel_id=1, source_target_pairs={{0,1},{1,0},{2,3},{3,2},{4,5},{5,4},{6,7},{7,6},{8,9},{9,8},{10,11... | collective-permute-start | bytes 393224 | tf_op jit(solution)/shard_map/ppermute | solution.py:437
  96.1 2.2 %collective-permute-start.43 = (bf16[144,512]{1,0:T(8,128)(2,1)S(1)}, bf16[144,512]{1,0:T(8,128)(2,1)S(1)}, u32[]{:S(2)}, u32[]{:S(2)}) collective-permute-start(bf16[144,512]{1,0:T(8,128)(2,1)S(1)} %get-tuple-element.102), channel_id=1, source_target_pairs={{0,1},{1,0},{2,3},{3,2},{4,5},{5,4},{6,7},{7,6},{8,9},{9,8},{10,11... | collective-permute-start | bytes 442376 | tf_op jit(solution)/shard_map/ppermute | solution.py:437
  98.5 8.8 %collective-permute-start.46 = (bf16[272,512]{1,0:T(8,128)(2,1)S(1)}, bf16[272,512]{1,0:T(8,128)(2,1)S(1)}, u32[]{:S(2)}, u32[]{:S(2)}) collective-permute-start(bf16[272,512]{1,0:T(8,128)(2,1)S(1)} %get-tuple-element.106), channel_id=1, source_target_pairs={{0,2},{1,3},{2,0},{3,1},{4,6},{5,7},{6,4},{7,5},{8,10},{9,11},{10,... | collective-permute-start | bytes 835592 | tf_op jit(solution)/shard_map/ppermute | solution.py:441
  (31 other events, 170.5 us)

commit v5 on v4

--- a/solution.py
+++ b/solution.py
@@ -552,12 +552,13 @@
             pltpu.VMEM(value_weight.shape, bf16),
             pltpu.SemaphoreType.DMA((13,)),
         ],
-        limit=50,
+        limit=49,
     )(
         index, tokens, core, across, diagonal, gain_one, query_weight, key_weight, value_weight,
         output_weight,
     )
     everyone = [block] + [swap_req(block, 2 * rel) for rel in range(1, peers)]
+    everyone[0] = call(hold, [VMEM, ANY], shaped(block.shape, bf16))(block, sine)
     (passing,) = for_neighbour(everyone, sine, [low_qkv + 3 * rank])
     block_second = call(hold, [VMEM, ANY], shaped(block_second.shape, bf16))(block_second, passing)
     second = [block_second] + [swap_req(block_second, 2 * rel) for rel in range(1, peers)]

time: 109 us -> 108 us (level)
  local copies, waits for them, and re-layouts: 4.31 us -> 2.41 us
  waiting for transfers between devices: 30.6 us -> 31.8 us
    unnamed x32 -> x28, local copies, waits for them, and re-layouts: 2.89 us -> 0.99 us
  transfers between devices with their start and end apart: 47 -> 47, of which waited for: 22 -> 22; matrix products, arithmetic and copies ran while one was open for 3% -> 4% of each run, Pallas kernels for 35% -> 35%
where the time goes in v5:
time: 108 us; the launch traced here: 107 us
  Pallas kernels  40 us (37%)
  waiting for transfers between devices  31.8 us (29%)
  starting transfers between devices  28.5 us (26%)
  local copies, waits for them, and re-layouts  2.41 us (2%)
  other arithmetic  2.36 us (2%)
  between operations  2.32 us (2%)
    ppermute x7, waiting for transfers between devices, swap_across(): return lax.ppermute(values, 'tp', [(k, k ^ 2) for k in range(4)])  14.1 us
    ppermute x10, starting transfers between devices, swap_req(): lax.ppermute(values, 'req', [(k, k ^ flips) for k in range(lax.axis_size(...  13 us
    pallas_call x2, Pallas kernels, per_device(): call(functools.partial(feed_forward, c), [SMEM] * 2 + [VMEM] * 19, terms,...  10.9 us
    ppermute x10, waiting for transfers between devices, swap_req(): lax.ppermute(values, 'req', [(k, k ^ flips) for k in range(lax.axis_size(...  10.4 us
    ppermute x7, starting transfers between devices, swap_across(): return lax.ppermute(values, 'tp', [(k, k ^ 2) for k in range(4)])  8.44 us
    pallas_call x2, Pallas kernels, per_device(): call(functools.partial(attend, c, heads, kv_heads), [SMEM] * 2 + [VMEM] *...  8.09 us
    ppermute x29, starting transfers between devices, swap_core(): return lax.ppermute(values, 'tp', [(k, k ^ 1) for k in range(4)])  6.96 us
    pallas_call x1, Pallas kernels, per_device(): call(project_qkv, [SMEM] + [VMEM] * 5 + [HBM] * 4, [shaped((row_count, wi...  6.45 us
  transfers between devices with their start and end apart: 47, of which 22 were waited for; matrix products, arithmetic and copies ran while one was open for 4% of the time, Pallas kernels for 35%

profile of v5, /device:TPU:0, one launch (start us, length us, event | category | flops | bytes accessed | tf_op | source)
XLA Modules:
  0.0 107.4 jit_solution(13954015926468823094)
XLA Ops:
  0.0 2.9 %collective-permute-start.8 = (bf16[512,512]{1,0:T(8,128)(2,1)}, bf16[512,512]{1,0:T(8,128)(2,1)S(1)}, u32[]{:S(2)}, u32[]{:S(2)}) collective-permute-start(bf16[512,512]{1,0:T(8,128)(2,1)} %own.5), channel_id=1, source_target_pairs={{0,2},{1,3},{2,0},{3,1},{4,6},{5,7},{6,4},{7,5},{8,10},{9,11},{10,... | collective-permute-start | bytes 1572872 | tf_op jit(solution)/shard_map/ppermute | solution.py:441
  2.9 1.9 %shard_map.235 = (bf16[2,96,512]{2,1,0:T(8,128)(2,1)}, bf16[2,272,256]{2,1,0:T(8,128)(2,1)}) custom-call(bf16[2,48,512]{2,1,0:T(8,128)(2,1)} %refs_0_.2, bf16[2,16,512]{2,1,0:T(8,128)(2,1)} %refs_1_.2, bf16[2,16,256]{2,1,0:T(8,128)(2,1)} %refs_2_.2, bf16[2,16,256]{2,1,0:T(8,128)(2,1)} %refs_3_.1, bf16[2,16,512]{2,1,0:T(8,128)(2,1)} %refs_4_.1, ...), custom_call_target="tpu_custom_call" | custom-call | flops 1 | bytes 1 | tf_op jit(solution)/shard_map/pallas_call | solution.py:534
  4.9 3.7 %collective-permute-start.3 = (bf16[2,96,512]{2,1,0:T(8,128)(2,1)}, bf16[2,96,512]{2,1,0:T(8,128)(2,1)S(1)}, u32[]{:S(2)}, u32[]{:S(2)}) collective-permute-start(bf16[2,96,512]{2,1,0:T(8,128)(2,1)} %get-tuple-element.57.block), channel_id=1, source_target_pairs={{0,24},{4,28},{8,16},{12,20},{16,8},{20,12},{24,0},{28,4},{1,25},{... | collective-permute-start | bytes 589832 | tf_op jit(solution)/shard_map/ppermute | solution.py:449
  8.5 0.8 collective-permute-start.1
  9.3 1.5 %collective-permute-start = (s32[1,4]{1,0:T(1,128)}, s32[1,4]{1,0:T(1,128)S(1)}, u32[]{:S(2)}, u32[]{:S(2)}) collective-permute-start(s32[1,4]{1,0:T(1,128)} %want_ref.5), channel_id=1, source_target_pairs={{0,4},{4,0},{8,12},{12,8},{16,20},{20,16},{24,28},{28,24},{1,5},{5... | collective-permute-start | bytes 56 | tf_op jit(solution)/shard_map/ppermute | solution.py:449
  10.8 1.4 %fusion.1 = (s32[1,1]{1,0:T(1,128)}, s32[1,1]{1,0:T(1,128)}, s32[1,1]{1,0:T(1,128)}) fusion(s32[1,4]{1,0:T(1,128)} %lens_ref.15), kind=kLoop, calls=%fused_computation.9 | loop fusion | bytes 24 | tf_op jit(solution)/shard_map/slice | solution.py:430
  15.5 1.6 %multiply_cosine_fusion = (f32[512,128]{1,0:T(8,128)S(1)}, f32[512,128]{1,0:T(8,128)S(1)}) fusion(f32[128]{0:T(128)S(1)} %pad_maximum_fusion, f32[512]{0:T(512)S(1)} %subtract_convert_fusion, f32[128]{0:T(128)} %constant.22.clone.1), kind=kLoop, calls=%fused_computation | loop fusion | flops 131072 | bytes 527360 | tf_op jit(solution)/shard_map/cos | solution.py:433
  17.1 0.9 copy-done.7
  18.1 7.1 %collective-permute-done.2.refs_2_ = bf16[2,96,512]{2,1,0:T(8,128)(2,1)S(1)} collective-permute-done((bf16[2,96,512]{2,1,0:T(8,128)(2,1)}, bf16[2,96,512]{2,1,0:T(8,128)(2,1)S(1)}, u32[]{:S(2)}, u32[]{:S(2)}) %collective-permute-start.2) | collective-permute-done | bytes 196640 | tf_op jit(solution)/shard_map/ppermute | solution.py:449
  25.8 1.6 %collective-permute-start.10 = (bf16[4,96,512]{2,1,0:T(8,128)(2,1)S(1)}, bf16[4,96,512]{2,1,0:T(8,128)(2,1)}, u32[]{:S(2)}, u32[]{:S(2)}) collective-permute-start(bf16[4,96,512]{2,1,0:T(8,128)(2,1)S(1)} %shard_map.237.after), channel_id=1, source_target_pairs={{0,4},{4,0},{8,12},{12,8},{16,20},{20,16},{24,28},{28,24},{1,5},{5... | collective-permute-start | bytes 1179656 | tf_op jit(solution)/shard_map/ppermute | solution.py:449
  27.4 2.5 %collective-permute-start.6 = (bf16[2,272,256]{2,1,0:T(8,128)(2,1)S(1)}, bf16[2,272,256]{2,1,0:T(8,128)(2,1)S(1)}, u32[]{:S(2)}, u32[]{:S(2)}) collective-permute-start(bf16[2,272,256]{2,1,0:T(8,128)(2,1)S(1)} %shard_map.238.refs_0_), channel_id=1, source_target_pairs={{0,24},{4,28},{8,16},{12,20},{16,8},{20,12},{24,0},{28,4},{1,25},{... | collective-permute-start | bytes 835592 | tf_op jit(solution)/shard_map/ppermute | solution.py:449
  29.9 1.9 %collective-permute-start.4 = (bf16[2,272,256]{2,1,0:T(8,128)(2,1)S(1)}, bf16[2,272,256]{2,1,0:T(8,128)(2,1)S(1)}, u32[]{:S(2)}, u32[]{:S(2)}) collective-permute-start(bf16[2,272,256]{2,1,0:T(8,128)(2,1)S(1)} %shard_map.238.refs_0_), channel_id=1, source_target_pairs={{0,8},{4,12},{8,0},{12,4},{16,24},{20,28},{24,16},{28,20},{1,9},{5... | collective-permute-start | bytes 835592 | tf_op jit(solution)/shard_map/ppermute | solution.py:449
  31.9 6.4 %shard_map.239 = (bf16[512,512]{1,0:T(8,128)(2,1)S(1)}, bf16[512,2048]{1,0:T(8,128)(2,1)}, f32[256,1024]{1,0:T(8,128)S(1)}, f32[256,1024]{1,0:T(8,128)S(1)}) custom-call(s32[1]{0:T(128)} %bitcast.4.index_ref, bf16[512,512]{1,0:T(8,128)(2,1)S(1)} %copy-done.1, bf16[512,512]{1,0:T(8,128)(2,1)} %collective-permute-done.7.core, ...), custom_call_target="tpu_custom_call" | custom-call | flops 1 | bytes 1 | tf_op jit(solution)/shard_map/pallas_call | solution.py:546
  38.4 1.8 %shard_map.240 = (bf16[48,512]{1,0:T(8,128)(2,1)S(1)}, bf16[4,48,512]{2,1,0:T(8,128)(2,1)S(1)}) custom-call(s32[1]{0:T(128)} %bitcast.me_ref, s32[1,4]{1,0:T(1,128)S(1)} %copy-done.11, s32[1,4]{1,0:T(1,128)S(1)} %copy-done.8, bf16[2,96,512]{2,1,0:T(8,128)(2,1)S(1)} %shard_map.236.refs_0_, bf16[2,96,512]{2,1,0:T(8,128)(2,1)S(1)} %copy-done.5, ...), custom_call_target="tpu_custom_call" | custom-call | flops 1 | bytes 1 | tf_op jit(solution)/shard_map/pallas_call | solution.py:565
  40.9 2.9 %collective-permute-done.13.low3 = bf16[48,512]{1,0:T(8,128)(2,1)S(1)} collective-permute-done((bf16[48,512]{1,0:T(8,128)(2,1)S(1)}, bf16[48,512]{1,0:T(8,128)(2,1)S(1)}, u32[]{:S(2)}, u32[]{:S(2)}) %collective-permute-start.13) | collective-permute-done | bytes 49184 | tf_op jit(solution)/shard_map/ppermute | solution.py:445
  43.8 1.0 collective-permute-done.12.low2
  45.0 4.0 %shard_map.241 = (bf16[256,256]{1,0:T(8,128)(2,1)S(1)}, bf16[256,256]{1,0:T(8,128)(2,1)S(1)}, f32[272,1024]{1,0:T(8,128)S(1)}, bf16[128,512]{1,0:T(8,128)(2,1)S(...) custom-call(s32[1]{0:T(128)} %bitcast.4.index_ref, ...), custom_call_target="tpu_custom_call" | custom-call | flops 1 | bytes 1 | tf_op jit(solution)/shard_map/pallas_call | solution.py:585
  49.7 1.8 %collective-permute-done.5.refs_2_ = bf16[2,272,256]{2,1,0:T(8,128)(2,1)S(1)} collective-permute-done((bf16[2,272,256]{2,1,0:T(8,128)(2,1)S(1)}, bf16[2,272,256]{2,1,0:T(8,128)(2,1)S(1)}, u32[]{:S(2)}, u32[]{:S(2)}) %collective-permute-start.5) | collective-permute-done | bytes 278560 | tf_op jit(solution)/shard_map/ppermute | solution.py:449
  54.0 4.1 %shard_map.250 = (bf16[256,256]{1,0:T(8,128)(2,1)}, bf16[256,256]{1,0:T(8,128)(2,1)}, f32[272,1024]{1,0:T(8,128)S(1)}, bf16[128,512]{1,0:T(8,128)(2,1)S(1)}, bf1...) custom-call(s32[1]{0:T(128)} %bitcast.4.index_ref, s32[1,4]{1,0:T(1,128)S(1)} %copy-done.8, ...), custom_call_target="tpu_custom_call" | custom-call | flops 1 | bytes 1 | tf_op jit(solution)/shard_map/pallas_call | solution.py:585
  58.7 1.5 %collective-permute-done.15.refs_4_ = bf16[4,96,256]{2,1,0:T(8,128)(2,1)S(1)} collective-permute-done((bf16[4,96,256]{2,1,0:T(8,128)(2,1)S(1)}, bf16[4,96,256]{2,1,0:T(8,128)(2,1)S(1)}, u32[]{:S(2)}, u32[]{:S(2)}) %collective-permute-start.15) | collective-permute-done | bytes 196640 | tf_op jit(solution)/shard_map/ppermute | solution.py:449
  60.2 1.0 shard_map.244.refs_5_.refs_3_.table.table0
  61.2 1.6 %collective-permute-start.21 = (bf16[192,512]{1,0:T(8,128)(2,1)S(1)}, bf16[192,512]{1,0:T(8,128)(2,1)S(1)}, u32[]{:S(2)}, u32[]{:S(2)}) collective-permute-start(bf16[192,512]{1,0:T(8,128)(2,1)S(1)} %shard_map.244.refs_5_.refs_3_.table.table0), channel_id=1, source_target_pairs={{0,2},{1,3},{2,0},{3,1},{4,6},{5,7},{6,4},{7,5},{8,10},{9,11},{10,... | collective-permute-start | bytes 589832 | tf_op jit(solution)/shard_map/ppermute | solution.py:441
  63.8 3.8 %shard_map.246 = (bf16[2048,768]{1,0:T(8,128)(2,1)S(1)}, bf16[2048,768]{1,0:T(8,128)(2,1)S(1)}, bf16[768,2048]{1,0:T(8,128)(2,1)S(1)}) custom-call(bf16[2048,768]{1,0:T(8,128)(2,1)} %refs_0_.3, bf16[2048,768]{1,0:T(8,128)(2,1)} %refs_1_.3, bf16[768,2048]{1,0:T(8,128)(2,1)} %refs_2_.3, bf16[192,512]{1,0:T(8,128)(2,1)S(1)} %shard_map.244.refs_5_.refs_3_.table.table0), custom_call_target="tpu_custom_call" | custom-call | flops 1 | bytes 1 | tf_op jit(solution)/shard_map/pallas_call | solution.py:510
  67.6 4.3 %collective-permute-done.21.table_across.table2.refs_5_ = bf16[192,512]{1,0:T(8,128)(2,1)S(1)} collective-permute-done((bf16[192,512]{1,0:T(8,128)(2,1)S(1)}, bf16[192,512]{1,0:T(8,128)(2,1)S(1)}, u32[]{:S(2)}, u32[]{:S(2)}) %collective-permute-start.21) | collective-permute-done | bytes 196640 | tf_op jit(solution)/shard_map/ppermute | solution.py:441
  73.1 1.0 shard_map.247
  75.2 0.8 shard_map.245
  76.2 5.5 %shard_map.248 = (f32[272,1024]{1,0:T(8,128)S(1)}, bf16[128,512]{1,0:T(8,128)(2,1)S(1)}, bf16[144,512]{1,0:T(8,128)(2,1)S(1)}, bf16[128,512]{1,0:T(8,128)(2,1)S(1)}, bf16[128,512]{1,0:T(8,128)(2,1)S(1)}) custom-call(s32[1]{0:T(128)} %bitcast.4.index_ref, s32[1,4]{1,0:T(1,128)S(1)} %copy-done.8, bf16[128,512]{1,0:T(8,128)(2,1)S(1)} %get-tuple-element.73.left0.refs_2_, ...), custom_call_target="tpu_custom_call" | custom-call | flops 1 | bytes 1 | tf_op jit(solution)/shard_map/pallas_call | solution.py:638
  84.1 1.5 %collective-permute-start.32 = (bf16[272,512]{1,0:T(8,128)(2,1)S(1)}, bf16[272,512]{1,0:T(8,128)(2,1)S(1)}, u32[]{:S(2)}, u32[]{:S(2)}) collective-permute-start(bf16[272,512]{1,0:T(8,128)(2,1)S(1)} %get-tuple-element.88), channel_id=1, source_target_pairs={{0,2},{1,3},{2,0},{3,1},{4,6},{5,7},{6,4},{7,5},{8,10},{9,11},{10,... | collective-permute-start | bytes 835592 | tf_op jit(solution)/shard_map/ppermute | solution.py:441
  85.9 0.9 shard_map.252
  89.0 5.5 %shard_map.253 = (f32[272,1024]{1,0:T(8,128)S(1)}, bf16[128,512]{1,0:T(8,128)(2,1)S(1)}, bf16[144,512]{1,0:T(8,128)(2,1)S(1)}, bf16[128,512]{1,0:T(8,128)(2,1)S(1)}, bf16[128,512]{1,0:T(8,128)(2,1)S(1)}) custom-call(s32[1]{0:T(128)} %bitcast.4.index_ref, s32[1,4]{1,0:T(1,128)S(1)} %copy-done.8, bf16[128,512]{1,0:T(8,128)(2,1)S(1)} %get-tuple-element.96.left0.refs_6_, ...), custom_call_target="tpu_custom_call" | custom-call | flops 1 | bytes 1 | tf_op jit(solution)/shard_map/pallas_call | solution.py:638
  97.4 8.2 %collective-permute-done.46.refs_5_ = bf16[272,512]{1,0:T(8,128)(2,1)S(1)} collective-permute-done((bf16[272,512]{1,0:T(8,128)(2,1)S(1)}, bf16[272,512]{1,0:T(8,128)(2,1)S(1)}, u32[]{:S(2)}, u32[]{:S(2)}) %collective-permute-start.46) | collective-permute-done | bytes 278560 | tf_op jit(solution)/shard_map/ppermute | solution.py:441
  105.7 1.7 %shard_map.255 = bf16[512,512]{1,0:T(8,128)(2,1)} custom-call(s32[1,4]{1,0:T(1,128)S(1)} %copy-done.8, bf16[64,512]{1,0:T(8,128)(2,1)S(1)} %get-tuple-element.71.table, f32[272,512]{1,0:T(8,128)S(1)} %get-tuple-element.87.refs_0_, bf16[272,512]{1,0:T(8,128)(2,1)S(1)} %collective-permute-done.32.refs_4_.refs_1_, ...), custom_call_target="tpu_custom_call" | custom-call | flops 1 | bytes 1 | tf_op jit(solution)/shard_map/pallas_call | solution.py:658
  (117 shorter events, 17.8 us)
Async XLA Ops:
  0.0 15.1 %collective-permute-start.8 = (bf16[512,512]{1,0:T(8,128)(2,1)}, bf16[512,512]{1,0:T(8,128)(2,1)S(1)}, u32[]{:S(2)}, u32[]{:S(2)}) collective-permute-start(bf16[512,512]{1,0:T(8,128)(2,1)} %own.5), channel_id=1, source_target_pairs={{0,2},{1,3},{2,0},{3,1},{4,6},{5,7},{6,4},{7,5},{8,10},{9,11},{10,... | collective-permute-start | bytes 1572872 | tf_op jit(solution)/shard_map/ppermute | solution.py:441
  4.9 13.2 %collective-permute-start.3 = (bf16[2,96,512]{2,1,0:T(8,128)(2,1)}, bf16[2,96,512]{2,1,0:T(8,128)(2,1)S(1)}, u32[]{:S(2)}, u32[]{:S(2)}) collective-permute-start(bf16[2,96,512]{2,1,0:T(8,128)(2,1)} %get-tuple-element.57.block), channel_id=1, source_target_pairs={{0,24},{4,28},{8,16},{12,20},{16,8},{20,12},{24,0},{28,4},{1,25},{... | collective-permute-start | bytes 589832 | tf_op jit(solution)/shard_map/ppermute | solution.py:449
  8.5 16.6 %collective-permute-start.2 = (bf16[2,96,512]{2,1,0:T(8,128)(2,1)}, bf16[2,96,512]{2,1,0:T(8,128)(2,1)S(1)}, u32[]{:S(2)}, u32[]{:S(2)}) collective-permute-start(bf16[2,96,512]{2,1,0:T(8,128)(2,1)} %get-tuple-element.57.block), channel_id=1, source_target_pairs={{0,16},{4,20},{8,24},{12,28},{16,0},{20,4},{24,8},{28,12},{1,17},{... | collective-permute-start | bytes 589832 | tf_op jit(solution)/shard_map/ppermute | solution.py:449
  8.5 16.6 %collective-permute-start.1 = (bf16[2,96,512]{2,1,0:T(8,128)(2,1)}, bf16[2,96,512]{2,1,0:T(8,128)(2,1)S(1)}, u32[]{:S(2)}, u32[]{:S(2)}) collective-permute-start(bf16[2,96,512]{2,1,0:T(8,128)(2,1)} %get-tuple-element.57.block), channel_id=1, source_target_pairs={{0,8},{4,12},{8,0},{12,4},{16,24},{20,28},{24,16},{28,20},{1,9},{5... | collective-permute-start | bytes 589832 | tf_op jit(solution)/shard_map/ppermute | solution.py:449
  9.3 5.5 %collective-permute-start = (s32[1,4]{1,0:T(1,128)}, s32[1,4]{1,0:T(1,128)S(1)}, u32[]{:S(2)}, u32[]{:S(2)}) collective-permute-start(s32[1,4]{1,0:T(1,128)} %want_ref.5), channel_id=1, source_target_pairs={{0,4},{4,0},{8,12},{12,8},{16,20},{20,16},{24,28},{28,24},{1,5},{5... | collective-permute-start | bytes 56 | tf_op jit(solution)/shard_map/ppermute | solution.py:449
  14.9 15.1 %collective-permute-start.7 = (bf16[512,512]{1,0:T(8,128)(2,1)}, bf16[512,512]{1,0:T(8,128)(2,1)}, u32[]{:S(2)}, u32[]{:S(2)}) collective-permute-start(bf16[512,512]{1,0:T(8,128)(2,1)} %own.5), channel_id=1, source_target_pairs={{0,1},{1,0},{2,3},{3,2},{4,5},{5,4},{6,7},{7,6},{8,9},{9,8},{10,11... | collective-permute-start | bytes 1572872 | tf_op jit(solution)/shard_map/ppermute | solution.py:437
  15.1 16.7 %collective-permute-start.9 = (bf16[512,512]{1,0:T(8,128)(2,1)S(1)}, bf16[512,512]{1,0:T(8,128)(2,1)}, u32[]{:S(2)}, u32[]{:S(2)}) collective-permute-start(bf16[512,512]{1,0:T(8,128)(2,1)S(1)} %collective-permute-done.8.across), channel_id=1, source_target_pairs={{0,1},{1,0},{2,3},{3,2},{4,5},{5,4},{6,7},{7,6},{8,9},{9,8},{10,11... | collective-permute-start | bytes 1572872 | tf_op jit(solution)/shard_map/ppermute | solution.py:437
  25.8 12.6 %collective-permute-start.10 = (bf16[4,96,512]{2,1,0:T(8,128)(2,1)S(1)}, bf16[4,96,512]{2,1,0:T(8,128)(2,1)}, u32[]{:S(2)}, u32[]{:S(2)}) collective-permute-start(bf16[4,96,512]{2,1,0:T(8,128)(2,1)S(1)} %shard_map.237.after), channel_id=1, source_target_pairs={{0,4},{4,0},{8,12},{12,8},{16,20},{20,16},{24,28},{28,24},{1,5},{5... | collective-permute-start | bytes 1179656 | tf_op jit(solution)/shard_map/ppermute | solution.py:449
  27.4 22.2 %collective-permute-start.6 = (bf16[2,272,256]{2,1,0:T(8,128)(2,1)S(1)}, bf16[2,272,256]{2,1,0:T(8,128)(2,1)S(1)}, u32[]{:S(2)}, u32[]{:S(2)}) collective-permute-start(bf16[2,272,256]{2,1,0:T(8,128)(2,1)S(1)} %shard_map.238.refs_0_), channel_id=1, source_target_pairs={{0,24},{4,28},{8,16},{12,20},{16,8},{20,12},{24,0},{28,4},{1,25},{... | collective-permute-start | bytes 835592 | tf_op jit(solution)/shard_map/ppermute | solution.py:449
  29.9 21.6 %collective-permute-start.5 = (bf16[2,272,256]{2,1,0:T(8,128)(2,1)S(1)}, bf16[2,272,256]{2,1,0:T(8,128)(2,1)S(1)}, u32[]{:S(2)}, u32[]{:S(2)}) collective-permute-start(bf16[2,272,256]{2,1,0:T(8,128)(2,1)S(1)} %shard_map.238.refs_0_), channel_id=1, source_target_pairs={{0,16},{4,20},{8,24},{12,28},{16,0},{20,4},{24,8},{28,12},{1,17},{... | collective-permute-start | bytes 835592 | tf_op jit(solution)/shard_map/ppermute | solution.py:449
  29.9 21.6 %collective-permute-start.4 = (bf16[2,272,256]{2,1,0:T(8,128)(2,1)S(1)}, bf16[2,272,256]{2,1,0:T(8,128)(2,1)S(1)}, u32[]{:S(2)}, u32[]{:S(2)}) collective-permute-start(bf16[2,272,256]{2,1,0:T(8,128)(2,1)S(1)} %shard_map.238.refs_0_), channel_id=1, source_target_pairs={{0,8},{4,12},{8,0},{12,4},{16,24},{20,28},{24,16},{28,20},{1,9},{5... | collective-permute-start | bytes 835592 | tf_op jit(solution)/shard_map/ppermute | solution.py:449
  40.2 3.6 %collective-permute-start.13 = (bf16[48,512]{1,0:T(8,128)(2,1)S(1)}, bf16[48,512]{1,0:T(8,128)(2,1)S(1)}, u32[]{:S(2)}, u32[]{:S(2)}) collective-permute-start(bf16[48,512]{1,0:T(8,128)(2,1)S(1)} %get-tuple-element.60.low0.after), channel_id=1, source_target_pairs={{0,3},{1,2},{2,1},{3,0},{4,7},{5,6},{6,5},{7,4},{8,11},{9,10},{10,... | collective-permute-start | bytes 147464 | tf_op jit(solution)/shard_map/ppermute | solution.py:445
  40.3 4.6 %collective-permute-start.12 = (bf16[48,512]{1,0:T(8,128)(2,1)S(1)}, bf16[48,512]{1,0:T(8,128)(2,1)S(1)}, u32[]{:S(2)}, u32[]{:S(2)}) collective-permute-start(bf16[48,512]{1,0:T(8,128)(2,1)S(1)} %get-tuple-element.60.low0.after), channel_id=1, source_target_pairs={{0,2},{1,3},{2,0},{3,1},{4,6},{5,7},{6,4},{7,5},{8,10},{9,11},{10,... | collective-permute-start | bytes 147464 | tf_op jit(solution)/shard_map/ppermute | solution.py:441
  49.0 3.8 %collective-permute-start.17 = (bf16[144,512]{1,0:T(8,128)(2,1)S(1)}, bf16[144,512]{1,0:T(8,128)(2,1)S(1)}, u32[]{:S(2)}, u32[]{:S(2)}) collective-permute-start(bf16[144,512]{1,0:T(8,128)(2,1)S(1)} %get-tuple-element.68), channel_id=1, source_target_pairs={{0,1},{1,0},{2,3},{3,2},{4,5},{5,4},{6,7},{7,6},{8,9},{9,8},{10,11... | collective-permute-start | bytes 442376 | tf_op jit(solution)/shard_map/ppermute | solution.py:437
  49.2 2.9 %collective-permute-start.16 = (bf16[128,512]{1,0:T(8,128)(2,1)S(1)}, bf16[128,512]{1,0:T(8,128)(2,1)S(1)}, u32[]{:S(2)}, u32[]{:S(2)}) collective-permute-start(bf16[128,512]{1,0:T(8,128)(2,1)S(1)} %get-tuple-element.67), channel_id=1, source_target_pairs={{0,1},{1,0},{2,3},{3,2},{4,5},{5,4},{6,7},{7,6},{8,9},{9,8},{10,11... | collective-permute-start | bytes 393224 | tf_op jit(solution)/shard_map/ppermute | solution.py:437
  49.6 2.5 %collective-permute-start.18 = (bf16[128,512]{1,0:T(8,128)(2,1)S(1)}, bf16[128,512]{1,0:T(8,128)(2,1)S(1)}, u32[]{:S(2)}, u32[]{:S(2)}) collective-permute-start(bf16[128,512]{1,0:T(8,128)(2,1)S(1)} %get-tuple-element.69), channel_id=1, source_target_pairs={{0,1},{1,0},{2,3},{3,2},{4,5},{5,4},{6,7},{7,6},{8,9},{9,8},{10,11... | collective-permute-start | bytes 393224 | tf_op jit(solution)/shard_map/ppermute | solution.py:437
  52.9 19.0 %collective-permute-start.20 = (bf16[272,1024]{1,0:T(8,128)(2,1)S(1)}, bf16[272,1024]{1,0:T(8,128)(2,1)S(1)}, u32[]{:S(2)}, u32[]{:S(2)}) collective-permute-start(bf16[272,1024]{1,0:T(8,128)(2,1)S(1)} %shard_map.243.refs_5_.chip.after), channel_id=1, source_target_pairs={{0,2},{1,3},{2,0},{3,1},{4,6},{5,7},{6,4},{7,5},{8,10},{9,11},{10,... | collective-permute-start | bytes 1671176 | tf_op jit(solution)/shard_map/ppermute | solution.py:441
  53.5 6.7 %collective-permute-start.15 = (bf16[4,96,256]{2,1,0:T(8,128)(2,1)S(1)}, bf16[4,96,256]{2,1,0:T(8,128)(2,1)S(1)}, u32[]{:S(2)}, u32[]{:S(2)}) collective-permute-start(bf16[4,96,256]{2,1,0:T(8,128)(2,1)S(1)} %get-tuple-element.65.refs_4_), channel_id=1, source_target_pairs={{0,4},{4,0},{8,12},{12,8},{16,20},{20,16},{24,28},{28,24},{1,5},{5... | collective-permute-start | bytes 589832 | tf_op jit(solution)/shard_map/ppermute | solution.py:449
  58.2 4.6 %collective-permute-start.33 = (bf16[128,512]{1,0:T(8,128)(2,1)S(1)}, bf16[128,512]{1,0:T(8,128)(2,1)S(1)}, u32[]{:S(2)}, u32[]{:S(2)}) collective-permute-start(bf16[128,512]{1,0:T(8,128)(2,1)S(1)} %get-tuple-element.92), channel_id=1, source_target_pairs={{0,1},{1,0},{2,3},{3,2},{4,5},{5,4},{6,7},{7,6},{8,9},{9,8},{10,11... | collective-permute-start | bytes 393224 | tf_op jit(solution)/shard_map/ppermute | solution.py:437
  58.2 5.1 %collective-permute-start.35 = (bf16[128,512]{1,0:T(8,128)(2,1)S(1)}, bf16[128,512]{1,0:T(8,128)(2,1)S(1)}, u32[]{:S(2)}, u32[]{:S(2)}) collective-permute-start(bf16[128,512]{1,0:T(8,128)(2,1)S(1)} %get-tuple-element.94), channel_id=1, source_target_pairs={{0,1},{1,0},{2,3},{3,2},{4,5},{5,4},{6,7},{7,6},{8,9},{9,8},{10,11... | collective-permute-start | bytes 393224 | tf_op jit(solution)/shard_map/ppermute | solution.py:437
  61.2 10.7 %collective-permute-start.21 = (bf16[192,512]{1,0:T(8,128)(2,1)S(1)}, bf16[192,512]{1,0:T(8,128)(2,1)S(1)}, u32[]{:S(2)}, u32[]{:S(2)}) collective-permute-start(bf16[192,512]{1,0:T(8,128)(2,1)S(1)} %shard_map.244.refs_5_.refs_3_.table.table0), channel_id=1, source_target_pairs={{0,2},{1,3},{2,0},{3,1},{4,6},{5,7},{6,4},{7,5},{8,10},{9,11},{10,... | collective-permute-start | bytes 589832 | tf_op jit(solution)/shard_map/ppermute | solution.py:441
  62.8 4.8 %collective-permute-start.34 = (bf16[144,512]{1,0:T(8,128)(2,1)S(1)}, bf16[144,512]{1,0:T(8,128)(2,1)S(1)}, u32[]{:S(2)}, u32[]{:S(2)}) collective-permute-start(bf16[144,512]{1,0:T(8,128)(2,1)S(1)} %get-tuple-element.93), channel_id=1, source_target_pairs={{0,1},{1,0},{2,3},{3,2},{4,5},{5,4},{6,7},{7,6},{8,9},{9,8},{10,11... | collective-permute-start | bytes 442376 | tf_op jit(solution)/shard_map/ppermute | solution.py:437
  62.8 4.8 %collective-permute-start.36 = (bf16[128,512]{1,0:T(8,128)(2,1)S(1)}, bf16[128,512]{1,0:T(8,128)(2,1)S(1)}, u32[]{:S(2)}, u32[]{:S(2)}) collective-permute-start(bf16[128,512]{1,0:T(8,128)(2,1)S(1)} %get-tuple-element.95), channel_id=1, source_target_pairs={{0,1},{1,0},{2,3},{3,2},{4,5},{5,4},{6,7},{7,6},{8,9},{9,8},{10,11... | collective-permute-start | bytes 393224 | tf_op jit(solution)/shard_map/ppermute | solution.py:437
  63.3 10.9 %collective-permute-start.14 = (bf16[4,176,256]{2,1,0:T(8,128)(2,1)S(1)}, bf16[4,176,256]{2,1,0:T(8,128)(2,1)S(1)}, u32[]{:S(2)}, u32[]{:S(2)}) collective-permute-start(bf16[4,176,256]{2,1,0:T(8,128)(2,1)S(1)} %get-tuple-element.64), channel_id=1, source_target_pairs={{0,4},{4,0},{8,12},{12,8},{16,20},{20,16},{24,28},{28,24},{1,5},{5... | collective-permute-start | bytes 1081352 | tf_op jit(solution)/shard_map/ppermute | solution.py:449
  72.0 13.9 %collective-permute-start.37 = (bf16[272,1024]{1,0:T(8,128)(2,1)S(1)}, bf16[272,1024]{1,0:T(8,128)(2,1)S(1)}, u32[]{:S(2)}, u32[]{:S(2)}) collective-permute-start(bf16[272,1024]{1,0:T(8,128)(2,1)S(1)} %shard_map.251.chip), channel_id=1, source_target_pairs={{0,2},{1,3},{2,0},{3,1},{4,6},{5,7},{6,4},{7,5},{8,10},{9,11},{10,... | collective-permute-start | bytes 1671176 | tf_op jit(solution)/shard_map/ppermute | solution.py:441
  72.6 2.1 %collective-permute-start.26 = (bf16[192,512]{1,0:T(8,128)(2,1)S(1)}, bf16[192,512]{1,0:T(8,128)(2,1)S(1)}, u32[]{:S(2)}, u32[]{:S(2)}) collective-permute-start(bf16[192,512]{1,0:T(8,128)(2,1)S(1)} %shard_map.244.refs_5_.refs_3_.table.table0), channel_id=1, source_target_pairs={{0,1},{1,0},{2,3},{3,2},{4,5},{5,4},{6,7},{7,6},{8,9},{9,8},{10,11... | collective-permute-start | bytes 589832 | tf_op jit(solution)/shard_map/ppermute | solution.py:437
  72.6 2.1 %collective-permute-start.27 = (bf16[192,512]{1,0:T(8,128)(2,1)S(1)}, bf16[192,512]{1,0:T(8,128)(2,1)S(1)}, u32[]{:S(2)}, u32[]{:S(2)}) collective-permute-start(bf16[192,512]{1,0:T(8,128)(2,1)S(1)} %collective-permute-done.21.table_across.table2.refs_5_), channel_id=1, source_target_pairs={{0,1},{1,0},{2,3},{3,2},{4,5},{5,4},{6,7},{7,6},{8,9},{9,8},{10,11... | collective-permute-start | bytes 589832 | tf_op jit(solution)/shard_map/ppermute | solution.py:437
  74.1 1.9 %collective-permute-start.24 = (bf16[128,512]{1,0:T(8,128)(2,1)S(1)}, bf16[128,512]{1,0:T(8,128)(2,1)S(1)}, u32[]{:S(2)}, u32[]{:S(2)}) collective-permute-start(bf16[128,512]{1,0:T(8,128)(2,1)S(1)} %get-tuple-element.75.right0), channel_id=1, source_target_pairs={{0,1},{1,0},{2,3},{3,2},{4,5},{5,4},{6,7},{7,6},{8,9},{9,8},{10,11... | collective-permute-start | bytes 393224 | tf_op jit(solution)/shard_map/ppermute | solution.py:437
  81.7 2.3 %collective-permute-start.29 = (bf16[144,512]{1,0:T(8,128)(2,1)S(1)}, bf16[144,512]{1,0:T(8,128)(2,1)S(1)}, u32[]{:S(2)}, u32[]{:S(2)}) collective-permute-start(bf16[144,512]{1,0:T(8,128)(2,1)S(1)} %get-tuple-element.84), channel_id=1, source_target_pairs={{0,1},{1,0},{2,3},{3,2},{4,5},{5,4},{6,7},{7,6},{8,9},{9,8},{10,11... | collective-permute-start | bytes 442376 | tf_op jit(solution)/shard_map/ppermute | solution.py:437
  84.1 11.5 %collective-permute-start.32 = (bf16[272,512]{1,0:T(8,128)(2,1)S(1)}, bf16[272,512]{1,0:T(8,128)(2,1)S(1)}, u32[]{:S(2)}, u32[]{:S(2)}) collective-permute-start(bf16[272,512]{1,0:T(8,128)(2,1)S(1)} %get-tuple-element.88), channel_id=1, source_target_pairs={{0,2},{1,3},{2,0},{3,1},{4,6},{5,7},{6,4},{7,5},{8,10},{9,11},{10,... | collective-permute-start | bytes 835592 | tf_op jit(solution)/shard_map/ppermute | solution.py:441
  94.5 2.2 %collective-permute-start.43 = (bf16[144,512]{1,0:T(8,128)(2,1)S(1)}, bf16[144,512]{1,0:T(8,128)(2,1)S(1)}, u32[]{:S(2)}, u32[]{:S(2)}) collective-permute-start(bf16[144,512]{1,0:T(8,128)(2,1)S(1)} %get-tuple-element.102), channel_id=1, source_target_pairs={{0,1},{1,0},{2,3},{3,2},{4,5},{5,4},{6,7},{7,6},{8,9},{9,8},{10,11... | collective-permute-start | bytes 442376 | tf_op jit(solution)/shard_map/ppermute | solution.py:437
  96.8 8.8 %collective-permute-start.46 = (bf16[272,512]{1,0:T(8,128)(2,1)S(1)}, bf16[272,512]{1,0:T(8,128)(2,1)S(1)}, u32[]{:S(2)}, u32[]{:S(2)}) collective-permute-start(bf16[272,512]{1,0:T(8,128)(2,1)S(1)} %get-tuple-element.106), channel_id=1, source_target_pairs={{0,2},{1,3},{2,0},{3,1},{4,6},{5,7},{6,4},{7,5},{8,10},{9,11},{10,... | collective-permute-start | bytes 835592 | tf_op jit(solution)/shard_map/ppermute | solution.py:441
  (29 other events, 163.0 us)

commit v6 on v5

--- a/solution.py
+++ b/solution.py
@@ -400,23 +400,22 @@
     away[row:, :] = stay[row:, :].astype(bf16)
 
 
-def finish(count, lens_ref, table, *refs):
-    out = refs[-1]
+def finish(first, lens_ref, table, *refs):
+    *done, stay, arrived, left, right, out = refs
+    row = 0
+    for part in done:
+        out[row : row + part.shape[0], :] = part[...]
+        row += part.shape[0]
     wanted = lens_ref.shape[1]
-    width = out.shape[1]
-    for c in range(count):
-        stay, arrived, *resid = refs[4 * c : 4 * c + 4]
-        half = resid[0].shape[0]
-        rows = 2 * half
-        masks = lane_masks(lens_ref, wanted, c * rows, rows)
-        lows = stay[rows:, 0:rows] + arrived[rows:, 0:rows].astype(f32)
-        total = stay[0:rows, :] + arrived[0:rows, :].astype(f32)
-        total = total + delta(lows.astype(bf16).astype(f32), masks, table[...])
-        for k, piece in enumerate(resid):
-            at = slice(k * half, (k + 1) * half)
-            out[c * rows + k * half : c * rows + (k + 1) * half, :] = (
-                total[at, :] + piece[...].astype(f32)
-            ).astype(bf16)
+    half = left.shape[0]
+    rows = 2 * half
+    masks = lane_masks(lens_ref, wanted, first, rows)
+    lows = stay[rows:, 0:rows] + arrived[rows:, 0:rows].astype(f32)
+    total = stay[0:rows, :] + arrived[0:rows, :].astype(f32)
+    total = total + delta(lows.astype(bf16).astype(f32), masks, table[...])
+    for k, piece in enumerate((left, right)):
+        at = slice(k * half, (k + 1) * half)
+        out[row + k * half : row + (k + 1) * half, :] = (total[at, :] + piece[...].astype(f32)).astype(bf16)
 
 
 def rotation_tables(lens, row_count):
@@ -631,7 +630,7 @@
         )
         residuals.append(resid)
 
-    ends = []
+    done = []
     arrived = gate_weight
     for c in range(CHUNKS):
         resid = residuals[c]
@@ -654,11 +653,15 @@
         )(keep, *[swap_core(piece) for piece in sends], arrived)
         after = away
         arrived = swap_across(away)
-        ends += [stay, arrived, *resid[:2]]
-    return call(
-        functools.partial(finish, CHUNKS), [SMEM] + [VMEM] * (1 + 4 * CHUNKS),
-        shaped((row_count, width), bf16),
-    )(lengths, down_b, *ends)
+        last = c == CHUNKS - 1
+        before = done if last else []
+        done.append(
+            call(
+                functools.partial(finish, c * rows), [SMEM] + [VMEM] * (5 + len(before)),
+                shaped((row_count if last else rows, width), bf16),
+            )(lengths, down_b, *before, stay, arrived, *resid[:2])
+        )
+    return done[-1]
 
 
 def solution(mesh):

time: 108 us -> 108 us (level)
    pallas_call x1 -> x2, Pallas kernels: 1.75 us -> 2.43 us  [per_device(): call(functools.partial(finish, c * rows), [SMEM] + [VMEM] * (5 + len(befo...]
  transfers between devices with their start and end apart: 47 -> 47, of which waited for: 22 -> 22; matrix products, arithmetic and copies ran while one was open for 4% -> 4% of each run, Pallas kernels for 35% -> 36%
where the time goes in v6:
time: 108 us; the launch traced here: 107 us
  Pallas kernels  40.7 us (38%)
  waiting for transfers between devices  31 us (29%)
  starting transfers between devices  28.5 us (26%)
  local copies, waits for them, and re-layouts  2.41 us (2%)
  other arithmetic  2.36 us (2%)
  between operations  2.33 us (2%)
    ppermute x7, waiting for transfers between devices, swap_across(): return lax.ppermute(values, 'tp', [(k, k ^ 2) for k in range(4)])  13.2 us
    ppermute x10, starting transfers between devices, swap_req(): lax.ppermute(values, 'req', [(k, k ^ flips) for k in range(lax.axis_size(...  13 us
    pallas_call x2, Pallas kernels, per_device(): call(functools.partial(feed_forward, c), [SMEM] * 2 + [VMEM] * 19, terms,...  10.9 us
    ppermute x10, waiting for transfers between devices, swap_req(): lax.ppermute(values, 'req', [(k, k ^ flips) for k in range(lax.axis_size(...  10.4 us
    ppermute x7, starting transfers between devices, swap_across(): return lax.ppermute(values, 'tp', [(k, k ^ 2) for k in range(4)])  8.44 us
    pallas_call x2, Pallas kernels, per_device(): call(functools.partial(attend, c, heads, kv_heads), [SMEM] * 2 + [VMEM] *...  8.09 us
    ppermute x29, starting transfers between devices, swap_core(): return lax.ppermute(values, 'tp', [(k, k ^ 1) for k in range(4)])  6.97 us
    pallas_call x1, Pallas kernels, per_device(): call(project_qkv, [SMEM] + [VMEM] * 5 + [HBM] * 4, [shaped((row_count, wi...  6.45 us
  transfers between devices with their start and end apart: 47, of which 22 were waited for; matrix products, arithmetic and copies ran while one was open for 4% of the time, Pallas kernels for 36%

profile of v6, /device:TPU:0, one launch (start us, length us, event | category | flops | bytes accessed | tf_op | source)
XLA Modules:
  0.0 107.3 jit_solution(16320483490148033762)
XLA Ops:
  0.0 2.9 %collective-permute-start.8 = (bf16[512,512]{1,0:T(8,128)(2,1)}, bf16[512,512]{1,0:T(8,128)(2,1)S(1)}, u32[]{:S(2)}, u32[]{:S(2)}) collective-permute-start(bf16[512,512]{1,0:T(8,128)(2,1)} %own.5), channel_id=1, source_target_pairs={{0,2},{1,3},{2,0},{3,1},{4,6},{5,7},{6,4},{7,5},{8,10},{9,11},{10,... | collective-permute-start | bytes 1572872 | tf_op jit(solution)/shard_map/ppermute | solution.py:440
  2.9 1.9 %shard_map.235 = (bf16[2,96,512]{2,1,0:T(8,128)(2,1)}, bf16[2,272,256]{2,1,0:T(8,128)(2,1)}) custom-call(bf16[2,48,512]{2,1,0:T(8,128)(2,1)} %refs_0_.2, bf16[2,16,512]{2,1,0:T(8,128)(2,1)} %refs_1_.2, bf16[2,16,256]{2,1,0:T(8,128)(2,1)} %refs_2_.2, bf16[2,16,256]{2,1,0:T(8,128)(2,1)} %refs_3_.1, bf16[2,16,512]{2,1,0:T(8,128)(2,1)} %refs_4_.1, ...), custom_call_target="tpu_custom_call" | custom-call | flops 1 | bytes 1 | tf_op jit(solution)/shard_map/pallas_call | solution.py:533
  4.9 3.7 %collective-permute-start.3 = (bf16[2,96,512]{2,1,0:T(8,128)(2,1)}, bf16[2,96,512]{2,1,0:T(8,128)(2,1)S(1)}, u32[]{:S(2)}, u32[]{:S(2)}) collective-permute-start(bf16[2,96,512]{2,1,0:T(8,128)(2,1)} %get-tuple-element.57.block), channel_id=1, source_target_pairs={{0,24},{4,28},{8,16},{12,20},{16,8},{20,12},{24,0},{28,4},{1,25},{... | collective-permute-start | bytes 589832 | tf_op jit(solution)/shard_map/ppermute | solution.py:448
  9.3 1.5 %collective-permute-start = (s32[1,4]{1,0:T(1,128)}, s32[1,4]{1,0:T(1,128)S(1)}, u32[]{:S(2)}, u32[]{:S(2)}) collective-permute-start(s32[1,4]{1,0:T(1,128)} %want_ref.5), channel_id=1, source_target_pairs={{0,4},{4,0},{8,12},{12,8},{16,20},{20,16},{24,28},{28,24},{1,5},{5... | collective-permute-start | bytes 56 | tf_op jit(solution)/shard_map/ppermute | solution.py:448
  10.8 1.4 %fusion.1 = (s32[1,1]{1,0:T(1,128)}, s32[1,1]{1,0:T(1,128)}, s32[1,1]{1,0:T(1,128)}) fusion(s32[1,4]{1,0:T(1,128)} %lens_ref.17), kind=kLoop, calls=%fused_computation.9 | loop fusion | bytes 24 | tf_op jit(solution)/shard_map/slice | solution.py:429
  15.5 1.6 %multiply_cosine_fusion = (f32[512,128]{1,0:T(8,128)S(1)}, f32[512,128]{1,0:T(8,128)S(1)}) fusion(f32[128]{0:T(128)S(1)} %pad_maximum_fusion, f32[512]{0:T(512)S(1)} %subtract_convert_fusion, f32[128]{0:T(128)} %constant.22.clone.1), kind=kLoop, calls=%fused_computation | loop fusion | flops 131072 | bytes 527360 | tf_op jit(solution)/shard_map/cos | solution.py:432
  17.1 0.9 copy-done.7
  18.1 7.1 %collective-permute-done.2.refs_2_ = bf16[2,96,512]{2,1,0:T(8,128)(2,1)S(1)} collective-permute-done((bf16[2,96,512]{2,1,0:T(8,128)(2,1)}, bf16[2,96,512]{2,1,0:T(8,128)(2,1)S(1)}, u32[]{:S(2)}, u32[]{:S(2)}) %collective-permute-start.2) | collective-permute-done | bytes 196640 | tf_op jit(solution)/shard_map/ppermute | solution.py:448
  25.8 1.6 %collective-permute-start.10 = (bf16[4,96,512]{2,1,0:T(8,128)(2,1)S(1)}, bf16[4,96,512]{2,1,0:T(8,128)(2,1)}, u32[]{:S(2)}, u32[]{:S(2)}) collective-permute-start(bf16[4,96,512]{2,1,0:T(8,128)(2,1)S(1)} %shard_map.237.after), channel_id=1, source_target_pairs={{0,4},{4,0},{8,12},{12,8},{16,20},{20,16},{24,28},{28,24},{1,5},{5... | collective-permute-start | bytes 1179656 | tf_op jit(solution)/shard_map/ppermute | solution.py:448
  27.4 2.5 %collective-permute-start.6 = (bf16[2,272,256]{2,1,0:T(8,128)(2,1)S(1)}, bf16[2,272,256]{2,1,0:T(8,128)(2,1)S(1)}, u32[]{:S(2)}, u32[]{:S(2)}) collective-permute-start(bf16[2,272,256]{2,1,0:T(8,128)(2,1)S(1)} %shard_map.238.refs_0_), channel_id=1, source_target_pairs={{0,24},{4,28},{8,16},{12,20},{16,8},{20,12},{24,0},{28,4},{1,25},{... | collective-permute-start | bytes 835592 | tf_op jit(solution)/shard_map/ppermute | solution.py:448
  29.9 1.9 %collective-permute-start.4 = (bf16[2,272,256]{2,1,0:T(8,128)(2,1)S(1)}, bf16[2,272,256]{2,1,0:T(8,128)(2,1)S(1)}, u32[]{:S(2)}, u32[]{:S(2)}) collective-permute-start(bf16[2,272,256]{2,1,0:T(8,128)(2,1)S(1)} %shard_map.238.refs_0_), channel_id=1, source_target_pairs={{0,8},{4,12},{8,0},{12,4},{16,24},{20,28},{24,16},{28,20},{1,9},{5... | collective-permute-start | bytes 835592 | tf_op jit(solution)/shard_map/ppermute | solution.py:448
  31.9 6.4 %shard_map.239 = (bf16[512,512]{1,0:T(8,128)(2,1)S(1)}, bf16[512,2048]{1,0:T(8,128)(2,1)}, f32[256,1024]{1,0:T(8,128)S(1)}, f32[256,1024]{1,0:T(8,128)S(1)}) custom-call(s32[1]{0:T(128)} %bitcast.4.index_ref, bf16[512,512]{1,0:T(8,128)(2,1)S(1)} %copy-done.1, bf16[512,512]{1,0:T(8,128)(2,1)} %collective-permute-done.7.core, ...), custom_call_target="tpu_custom_call" | custom-call | flops 1 | bytes 1 | tf_op jit(solution)/shard_map/pallas_call | solution.py:545
  38.4 1.8 %shard_map.240 = (bf16[48,512]{1,0:T(8,128)(2,1)S(1)}, bf16[4,48,512]{2,1,0:T(8,128)(2,1)S(1)}) custom-call(s32[1]{0:T(128)} %bitcast.me_ref, s32[1,4]{1,0:T(1,128)S(1)} %copy-done.11, s32[1,4]{1,0:T(1,128)S(1)} %copy-done.8, bf16[2,96,512]{2,1,0:T(8,128)(2,1)S(1)} %shard_map.236.refs_0_, bf16[2,96,512]{2,1,0:T(8,128)(2,1)S(1)} %copy-done.5, ...), custom_call_target="tpu_custom_call" | custom-call | flops 1 | bytes 1 | tf_op jit(solution)/shard_map/pallas_call | solution.py:564
  40.9 2.9 %collective-permute-done.13.low3 = bf16[48,512]{1,0:T(8,128)(2,1)S(1)} collective-permute-done((bf16[48,512]{1,0:T(8,128)(2,1)S(1)}, bf16[48,512]{1,0:T(8,128)(2,1)S(1)}, u32[]{:S(2)}, u32[]{:S(2)}) %collective-permute-start.13) | collective-permute-done | bytes 49184 | tf_op jit(solution)/shard_map/ppermute | solution.py:444
  43.8 1.0 collective-permute-done.12.low2
  45.0 4.0 %shard_map.241 = (bf16[256,256]{1,0:T(8,128)(2,1)S(1)}, bf16[256,256]{1,0:T(8,128)(2,1)S(1)}, f32[272,1024]{1,0:T(8,128)S(1)}, bf16[128,512]{1,0:T(8,128)(2,1)S(...) custom-call(s32[1]{0:T(128)} %bitcast.4.index_ref, ...), custom_call_target="tpu_custom_call" | custom-call | flops 1 | bytes 1 | tf_op jit(solution)/shard_map/pallas_call | solution.py:584
  49.7 1.8 %collective-permute-done.5.refs_2_ = bf16[2,272,256]{2,1,0:T(8,128)(2,1)S(1)} collective-permute-done((bf16[2,272,256]{2,1,0:T(8,128)(2,1)S(1)}, bf16[2,272,256]{2,1,0:T(8,128)(2,1)S(1)}, u32[]{:S(2)}, u32[]{:S(2)}) %collective-permute-start.5) | collective-permute-done | bytes 278560 | tf_op jit(solution)/shard_map/ppermute | solution.py:448
  54.0 4.1 %shard_map.251 = (bf16[256,256]{1,0:T(8,128)(2,1)}, bf16[256,256]{1,0:T(8,128)(2,1)}, f32[272,1024]{1,0:T(8,128)S(1)}, bf16[128,512]{1,0:T(8,128)(2,1)S(1)}, bf1...) custom-call(s32[1]{0:T(128)} %bitcast.4.index_ref, s32[1,4]{1,0:T(1,128)S(1)} %copy-done.8, ...), custom_call_target="tpu_custom_call" | custom-call | flops 1 | bytes 1 | tf_op jit(solution)/shard_map/pallas_call | solution.py:584
  58.7 1.5 %collective-permute-done.15.refs_4_ = bf16[4,96,256]{2,1,0:T(8,128)(2,1)S(1)} collective-permute-done((bf16[4,96,256]{2,1,0:T(8,128)(2,1)S(1)}, bf16[4,96,256]{2,1,0:T(8,128)(2,1)S(1)}, u32[]{:S(2)}, u32[]{:S(2)}) %collective-permute-start.15) | collective-permute-done | bytes 196640 | tf_op jit(solution)/shard_map/ppermute | solution.py:448
  60.2 1.0 shard_map.244.refs_5_.refs_3_.table.table0
  61.2 1.6 %collective-permute-start.21 = (bf16[192,512]{1,0:T(8,128)(2,1)S(1)}, bf16[192,512]{1,0:T(8,128)(2,1)S(1)}, u32[]{:S(2)}, u32[]{:S(2)}) collective-permute-start(bf16[192,512]{1,0:T(8,128)(2,1)S(1)} %shard_map.244.refs_5_.refs_3_.table.table0), channel_id=1, source_target_pairs={{0,2},{1,3},{2,0},{3,1},{4,6},{5,7},{6,4},{7,5},{8,10},{9,11},{10,... | collective-permute-start | bytes 589832 | tf_op jit(solution)/shard_map/ppermute | solution.py:440
  63.8 3.8 %shard_map.246 = (bf16[2048,768]{1,0:T(8,128)(2,1)S(1)}, bf16[2048,768]{1,0:T(8,128)(2,1)S(1)}, bf16[768,2048]{1,0:T(8,128)(2,1)S(1)}) custom-call(bf16[2048,768]{1,0:T(8,128)(2,1)} %refs_0_.3, bf16[2048,768]{1,0:T(8,128)(2,1)} %refs_1_.3, bf16[768,2048]{1,0:T(8,128)(2,1)} %refs_2_.3, bf16[192,512]{1,0:T(8,128)(2,1)S(1)} %shard_map.244.refs_5_.refs_3_.table.table0), custom_call_target="tpu_custom_call" | custom-call | flops 1 | bytes 1 | tf_op jit(solution)/shard_map/pallas_call | solution.py:509
  67.6 4.3 %collective-permute-done.21.table_across.table2.refs_5_ = bf16[192,512]{1,0:T(8,128)(2,1)S(1)} collective-permute-done((bf16[192,512]{1,0:T(8,128)(2,1)S(1)}, bf16[192,512]{1,0:T(8,128)(2,1)S(1)}, u32[]{:S(2)}, u32[]{:S(2)}) %collective-permute-start.21) | collective-permute-done | bytes 196640 | tf_op jit(solution)/shard_map/ppermute | solution.py:440
  73.1 1.0 shard_map.247
  75.2 0.8 shard_map.245
  76.2 5.5 %shard_map.248 = (f32[272,1024]{1,0:T(8,128)S(1)}, bf16[128,512]{1,0:T(8,128)(2,1)S(1)}, bf16[144,512]{1,0:T(8,128)(2,1)S(1)}, bf16[128,512]{1,0:T(8,128)(2,1)S(1)}, bf16[128,512]{1,0:T(8,128)(2,1)S(1)}) custom-call(s32[1]{0:T(128)} %bitcast.4.index_ref, s32[1,4]{1,0:T(1,128)S(1)} %copy-done.8, bf16[128,512]{1,0:T(8,128)(2,1)S(1)} %get-tuple-element.73.left0.refs_2_, ...), custom_call_target="tpu_custom_call" | custom-call | flops 1 | bytes 1 | tf_op jit(solution)/shard_map/pallas_call | solution.py:637
  84.1 1.5 %collective-permute-start.32 = (bf16[272,512]{1,0:T(8,128)(2,1)S(1)}, bf16[272,512]{1,0:T(8,128)(2,1)S(1)}, u32[]{:S(2)}, u32[]{:S(2)}) collective-permute-start(bf16[272,512]{1,0:T(8,128)(2,1)S(1)} %get-tuple-element.88), channel_id=1, source_target_pairs={{0,2},{1,3},{2,0},{3,1},{4,6},{5,7},{6,4},{7,5},{8,10},{9,11},{10,... | collective-permute-start | bytes 835592 | tf_op jit(solution)/shard_map/ppermute | solution.py:440
  85.9 0.9 shard_map.253
  89.0 5.5 %shard_map.254 = (f32[272,1024]{1,0:T(8,128)S(1)}, bf16[128,512]{1,0:T(8,128)(2,1)S(1)}, bf16[144,512]{1,0:T(8,128)(2,1)S(1)}, bf16[128,512]{1,0:T(8,128)(2,1)S(1)}, bf16[128,512]{1,0:T(8,128)(2,1)S(1)}) custom-call(s32[1]{0:T(128)} %bitcast.4.index_ref, s32[1,4]{1,0:T(1,128)S(1)} %copy-done.8, bf16[128,512]{1,0:T(8,128)(2,1)S(1)} %get-tuple-element.96.left0.refs_3_, ...), custom_call_target="tpu_custom_call" | custom-call | flops 1 | bytes 1 | tf_op jit(solution)/shard_map/pallas_call | solution.py:637
  97.4 0.8 shard_map.250.refs_0_
  98.3 7.4 %collective-permute-done.46.refs_2_ = bf16[272,512]{1,0:T(8,128)(2,1)S(1)} collective-permute-done((bf16[272,512]{1,0:T(8,128)(2,1)S(1)}, bf16[272,512]{1,0:T(8,128)(2,1)S(1)}, u32[]{:S(2)}, u32[]{:S(2)}) %collective-permute-start.46) | collective-permute-done | bytes 278560 | tf_op jit(solution)/shard_map/ppermute | solution.py:440
  105.7 1.6 %shard_map.256 = bf16[512,512]{1,0:T(8,128)(2,1)} custom-call(s32[1,4]{1,0:T(1,128)S(1)} %copy-done.8, bf16[64,512]{1,0:T(8,128)(2,1)S(1)} %get-tuple-element.71.table, bf16[256,512]{1,0:T(8,128)(2,1)S(1)} %shard_map.250.refs_0_, f32[272,512]{1,0:T(8,128)S(1)} %get-tuple-element.105.refs_1_, bf16[272,512]{1,0:T(8,128)(2,1)S(1)} %collective-permute-done.46.refs_2_, ...), custom_call_target="tpu_custom_call" | custom-call | flops 1 | bytes 1 | tf_op jit(solution)/shard_map/pallas_call | solution.py:659
  (118 shorter events, 18.6 us)
Async XLA Ops:
  0.0 15.1 %collective-permute-start.8 = (bf16[512,512]{1,0:T(8,128)(2,1)}, bf16[512,512]{1,0:T(8,128)(2,1)S(1)}, u32[]{:S(2)}, u32[]{:S(2)}) collective-permute-start(bf16[512,512]{1,0:T(8,128)(2,1)} %own.5), channel_id=1, source_target_pairs={{0,2},{1,3},{2,0},{3,1},{4,6},{5,7},{6,4},{7,5},{8,10},{9,11},{10,... | collective-permute-start | bytes 1572872 | tf_op jit(solution)/shard_map/ppermute | solution.py:440
  4.9 13.2 %collective-permute-start.3 = (bf16[2,96,512]{2,1,0:T(8,128)(2,1)}, bf16[2,96,512]{2,1,0:T(8,128)(2,1)S(1)}, u32[]{:S(2)}, u32[]{:S(2)}) collective-permute-start(bf16[2,96,512]{2,1,0:T(8,128)(2,1)} %get-tuple-element.57.block), channel_id=1, source_target_pairs={{0,24},{4,28},{8,16},{12,20},{16,8},{20,12},{24,0},{28,4},{1,25},{... | collective-permute-start | bytes 589832 | tf_op jit(solution)/shard_map/ppermute | solution.py:448
  8.5 16.6 %collective-permute-start.2 = (bf16[2,96,512]{2,1,0:T(8,128)(2,1)}, bf16[2,96,512]{2,1,0:T(8,128)(2,1)S(1)}, u32[]{:S(2)}, u32[]{:S(2)}) collective-permute-start(bf16[2,96,512]{2,1,0:T(8,128)(2,1)} %get-tuple-element.57.block), channel_id=1, source_target_pairs={{0,16},{4,20},{8,24},{12,28},{16,0},{20,4},{24,8},{28,12},{1,17},{... | collective-permute-start | bytes 589832 | tf_op jit(solution)/shard_map/ppermute | solution.py:448
  8.5 16.6 %collective-permute-start.1 = (bf16[2,96,512]{2,1,0:T(8,128)(2,1)}, bf16[2,96,512]{2,1,0:T(8,128)(2,1)S(1)}, u32[]{:S(2)}, u32[]{:S(2)}) collective-permute-start(bf16[2,96,512]{2,1,0:T(8,128)(2,1)} %get-tuple-element.57.block), channel_id=1, source_target_pairs={{0,8},{4,12},{8,0},{12,4},{16,24},{20,28},{24,16},{28,20},{1,9},{5... | collective-permute-start | bytes 589832 | tf_op jit(solution)/shard_map/ppermute | solution.py:448
  9.3 5.5 %collective-permute-start = (s32[1,4]{1,0:T(1,128)}, s32[1,4]{1,0:T(1,128)S(1)}, u32[]{:S(2)}, u32[]{:S(2)}) collective-permute-start(s32[1,4]{1,0:T(1,128)} %want_ref.5), channel_id=1, source_target_pairs={{0,4},{4,0},{8,12},{12,8},{16,20},{20,16},{24,28},{28,24},{1,5},{5... | collective-permute-start | bytes 56 | tf_op jit(solution)/shard_map/ppermute | solution.py:448
  14.9 15.1 %collective-permute-start.7 = (bf16[512,512]{1,0:T(8,128)(2,1)}, bf16[512,512]{1,0:T(8,128)(2,1)}, u32[]{:S(2)}, u32[]{:S(2)}) collective-permute-start(bf16[512,512]{1,0:T(8,128)(2,1)} %own.5), channel_id=1, source_target_pairs={{0,1},{1,0},{2,3},{3,2},{4,5},{5,4},{6,7},{7,6},{8,9},{9,8},{10,11... | collective-permute-start | bytes 1572872 | tf_op jit(solution)/shard_map/ppermute | solution.py:436
  15.1 16.7 %collective-permute-start.9 = (bf16[512,512]{1,0:T(8,128)(2,1)S(1)}, bf16[512,512]{1,0:T(8,128)(2,1)}, u32[]{:S(2)}, u32[]{:S(2)}) collective-permute-start(bf16[512,512]{1,0:T(8,128)(2,1)S(1)} %collective-permute-done.8.across), channel_id=1, source_target_pairs={{0,1},{1,0},{2,3},{3,2},{4,5},{5,4},{6,7},{7,6},{8,9},{9,8},{10,11... | collective-permute-start | bytes 1572872 | tf_op jit(solution)/shard_map/ppermute | solution.py:436
  25.8 12.6 %collective-permute-start.10 = (bf16[4,96,512]{2,1,0:T(8,128)(2,1)S(1)}, bf16[4,96,512]{2,1,0:T(8,128)(2,1)}, u32[]{:S(2)}, u32[]{:S(2)}) collective-permute-start(bf16[4,96,512]{2,1,0:T(8,128)(2,1)S(1)} %shard_map.237.after), channel_id=1, source_target_pairs={{0,4},{4,0},{8,12},{12,8},{16,20},{20,16},{24,28},{28,24},{1,5},{5... | collective-permute-start | bytes 1179656 | tf_op jit(solution)/shard_map/ppermute | solution.py:448
  27.4 22.2 %collective-permute-start.6 = (bf16[2,272,256]{2,1,0:T(8,128)(2,1)S(1)}, bf16[2,272,256]{2,1,0:T(8,128)(2,1)S(1)}, u32[]{:S(2)}, u32[]{:S(2)}) collective-permute-start(bf16[2,272,256]{2,1,0:T(8,128)(2,1)S(1)} %shard_map.238.refs_0_), channel_id=1, source_target_pairs={{0,24},{4,28},{8,16},{12,20},{16,8},{20,12},{24,0},{28,4},{1,25},{... | collective-permute-start | bytes 835592 | tf_op jit(solution)/shard_map/ppermute | solution.py:448
  29.9 21.6 %collective-permute-start.5 = (bf16[2,272,256]{2,1,0:T(8,128)(2,1)S(1)}, bf16[2,272,256]{2,1,0:T(8,128)(2,1)S(1)}, u32[]{:S(2)}, u32[]{:S(2)}) collective-permute-start(bf16[2,272,256]{2,1,0:T(8,128)(2,1)S(1)} %shard_map.238.refs_0_), channel_id=1, source_target_pairs={{0,16},{4,20},{8,24},{12,28},{16,0},{20,4},{24,8},{28,12},{1,17},{... | collective-permute-start | bytes 835592 | tf_op jit(solution)/shard_map/ppermute | solution.py:448
  29.9 21.6 %collective-permute-start.4 = (bf16[2,272,256]{2,1,0:T(8,128)(2,1)S(1)}, bf16[2,272,256]{2,1,0:T(8,128)(2,1)S(1)}, u32[]{:S(2)}, u32[]{:S(2)}) collective-permute-start(bf16[2,272,256]{2,1,0:T(8,128)(2,1)S(1)} %shard_map.238.refs_0_), channel_id=1, source_target_pairs={{0,8},{4,12},{8,0},{12,4},{16,24},{20,28},{24,16},{28,20},{1,9},{5... | collective-permute-start | bytes 835592 | tf_op jit(solution)/shard_map/ppermute | solution.py:448
  40.2 3.6 %collective-permute-start.13 = (bf16[48,512]{1,0:T(8,128)(2,1)S(1)}, bf16[48,512]{1,0:T(8,128)(2,1)S(1)}, u32[]{:S(2)}, u32[]{:S(2)}) collective-permute-start(bf16[48,512]{1,0:T(8,128)(2,1)S(1)} %get-tuple-element.60.low0.after), channel_id=1, source_target_pairs={{0,3},{1,2},{2,1},{3,0},{4,7},{5,6},{6,5},{7,4},{8,11},{9,10},{10,... | collective-permute-start | bytes 147464 | tf_op jit(solution)/shard_map/ppermute | solution.py:444
  40.3 4.6 %collective-permute-start.12 = (bf16[48,512]{1,0:T(8,128)(2,1)S(1)}, bf16[48,512]{1,0:T(8,128)(2,1)S(1)}, u32[]{:S(2)}, u32[]{:S(2)}) collective-permute-start(bf16[48,512]{1,0:T(8,128)(2,1)S(1)} %get-tuple-element.60.low0.after), channel_id=1, source_target_pairs={{0,2},{1,3},{2,0},{3,1},{4,6},{5,7},{6,4},{7,5},{8,10},{9,11},{10,... | collective-permute-start | bytes 147464 | tf_op jit(solution)/shard_map/ppermute | solution.py:440
  49.0 3.8 %collective-permute-start.17 = (bf16[144,512]{1,0:T(8,128)(2,1)S(1)}, bf16[144,512]{1,0:T(8,128)(2,1)S(1)}, u32[]{:S(2)}, u32[]{:S(2)}) collective-permute-start(bf16[144,512]{1,0:T(8,128)(2,1)S(1)} %get-tuple-element.68), channel_id=1, source_target_pairs={{0,1},{1,0},{2,3},{3,2},{4,5},{5,4},{6,7},{7,6},{8,9},{9,8},{10,11... | collective-permute-start | bytes 442376 | tf_op jit(solution)/shard_map/ppermute | solution.py:436
  49.2 2.9 %collective-permute-start.16 = (bf16[128,512]{1,0:T(8,128)(2,1)S(1)}, bf16[128,512]{1,0:T(8,128)(2,1)S(1)}, u32[]{:S(2)}, u32[]{:S(2)}) collective-permute-start(bf16[128,512]{1,0:T(8,128)(2,1)S(1)} %get-tuple-element.67), channel_id=1, source_target_pairs={{0,1},{1,0},{2,3},{3,2},{4,5},{5,4},{6,7},{7,6},{8,9},{9,8},{10,11... | collective-permute-start | bytes 393224 | tf_op jit(solution)/shard_map/ppermute | solution.py:436
  49.6 2.5 %collective-permute-start.18 = (bf16[128,512]{1,0:T(8,128)(2,1)S(1)}, bf16[128,512]{1,0:T(8,128)(2,1)S(1)}, u32[]{:S(2)}, u32[]{:S(2)}) collective-permute-start(bf16[128,512]{1,0:T(8,128)(2,1)S(1)} %get-tuple-element.69), channel_id=1, source_target_pairs={{0,1},{1,0},{2,3},{3,2},{4,5},{5,4},{6,7},{7,6},{8,9},{9,8},{10,11... | collective-permute-start | bytes 393224 | tf_op jit(solution)/shard_map/ppermute | solution.py:436
  52.9 19.0 %collective-permute-start.20 = (bf16[272,1024]{1,0:T(8,128)(2,1)S(1)}, bf16[272,1024]{1,0:T(8,128)(2,1)S(1)}, u32[]{:S(2)}, u32[]{:S(2)}) collective-permute-start(bf16[272,1024]{1,0:T(8,128)(2,1)S(1)} %shard_map.243.refs_5_.chip.after), channel_id=1, source_target_pairs={{0,2},{1,3},{2,0},{3,1},{4,6},{5,7},{6,4},{7,5},{8,10},{9,11},{10,... | collective-permute-start | bytes 1671176 | tf_op jit(solution)/shard_map/ppermute | solution.py:440
  53.5 6.7 %collective-permute-start.15 = (bf16[4,96,256]{2,1,0:T(8,128)(2,1)S(1)}, bf16[4,96,256]{2,1,0:T(8,128)(2,1)S(1)}, u32[]{:S(2)}, u32[]{:S(2)}) collective-permute-start(bf16[4,96,256]{2,1,0:T(8,128)(2,1)S(1)} %get-tuple-element.65.refs_4_), channel_id=1, source_target_pairs={{0,4},{4,0},{8,12},{12,8},{16,20},{20,16},{24,28},{28,24},{1,5},{5... | collective-permute-start | bytes 589832 | tf_op jit(solution)/shard_map/ppermute | solution.py:448
  58.2 4.6 %collective-permute-start.33 = (bf16[128,512]{1,0:T(8,128)(2,1)S(1)}, bf16[128,512]{1,0:T(8,128)(2,1)S(1)}, u32[]{:S(2)}, u32[]{:S(2)}) collective-permute-start(bf16[128,512]{1,0:T(8,128)(2,1)S(1)} %get-tuple-element.92), channel_id=1, source_target_pairs={{0,1},{1,0},{2,3},{3,2},{4,5},{5,4},{6,7},{7,6},{8,9},{9,8},{10,11... | collective-permute-start | bytes 393224 | tf_op jit(solution)/shard_map/ppermute | solution.py:436
  58.2 5.1 %collective-permute-start.35 = (bf16[128,512]{1,0:T(8,128)(2,1)S(1)}, bf16[128,512]{1,0:T(8,128)(2,1)S(1)}, u32[]{:S(2)}, u32[]{:S(2)}) collective-permute-start(bf16[128,512]{1,0:T(8,128)(2,1)S(1)} %get-tuple-element.94), channel_id=1, source_target_pairs={{0,1},{1,0},{2,3},{3,2},{4,5},{5,4},{6,7},{7,6},{8,9},{9,8},{10,11... | collective-permute-start | bytes 393224 | tf_op jit(solution)/shard_map/ppermute | solution.py:436
  61.2 10.7 %collective-permute-start.21 = (bf16[192,512]{1,0:T(8,128)(2,1)S(1)}, bf16[192,512]{1,0:T(8,128)(2,1)S(1)}, u32[]{:S(2)}, u32[]{:S(2)}) collective-permute-start(bf16[192,512]{1,0:T(8,128)(2,1)S(1)} %shard_map.244.refs_5_.refs_3_.table.table0), channel_id=1, source_target_pairs={{0,2},{1,3},{2,0},{3,1},{4,6},{5,7},{6,4},{7,5},{8,10},{9,11},{10,... | collective-permute-start | bytes 589832 | tf_op jit(solution)/shard_map/ppermute | solution.py:440
  62.8 4.8 %collective-permute-start.34 = (bf16[144,512]{1,0:T(8,128)(2,1)S(1)}, bf16[144,512]{1,0:T(8,128)(2,1)S(1)}, u32[]{:S(2)}, u32[]{:S(2)}) collective-permute-start(bf16[144,512]{1,0:T(8,128)(2,1)S(1)} %get-tuple-element.93), channel_id=1, source_target_pairs={{0,1},{1,0},{2,3},{3,2},{4,5},{5,4},{6,7},{7,6},{8,9},{9,8},{10,11... | collective-permute-start | bytes 442376 | tf_op jit(solution)/shard_map/ppermute | solution.py:436
  62.8 4.8 %collective-permute-start.36 = (bf16[128,512]{1,0:T(8,128)(2,1)S(1)}, bf16[128,512]{1,0:T(8,128)(2,1)S(1)}, u32[]{:S(2)}, u32[]{:S(2)}) collective-permute-start(bf16[128,512]{1,0:T(8,128)(2,1)S(1)} %get-tuple-element.95), channel_id=1, source_target_pairs={{0,1},{1,0},{2,3},{3,2},{4,5},{5,4},{6,7},{7,6},{8,9},{9,8},{10,11... | collective-permute-start | bytes 393224 | tf_op jit(solution)/shard_map/ppermute | solution.py:436
  63.3 10.9 %collective-permute-start.14 = (bf16[4,176,256]{2,1,0:T(8,128)(2,1)S(1)}, bf16[4,176,256]{2,1,0:T(8,128)(2,1)S(1)}, u32[]{:S(2)}, u32[]{:S(2)}) collective-permute-start(bf16[4,176,256]{2,1,0:T(8,128)(2,1)S(1)} %get-tuple-element.64), channel_id=1, source_target_pairs={{0,4},{4,0},{8,12},{12,8},{16,20},{20,16},{24,28},{28,24},{1,5},{5... | collective-permute-start | bytes 1081352 | tf_op jit(solution)/shard_map/ppermute | solution.py:448
  72.0 13.9 %collective-permute-start.37 = (bf16[272,1024]{1,0:T(8,128)(2,1)S(1)}, bf16[272,1024]{1,0:T(8,128)(2,1)S(1)}, u32[]{:S(2)}, u32[]{:S(2)}) collective-permute-start(bf16[272,1024]{1,0:T(8,128)(2,1)S(1)} %shard_map.252.chip), channel_id=1, source_target_pairs={{0,2},{1,3},{2,0},{3,1},{4,6},{5,7},{6,4},{7,5},{8,10},{9,11},{10,... | collective-permute-start | bytes 1671176 | tf_op jit(solution)/shard_map/ppermute | solution.py:440
  72.6 2.1 %collective-permute-start.26 = (bf16[192,512]{1,0:T(8,128)(2,1)S(1)}, bf16[192,512]{1,0:T(8,128)(2,1)S(1)}, u32[]{:S(2)}, u32[]{:S(2)}) collective-permute-start(bf16[192,512]{1,0:T(8,128)(2,1)S(1)} %shard_map.244.refs_5_.refs_3_.table.table0), channel_id=1, source_target_pairs={{0,1},{1,0},{2,3},{3,2},{4,5},{5,4},{6,7},{7,6},{8,9},{9,8},{10,11... | collective-permute-start | bytes 589832 | tf_op jit(solution)/shard_map/ppermute | solution.py:436
  72.6 2.1 %collective-permute-start.27 = (bf16[192,512]{1,0:T(8,128)(2,1)S(1)}, bf16[192,512]{1,0:T(8,128)(2,1)S(1)}, u32[]{:S(2)}, u32[]{:S(2)}) collective-permute-start(bf16[192,512]{1,0:T(8,128)(2,1)S(1)} %collective-permute-done.21.table_across.table2.refs_5_), channel_id=1, source_target_pairs={{0,1},{1,0},{2,3},{3,2},{4,5},{5,4},{6,7},{7,6},{8,9},{9,8},{10,11... | collective-permute-start | bytes 589832 | tf_op jit(solution)/shard_map/ppermute | solution.py:436
  74.1 1.9 %collective-permute-start.24 = (bf16[128,512]{1,0:T(8,128)(2,1)S(1)}, bf16[128,512]{1,0:T(8,128)(2,1)S(1)}, u32[]{:S(2)}, u32[]{:S(2)}) collective-permute-start(bf16[128,512]{1,0:T(8,128)(2,1)S(1)} %get-tuple-element.75.right0), channel_id=1, source_target_pairs={{0,1},{1,0},{2,3},{3,2},{4,5},{5,4},{6,7},{7,6},{8,9},{9,8},{10,11... | collective-permute-start | bytes 393224 | tf_op jit(solution)/shard_map/ppermute | solution.py:436
  81.7 2.3 %collective-permute-start.29 = (bf16[144,512]{1,0:T(8,128)(2,1)S(1)}, bf16[144,512]{1,0:T(8,128)(2,1)S(1)}, u32[]{:S(2)}, u32[]{:S(2)}) collective-permute-start(bf16[144,512]{1,0:T(8,128)(2,1)S(1)} %get-tuple-element.84), channel_id=1, source_target_pairs={{0,1},{1,0},{2,3},{3,2},{4,5},{5,4},{6,7},{7,6},{8,9},{9,8},{10,11... | collective-permute-start | bytes 442376 | tf_op jit(solution)/shard_map/ppermute | solution.py:436
  84.1 11.5 %collective-permute-start.32 = (bf16[272,512]{1,0:T(8,128)(2,1)S(1)}, bf16[272,512]{1,0:T(8,128)(2,1)S(1)}, u32[]{:S(2)}, u32[]{:S(2)}) collective-permute-start(bf16[272,512]{1,0:T(8,128)(2,1)S(1)} %get-tuple-element.88), channel_id=1, source_target_pairs={{0,2},{1,3},{2,0},{3,1},{4,6},{5,7},{6,4},{7,5},{8,10},{9,11},{10,... | collective-permute-start | bytes 835592 | tf_op jit(solution)/shard_map/ppermute | solution.py:440
  94.5 2.2 %collective-permute-start.43 = (bf16[144,512]{1,0:T(8,128)(2,1)S(1)}, bf16[144,512]{1,0:T(8,128)(2,1)S(1)}, u32[]{:S(2)}, u32[]{:S(2)}) collective-permute-start(bf16[144,512]{1,0:T(8,128)(2,1)S(1)} %get-tuple-element.102), channel_id=1, source_target_pairs={{0,1},{1,0},{2,3},{3,2},{4,5},{5,4},{6,7},{7,6},{8,9},{9,8},{10,11... | collective-permute-start | bytes 442376 | tf_op jit(solution)/shard_map/ppermute | solution.py:436
  96.8 8.8 %collective-permute-start.46 = (bf16[272,512]{1,0:T(8,128)(2,1)S(1)}, bf16[272,512]{1,0:T(8,128)(2,1)S(1)}, u32[]{:S(2)}, u32[]{:S(2)}) collective-permute-start(bf16[272,512]{1,0:T(8,128)(2,1)S(1)} %get-tuple-element.106), channel_id=1, source_target_pairs={{0,2},{1,3},{2,0},{3,1},{4,6},{5,7},{6,4},{7,5},{8,10},{9,11},{10,... | collective-permute-start | bytes 835592 | tf_op jit(solution)/shard_map/ppermute | solution.py:440
  (29 other events, 163.0 us)
